TPU v7x, 256 devices: a whole 4x4x8 slice. The times are simulated.
256 devices in a mesh: src: 64 (over y, z, core), tgt: 4 (over x).
Axes of the slice: x: 4, y: 4, z: 8, core: 2. Of those that a mesh axis runs over, the one named last changes fastest.
Arguments:
- source_features: bfloat16 [524288, 64], P('src'), may hold values from -6 to 6
- target_features: bfloat16 [4, 8192, 64], P('tgt', 'src'), may hold values from -6 to 6
- block_targets: int32 [4096, 4, 8], P('src', 'tgt'), may hold values from -1 to 63, as said below
Outputs:
- source_dual: float32 [524288], P('src')
- target_dual: float32 [4, 8192], P('tgt', 'src')
Inputs may be any that keep to these rules, and one draw needn't show every extreme that they name: `block_targets`: listed entries come first in each slot row and are distinct; every source block lists entry s mod 64 in every group, so every source cell and every target cell has allowed pairs; source block 0 lists 8 blocks in every group.
All inputs are finite; a program needn't handle non-finite values.
Results may differ from a plain program's by a relative error of at most 0.0009.
Values may be sent and summed in bfloat16 or wider, within the bound.
A program may use at most 64 MiB of HBM per device.

v0:
```python
import math

import jax
import jax.numpy as jnp
from jax import lax
from jax.sharding import PartitionSpec as P

BLK = 128
DIM = 64
ITERS = 2


EPSILON = 0.01
NEGATIVE = -1e30


def as_sent(array):

    def short(part):
        return part.astype(jnp.bfloat16) if part.dtype == jnp.float32 else part

    return jax.tree.map(short, array)


def joined(array, axis, combine):
    everything = jax.tree.map(lambda part: lax.all_gather(part, axis), array)
    leading = jax.tree.map(lambda part: part[0], everything)

    def turn(k, so_far):
        return combine(so_far, jax.tree.map(lambda part: part[k], everything))

    return lax.fori_loop(1, lax.axis_size(axis), turn, leading)


def tile_costs(source_tile, target_tiles):
    cross_term = jnp.einsum(
        "gid,gkjd->gkij", source_tile, target_tiles, preferred_element_type=jnp.float32
    )
    source_f = source_tile.astype(jnp.float32)
    target_f = target_tiles.astype(jnp.float32)
    source_sq = jnp.sum(source_f * source_f, axis=-1)
    target_sq = jnp.sum(target_f * target_f, axis=-1)
    return (source_sq[:, None, :, None] + target_sq[:, :, None, :] - 2.0 * cross_term) * (
        1.0 / source_tile.shape[-1]
    )


def combine_lse(first_pair, second_pair):
    peak = jnp.maximum(first_pair[0], second_pair[0])
    total = first_pair[1] * jnp.exp(first_pair[0] - peak) + second_pair[1] * jnp.exp(
        second_pair[0] - peak
    )
    return (peak, total)


def local(source_features, target_features, block_targets):
    row_count = source_features.shape[0]
    source_blocks = row_count // BLK
    slot_count = block_targets.shape[2]
    src_count = lax.axis_size("src")
    tgt_count = lax.axis_size("tgt")
    target_full = lax.all_gather(target_features, "src", axis=1, tiled=True)[0]
    target_blocks = target_full.shape[0] // BLK
    target_tiles = target_full.reshape(target_blocks, BLK, DIM)
    share_length = target_blocks * BLK // src_count
    share_start = lax.axis_index("src") * share_length
    local_targets = block_targets[:, 0, :]
    present = local_targets >= 0
    local_index = jnp.where(present, local_targets, 0)
    group_size = math.gcd(8, source_blocks)
    turn_count = source_blocks // group_size
    source_tiles = source_features.reshape(turn_count, group_size, BLK, DIM)
    index_groups = local_index.reshape(turn_count, group_size, slot_count)
    present_groups = present.reshape(turn_count, group_size, slot_count)
    log_source = -math.log(row_count * src_count)
    log_target = -math.log(target_blocks * BLK * tgt_count)
    flat_index = jnp.where(present.reshape(-1), local_index.reshape(-1), target_blocks)
    safe_index = jnp.minimum(flat_index, target_blocks - 1)
    target_dual = jnp.zeros((target_blocks * BLK,), jnp.float32)
    dual_share = jnp.zeros((share_length,), jnp.float32)
    source_dual = jnp.zeros((row_count,), jnp.float32)
    for iteration in range(ITERS):
        dual_tiles = target_dual.reshape(target_blocks, BLK)

        def row_one_group(operands):
            source_tile, index_tile, present_tile = operands
            costs = tile_costs(source_tile, target_tiles[index_tile])
            scores = (dual_tiles[index_tile][:, :, None, :] - costs) / EPSILON
            mask_tile = present_tile[:, :, None, None]
            scores = jnp.where(mask_tile, scores, NEGATIVE)
            peak = jnp.max(scores, axis=(1, 3))
            total = jnp.sum(
                jnp.where(mask_tile, jnp.exp(scores - peak[:, None, :, None]), 0.0), axis=(1, 3)
            )
            return (peak, total)

        row_peaks, row_totals = lax.map(row_one_group, (source_tiles, index_groups, present_groups))
        row_peaks = row_peaks.reshape(-1)
        row_totals = row_totals.reshape(-1)
        row_peak = lax.pmax(as_sent(row_peaks), "tgt").astype(row_peaks.dtype)
        row_totals = lax.psum(
            (row_totals * jnp.exp(row_peaks - row_peak)).astype(jnp.bfloat16), "tgt"
        ).astype(jnp.float32)
        row_peaks = row_peak
        source_dual = EPSILON * log_source - EPSILON * (row_peaks + jnp.log(row_totals))
        dual_groups = source_dual.reshape(turn_count, group_size, BLK)

        def column_one_group(operands):
            source_tile, dual_tile, index_tile, present_tile = operands
            costs = tile_costs(source_tile, target_tiles[index_tile])
            scores = (dual_tile[:, None, :, None] - costs) / EPSILON
            mask_tile = present_tile[:, :, None, None]
            scores = jnp.where(mask_tile, scores, NEGATIVE)
            peak = jnp.max(scores, axis=2)
            total = jnp.sum(
                jnp.where(mask_tile, jnp.exp(scores - peak[:, :, None, :]), 0.0), axis=2
            )
            return (peak, total)

        peaks, totals = lax.map(
            column_one_group, (source_tiles, dual_groups, index_groups, present_groups)
        )
        peaks = peaks.reshape(-1, BLK)
        totals = totals.reshape(-1, BLK)
        col_peak = (
            jnp.full((target_blocks, BLK), NEGATIVE, jnp.float32)
            .at[flat_index]
            .max(peaks, mode="drop")
        )
        shifted = totals * jnp.exp(peaks - col_peak[safe_index])
        col_total = (
            jnp.zeros((target_blocks, BLK), jnp.float32).at[flat_index].add(shifted, mode="drop")
        )
        col_peak, col_total = (col_peak.reshape(-1), col_total.reshape(-1))
        col_peak, col_total = joined((col_peak, col_total), "src", combine_lse)
        target_dual = EPSILON * log_target - EPSILON * (col_peak + jnp.log(col_total))
        dual_share = lax.dynamic_slice_in_dim(target_dual, share_start, share_length, 0)
    return (source_dual, dual_share.reshape(1, share_length))


def solution(mesh):
    in_specs = (P("src", None), P("tgt", "src", None), P("src", "tgt", None))
    out_specs = (P("src"), P("tgt", "src"))
    return jax.shard_map(local, mesh=mesh, in_specs=in_specs, out_specs=out_specs, check_vma=False)
```

profile of v0, /device:TPU:1, one launch (start us, length us, event | category | flops | bytes accessed | tf_op | source)
XLA Modules:
  0.0 1041.1 jit_solution(13016636313160570242)
XLA Ops:
  11.1 74.2 %all-gather.10.cloned.1.call-done = bf16[1,8192,64]{1,2,0:T(8,128)(2,1)} async-done(((bf16[1,128,64]{1,2,0:T(8,128)(2,1)}), bf16[1,8192,64]{1,2,0:T(8,128)(2,1)}) %all-gather.10.cloned.1.call-update) | async-done | bytes 1048592 | tf_op jit(solution)/shard_map/all_gather | solution.py:62
  87.3 116.1 %while.82 = (s32[]{:T(128)}, f32[8,8,128]{2,1,0:T(8,128)S(1)}, f32[8,8,128]{2,1,0:T(8,128)S(1)}, pred[8,8,8]{2,1,0:T(8,128)(4,1)S(1)}, s32[8,8,8]{2,1,0:T(8,128)...) while((s32[]{:T(128)}, f32[8,8,128]{2,1,0:T(8,128)S(1)}, ...), condition=%wide.region_5.6_spmd, body=%wide.region_0.5_spmd.sunk | while | flops 154851520 | bytes 13155381 | solution.py:97
  93.0 5.8 fusion.69
  122.0 5.8 fusion.69
  151.0 5.8 fusion.69
  165.6 5.8 fusion.69
  180.1 5.8 fusion.69
  203.4 13.0 %pmax.14 = bf16[8192]{0:T(1024)(128)(2,1)S(1)} all-reduce(bf16[8192]{0:T(1024)(128)(2,1)S(1)} %bitcast_convert_fusion.1), channel_id=1, replica_groups=mesh['src'=64,'tgt'=4] {'tgt'}, use_global_device_ids=true, to_apply=%region_6.7 | all-reduce | flops 8192 | bytes 32768 | tf_op jit(solution)/shard_map/pmax | solution.py:100
  216.4 10.8 %psum.14 = bf16[8192]{0:T(1024)(128)(2,1)S(1)} all-reduce(bf16[8192]{0:T(1024)(128)(2,1)S(1)} %fusion.38), channel_id=1, replica_groups=mesh['src'=64,'tgt'=4] {'tgt'}, use_global_device_ids=true, to_apply=%region_7.8 | all-reduce | flops 8192 | bytes 32768 | tf_op jit(solution)/shard_map/psum | solution.py:101
  228.0 88.7 %while.83 = (s32[]{:T(128)}, f32[8,8,8,128]{3,2,1,0:T(8,128)S(1)}, f32[8,8,8,128]{3,2,1,0:T(8,128)}, pred[8,8,8]{2,1,0:T(8,128)(4,1)S(1)}, f32[8,8,128]{2,1,0:T(...) while((s32[]{:T(128)}, f32[8,8,8,128]{3,2,1,0:T(8,128)S(1)}, ...), condition=%wide.region_13.14_spmd, body=%wide.region_8.13_spmd.sunk | while | flops 154837184 | bytes 13208881 | solution.py:120
  326.4 81.4 %all-gather.14.cloned.1.call-done = f32[64,1,8192]{2,1,0:T(1,128)} async-done(((f32[1,1,8192]{2,1,0:T(1,128)}), f32[64,1,8192]{2,1,0:T(1,128)}) %all-gather.14.cloned.1.call-update) | async-done | bytes 2097168 | tf_op jit(solution)/shard_map/all_gather | solution.py:26
  412.0 74.2 %all-gather.12.cloned.1.call-done = f32[64,1,8192]{2,1,0:T(1,128)} async-done(((f32[1,1,8192]{2,1,0:T(1,128)}), f32[64,1,8192]{2,1,0:T(1,128)}) %all-gather.12.cloned.1.call-update) | async-done | bytes 2097168 | tf_op jit(solution)/shard_map/all_gather | solution.py:26
  490.4 72.1 %while.84 = (s32[]{:T(128)}, f32[8192]{0:T(1024)S(1)}, f32[8192]{0:T(1024)S(1)}, f32[64,8192]{1,0:T(8,128)}, f32[64,8192]{1,0:T(8,128)}, /*index=5*/s32[]{:T(128)}, s32[]{:T(128)}, s32[]{:T(128)}) while((s32[]{:T(128)}, f32[8192]{0:T(1024)S(1)}, f32[8192]{0:T(1024)S(1)}, f32[64,8192]{1,0:T(8,128)}, f32[64,8192]{1,0:T(8,128)}, ...), condition=%wide.region_17.18_spmd, body=%wide.region_16.17_spmd.sunk | while | flops 49157 | bytes 327811 | solution.py:32
  562.5 116.0 %while.85 = (s32[]{:T(128)}, f32[8,8,128]{2,1,0:T(8,128)S(1)}, f32[8,8,128]{2,1,0:T(8,128)S(1)}, pred[8,8,8]{2,1,0:T(8,128)(4,1)S(1)}, s32[8,8,8]{2,1,0:T(8,128)...) while((s32[]{:T(128)}, f32[8,8,128]{2,1,0:T(8,128)S(1)}, ...), condition=%wide.region_23.24_spmd, body=%wide.region_18.23_spmd.sunk | while | flops 154851520 | bytes 13122609 | solution.py:97
  568.2 5.8 fusion.73
  582.7 5.8 fusion.73
  626.2 5.8 fusion.73
  655.2 5.8 fusion.73
  678.6 13.1 %pmax.15 = bf16[8192]{0:T(1024)(128)(2,1)S(1)} all-reduce(bf16[8192]{0:T(1024)(128)(2,1)S(1)} %bitcast_convert_fusion), channel_id=1, replica_groups=mesh['src'=64,'tgt'=4] {'tgt'}, use_global_device_ids=true, to_apply=%region_24.25 | all-reduce | flops 8192 | bytes 32768 | tf_op jit(solution)/shard_map/pmax | solution.py:100
  691.7 10.8 %psum.15 = bf16[8192]{0:T(1024)(128)(2,1)S(1)} all-reduce(bf16[8192]{0:T(1024)(128)(2,1)S(1)} %fusion.44), channel_id=1, replica_groups=mesh['src'=64,'tgt'=4] {'tgt'}, use_global_device_ids=true, to_apply=%region_25.26 | all-reduce | flops 8192 | bytes 32768 | tf_op jit(solution)/shard_map/psum | solution.py:101
  703.3 88.7 %while.86 = (s32[]{:T(128)}, f32[8,8,8,128]{3,2,1,0:T(8,128)S(1)}, f32[8,8,8,128]{3,2,1,0:T(8,128)}, pred[8,8,8]{2,1,0:T(8,128)(4,1)S(1)}, f32[8,8,128]{2,1,0:T(...) while((s32[]{:T(128)}, f32[8,8,8,128]{3,2,1,0:T(8,128)S(1)}, ...), condition=%wide.region_31.32_spmd, body=%wide.region_26.31_spmd.sunk | while | flops 154837184 | bytes 13208881 | solution.py:120
  800.0 80.1 %all-gather.18.cloned.1.call-done = f32[64,1,8192]{2,1,0:T(1,128)} async-done(((f32[1,1,8192]{2,1,0:T(1,128)}), f32[64,1,8192]{2,1,0:T(1,128)}) %all-gather.18.cloned.1.call-update) | async-done | bytes 2097168 | tf_op jit(solution)/shard_map/all_gather | solution.py:26
  884.2 73.4 %all-gather.16.cloned.1.call-done = f32[64,1,8192]{2,1,0:T(1,128)} async-done(((f32[1,1,8192]{2,1,0:T(1,128)}), f32[64,1,8192]{2,1,0:T(1,128)}) %all-gather.16.cloned.1.call-update) | async-done | bytes 2097168 | tf_op jit(solution)/shard_map/all_gather | solution.py:26
  961.9 72.1 %while.87 = (s32[]{:T(128)}, f32[8192]{0:T(1024)S(1)}, f32[8192]{0:T(1024)S(1)}, f32[64,8192]{1,0:T(8,128)}, f32[64,8192]{1,0:T(8,128)}, /*index=5*/s32[]{:T(128)}, s32[]{:T(128)}, s32[]{:T(128)}) while((s32[]{:T(128)}, f32[8192]{0:T(1024)S(1)}, f32[8192]{0:T(1024)S(1)}, f32[64,8192]{1,0:T(8,128)}, f32[64,8192]{1,0:T(8,128)}, ...), condition=%wide.region_35.36_spmd, body=%wide.region_34.35_spmd.sunk | while | flops 49157 | bytes 327811 | solution.py:32
  (664 shorter events, 538.9 us)
Async XLA Ops:
  7.2 78.1 %all-gather.10.cloned.1.call-start = ((), (), s32[]{:S(2)}) async-start(), calls=%async_computation | async-start | bytes 1064960 | tf_op jit(solution)/shard_map/all_gather | solution.py:62
  7.9 399.9 %all-gather.14.cloned.1.call-start = ((), (), s32[]{:S(2)}) async-start(), calls=%async_computation.2 | async-start | bytes 2129920 | tf_op jit(solution)/shard_map/all_gather | solution.py:26
  319.0 6.7 copy-start.1
  325.6 160.5 %all-gather.12.cloned.1.call-start = ((), (), s32[]{:S(2)}) async-start(), calls=%async_computation.1 | async-start | bytes 2129920 | tf_op jit(solution)/shard_map/all_gather | solution.py:26
  326.4 553.7 %all-gather.18.cloned.1.call-start = ((), (), s32[]{:S(2)}) async-start(), calls=%async_computation.4 | async-start | bytes 2129920 | tf_op jit(solution)/shard_map/all_gather | solution.py:26
  407.8 82.6 %slice-start.2 = ((f32[64,1,8192]{2,1,0:T(1,128)}), f32[1,1,8192]{2,1,0:T(1,128)S(1)}, s32[]{:S(2)}) async-start(f32[64,1,8192]{2,1,0:T(1,128)} %all-gather.14.cloned.1.call-done), calls=%async_computation.7 | async-start | bytes 65536 | tf_op jit(solution)/shard_map/slice | solution.py:27
  486.2 4.2 slice-start.3
  792.0 169.9 %copy-start.2 = (f32[8,8,128]{2,1,0:T(8,128)}, f32[8,8,128]{2,1,0:T(8,128)S(1)}, u32[]{:S(2)}) copy-start(f32[8,8,128]{2,1,0:T(8,128)S(1)} %get-tuple-element.1103) | copy-start | bytes 98308
  794.5 4.9 copy-start
  799.4 158.3 %all-gather.16.cloned.1.call-start = ((), (), s32[]{:S(2)}) async-start(), calls=%async_computation.3 | async-start | bytes 2129920 | tf_op jit(solution)/shard_map/all_gather | solution.py:26
  880.0 81.8 %slice-start = ((f32[64,1,8192]{2,1,0:T(1,128)}), f32[1,1,8192]{2,1,0:T(1,128)S(1)}, s32[]{:S(2)}) async-start(f32[64,1,8192]{2,1,0:T(1,128)} %all-gather.18.cloned.1.call-done), calls=%async_computation.5 | async-start | bytes 65536 | tf_op jit(solution)/shard_map/slice | solution.py:27
  957.7 4.2 slice-start.1
Sparse Core Ops, SparseCore 0:
  10.6 74.6 all-gather.9
  325.8 81.9 all-gather.13
  411.2 74.9 all-gather.11
  799.5 80.5 all-gather.17
  882.7 74.9 all-gather.15
where the time goes:
time: 1050 us; the launch traced here: 1040 us
  waiting for transfers between devices  385 us (37%)
  local copies, waits for them, and re-layouts  254 us (24%)
  other arithmetic  194 us (18%)
  matrix products  140 us (13%)
  blocking collectives  47.7 us (5%)
  between operations  14 us (1%)
    all_gather x4, waiting for transfers between devices, joined(): everything = jax.tree.map(lambda part: lax.all_gather(part, axis), array)  309 us
    dot_general x32, matrix products, tile_costs(): jnp.einsum('gid,gkjd->gkij', source_tile, target_tiles, preferred_element...  140 us
    dynamic_slice x126, local copies, waits for them, and re-layouts, turn(): return combine(so_far, jax.tree.map(lambda part: part[k], everything))  136 us
    reduce_sum x32, other arithmetic, tile_costs(): target_sq = jnp.sum(target_f * target_f, axis=-1)  87.8 us
    all_gather x1, waiting for transfers between devices, local(): target_full = lax.all_gather(target_features, 'src', axis=1, tiled=True)[0]  74.2 us
    reduce_sum x16, other arithmetic, row_one_group(): jnp.sum(jnp.where(mask_tile, jnp.exp(scores - peak[:, None, :, None]), 0....  47.5 us
    reduce_sum x16, other arithmetic, column_one_group(): jnp.sum(jnp.where(mask_tile, jnp.exp(scores - peak[:, :, None, :]), 0.0),...  38.3 us
    gather x16, local copies, waits for them, and re-layouts, row_one_group(): costs = tile_costs(source_tile, target_tiles[index_tile])  34.7 us
  transfers between devices with their start and end apart: 5, of which 5 were waited for; matrix products, arithmetic and copies ran while one was open for 1% of the time, Pallas kernels for 0%

commit v1 on v0

v1 whole, which is shorter than its diff:
```python
import functools
import math

import jax
import jax.numpy as jnp
from jax import lax
from jax.experimental import pallas as pl
from jax.experimental.pallas import tpu as pltpu
from jax.sharding import PartitionSpec as P

BLK = 128
DIM = 64
HALF = BLK // 2
NBLK = 64
SLOTS = 8
CHUNK = 4
STRIDE = NBLK + CHUNK
EPSILON = 0.01
NS = 524288
NT = 32768
NY, NZ, NX = 4, 8, 4
RATE = 2.0 / (DIM * EPSILON)
C2 = RATE / math.log(2.0)
LOG_NS = math.log(NS) / RATE
LOG_NT = math.log(NT) / RATE
LOW = -1.0e30
MAX_CHUNKS = 192
MESH = pl.DeviceIdType.MESH
VMEM = pl.BlockSpec(memory_space=pltpu.VMEM)
SMEM = pl.BlockSpec(memory_space=pltpu.SMEM)
f32, bf16 = jnp.float32, jnp.bfloat16


def iota(shape, dim):
    return lax.broadcasted_iota(jnp.int32, shape, dim)


def pieces(v):
    hi = v.astype(bf16).astype(f32)
    rest = v - hi
    mid = rest.astype(bf16).astype(f32)
    return hi, mid, rest - mid


def params(collective_id=None):
    if collective_id is None:
        return pltpu.CompilerParams(vmem_limit_bytes=40 << 20)
    return pltpu.CompilerParams(
        vmem_limit_bytes=40 << 20, collective_id=collective_id, has_side_effects=True
    )


def fold_potential(pot, aug):
    row = iota((HALF, BLK), 0)
    lane = iota((HALF, BLK), 1)
    pick = (lane % HALF == row).astype(bf16)
    n = iota((8, 16, BLK), 1)
    h = iota((8, 16, BLK), 2) // HALF
    keep = ((n < 6) & (n // 3 == h)) | ((n >= 6) & (n < 9) & (h == 0))
    for g in range(8):
        hi, mid, lo = (v[:, None, :] for v in pieces(pot[8 * g : 8 * g + 8, :]))
        rows = jnp.where(
            n >= 6, 1.0, jnp.where(n % 3 == 0, hi, jnp.where(n % 3 == 1, mid, lo))
        )
        rows = jnp.where(keep, rows, 0.0).reshape(BLK, BLK).astype(bf16)
        turned = lax.dot_general(pick, rows, (((1,), (1,)), ((), ())), preferred_element_type=f32)
        for k in range(8):
            aug[8 * g + k] = jnp.where(lane // 16 == k, turned, 0.0).astype(bf16)


def null_tile(aug):
    n = iota((HALF, BLK), 1)
    aug[NBLK] = jnp.where((n == 0) | (n == 3), LOW, 0.0).astype(bf16)


def weight_pattern():
    n = iota((16, BLK), 0)
    left = ((n < 3)).astype(bf16)
    right = ((n >= 3) & (n < 6)).astype(bf16)
    return left, right


def sweep(count, chunk_p, slots, lhs, aug, weights, pattern, pot_rows, bufs, process):
    left, right = pattern
    zero = jnp.zeros((DIM, BLK), bf16)

    def scores(n, buf):
        p = chunk_p[n]
        safe = jnp.minimum(p, NBLK - 1)
        ids = slots(n)
        w = weights(safe)
        if pot_rows is None:
            l16, r16 = left, right
        else:
            extra = pot_rows[safe]
            l16, r16 = left + extra, right + extra
        top = jnp.concatenate([w, zero], axis=1)
        mid = jnp.concatenate([zero, w], axis=1)
        low = jnp.concatenate([l16, r16], axis=1)
        rhs = jnp.concatenate([top, mid] + [low] * 8, axis=0)
        body = jnp.concatenate([lhs[jnp.minimum(q, NBLK - 1)] for q in ids], axis=0)
        tail = jnp.concatenate([aug[q] for q in ids], axis=0)
        both = jnp.concatenate([body, tail], axis=1)
        buf[...] = jnp.dot(both, rhs, preferred_element_type=f32)

    b0, b1, b2, b3 = bufs
    scores(0, b0)
    scores(1, b1)

    @pl.loop(0, (count + 3) // 4)
    def _(turn):
        n = 4 * turn
        scores(n + 2, b2)
        scores(n + 3, b3)
        process(n, chunk_p[n], b0)
        process(n + 1, chunk_p[n + 1], b1)
        scores(n + 4, b0)
        scores(n + 5, b1)
        process(n + 2, chunk_p[n + 2], b2)
        process(n + 3, chunk_p[n + 3], b3)


def max_process(peak, total):
    def process(n, p, buf):
        u = buf[...].reshape(CHUNK * HALF // 8, 8, 2 * BLK)
        top = jnp.max(u, axis=0)
        top = jnp.maximum(top[:, :BLK], top[:, BLK:])
        old = peak[p]
        new = jnp.maximum(old, top)
        new2 = jnp.concatenate([new, new], axis=1)
        e = jnp.sum(jnp.exp2((u - new2[None]) * C2), axis=0)
        peak[p] = new
        total[p] = total[p] * jnp.exp2((old - new) * C2) + (e[:, :BLK] + e[:, BLK:])

    return process


def sum_process(total):
    def process(n, p, buf):
        u = buf[...].reshape(CHUNK * HALF // 8, 8, 2 * BLK)
        e = jnp.sum(jnp.exp2(u * C2), axis=0)
        total[p] = total[p] + (e[:, :BLK] + e[:, BLK:])

    return process


def init_peaks(peak, total):
    peak[...] = jnp.full(peak.shape, LOW, f32)
    total[...] = jnp.zeros(total.shape, f32)


def finish_peaks(peak, total):
    m = peak[0:NBLK]
    top = jnp.max(m, axis=1)
    s = jnp.sum(total[0:NBLK] * jnp.exp2((m - top[:, None, :]) * C2), axis=1)
    return top + jnp.log2(s) * (1.0 / C2)


def row_chunks(bt, chunk_p, chunk_b):
    def step(p, n):
        chunk_p[n] = p
        chunk_b[n] = p * SLOTS
        more = (bt[p * SLOTS + CHUNK] >= 0).astype(jnp.int32)
        chunk_p[n + 1] = p
        chunk_b[n + 1] = p * SLOTS + CHUNK
        return n + 1 + more

    count = lax.fori_loop(0, NBLK, step, 0)
    for k in range(6):
        chunk_p[count + k] = NBLK
        chunk_b[count + k] = 0
    return count


def row_slots(bt, chunk_p, chunk_b):
    def slots(n):
        base, live = chunk_b[n], chunk_p[n] < NBLK
        ids = [bt[base + k] for k in range(CHUNK)]
        return [jnp.where((v >= 0) & live, v, NBLK) for v in ids]

    return slots


def col_chunks(lists, chunk_p, chunk_b):
    def step(t, n):
        size = lists[NBLK * STRIDE + t]
        for c in range(NBLK // CHUNK):
            chunk_p[n + c] = t
            chunk_b[n + c] = t * STRIDE + c * CHUNK
        return n + (size + CHUNK - 1) // CHUNK

    count = lax.fori_loop(0, NBLK, step, 0)
    for k in range(6):
        chunk_p[count + k] = NBLK
        chunk_b[count + k] = 0
    return count


def col_slots(lists, chunk_p, chunk_b):
    def slots(n):
        base, p = chunk_b[n], chunk_p[n]
        size = jnp.where(p < NBLK, lists[NBLK * STRIDE + jnp.minimum(p, NBLK - 1)], 0)
        first = base - p * STRIDE
        return [jnp.where(first + k < size, lists[base + k], NBLK) for k in range(CHUNK)]

    return slots


def row1_kernel(bt, yfold, xt, out, lists, aug, peak, total, chunk_p, chunk_b, b0, b1, b2, b3):
    k = iota((2 * BLK, BLK), 0) % BLK // DIM
    n = iota((2 * BLK, BLK), 1) % 16
    take = jnp.where((n < 6) & (n // 3 == k), -0.5, 0.0).astype(bf16)
    lane = iota((4 * HALF, BLK), 1)

    @pl.loop(0, NBLK // 4)
    def _(g):
        y = jnp.concatenate([yfold[4 * g + i] for i in range(4)], axis=0).astype(f32)
        sq = y * y
        hi = sq.astype(bf16)
        lo = (sq - hi.astype(f32)).astype(bf16)
        v = jnp.dot(jnp.concatenate([hi, lo], axis=1), take, preferred_element_type=f32)
        p0, p1, p2 = pieces(v)
        l = lane % 16
        v = jnp.where(l >= 6, jnp.where(l < 9, 1.0, 0.0), jnp.where(l % 3 == 0, p0, jnp.where(l % 3 == 1, p1, p2)))
        for i in range(4):
            part = v[i * HALF : (i + 1) * HALF]
            mine = lane[:HALF] // 16 == (4 * g + i) % 8
            aug[4 * g + i] = jnp.where(mine, part, 0.0).astype(bf16)

    null_tile(aug)
    init_peaks(peak, total)
    for t in range(NBLK + 1):
        lists[NBLK * STRIDE + t] = 0
    count = row_chunks(bt, chunk_p, chunk_b)
    slots = row_slots(bt, chunk_p, chunk_b)
    work = max_process(peak, total)

    def process(n, p, buf):
        for v in slots(n):
            at = lists[NBLK * STRIDE + v]
            at = jnp.where(v < NBLK, at, 0)
            lists[jnp.where(v < NBLK, v * STRIDE + at, NBLK * STRIDE + NBLK + 1)] = p
            lists[NBLK * STRIDE + v] = at + 1
        work(n, p, buf)

    sweep(
        count, chunk_p, slots, yfold, aug,
        lambda p: xt[:, pl.ds(pl.multiple_of(p * BLK, BLK), BLK)],
        weight_pattern(), None, (b0, b1, b2, b3), process,
    )
    out[...] = finish_peaks(peak, total)


def col1_kernel(lists, a, xfold, yt, out, aug, peak, total, chunk_p, chunk_b, b0, b1, b2, b3):
    fold_potential(a, aug)
    null_tile(aug)
    init_peaks(peak, total)
    count = col_chunks(lists, chunk_p, chunk_b)
    sweep(
        count, chunk_p, col_slots(lists, chunk_p, chunk_b), xfold, aug, lambda t: yt[t],
        weight_pattern(), None, (b0, b1, b2, b3), max_process(peak, total),
    )
    out[...] = finish_peaks(peak, total)


def spread_rows(pot, rows):
    n = iota((8, 16, BLK), 1)
    for g in range(8):
        hi, mid, lo = (v[:, None, :] for v in pieces(pot[8 * g : 8 * g + 8, :]))
        v = jnp.where(n == 6, hi, jnp.where(n == 7, mid, jnp.where(n == 8, lo, 0.0)))
        rows[8 * g : 8 * g + 8] = v.astype(bf16)


def row2_kernel(bt, a, b, yfold, xt, out, aug, rows, total, chunk_p, chunk_b, b0, b1, b2, b3):
    fold_potential(b, aug)
    null_tile(aug)
    spread_rows(a, rows)
    total[...] = jnp.zeros(total.shape, f32)
    count = row_chunks(bt, chunk_p, chunk_b)
    sweep(
        count, chunk_p, row_slots(bt, chunk_p, chunk_b), yfold, aug,
        lambda p: xt[:, pl.ds(pl.multiple_of(p * BLK, BLK), BLK)],
        weight_pattern(), rows, (b0, b1, b2, b3), sum_process(total),
    )
    out[...] = jnp.sum(total[0:NBLK], axis=1)


def col2_kernel(lists, a, b, xfold, yt, xt, out, f_out, aug, rows, total, chunk_p, chunk_b, b0, b1, b2, b3):
    fold_potential(a, aug)
    null_tile(aug)
    spread_rows(b, rows)
    total[...] = jnp.zeros(total.shape, f32)
    count = col_chunks(lists, chunk_p, chunk_b)

    @pl.loop(0, NBLK)
    def _(p):
        x = xt[:, pl.ds(pl.multiple_of(p * BLK, BLK), BLK)].astype(f32)
        sq = jnp.sum(x * x, axis=0, keepdims=True)
        f_out[pl.ds(p, 1), :] = a[pl.ds(p, 1), :] * (1.0 / 32) + sq * (1.0 / 64)

    sweep(
        count, chunk_p, col_slots(lists, chunk_p, chunk_b), xfold, aug, lambda t: yt[t],
        weight_pattern(), rows, (b0, b1, b2, b3), sum_process(total),
    )
    out[...] = jnp.sum(total[0:NBLK], axis=1)


def work_scratch(peaks, rows):
    acc = pltpu.VMEM((NBLK + 1, 8, BLK), f32)
    kinds = [pltpu.VMEM((NBLK + 1, HALF, BLK), bf16)]
    if rows:
        kinds.append(pltpu.VMEM((NBLK, 16, BLK), bf16))
    kinds += [acc] * (2 if peaks else 1)
    kinds += [pltpu.SMEM((MAX_CHUNKS + 16,), jnp.int32)] * 2
    kinds += [pltpu.VMEM((CHUNK * HALF, 2 * BLK), f32)] * 4
    return kinds


def duals(n=NBLK):
    return jax.ShapeDtypeStruct((n, BLK), f32)


def place():
    i = lax.axis_index("src")
    core, z, y = lax.rem(i, 2), lax.rem(i // 2, NZ), i // (2 * NZ)
    return y, z, core


def at(y, z, core):
    return {"src": (y * NZ + z) * 2 + core}


def greet(devices):
    barrier = pltpu.get_barrier_semaphore()
    for d in devices:
        pl.semaphore_signal(barrier, inc=1, device_id=d, device_id_type=MESH)
    pl.semaphore_wait(barrier, len(devices))


def send(src, dst, sends, recvs, k, device):
    copy = pltpu.make_async_remote_copy(
        src_ref=src, dst_ref=dst, send_sem=sends.at[k], recv_sem=recvs.at[k],
        device_id=device, device_id_type=MESH,
    )
    copy.start()
    return copy


def gather_kernel(y_ref, out, zs, zr, ys, yr, cs, cr, ls):
    y, z, core = place()
    z_devices = [at(y, lax.rem(z + k, NZ), core) for k in range(1, NZ)]
    y_devices = [at(lax.rem(y + k, NY), z, core) for k in range(1, NY)]
    mate = at(y, z, 1 - core)
    mine = pltpu.make_async_copy(y_ref, out.at[y, z, core], ls.at[0])
    mine.start()
    greet(z_devices + y_devices + [mate])
    copies = [send(y_ref, out.at[y, z, core], zs, zr, k, d) for k, d in enumerate(z_devices)]
    mine.wait()
    for c in copies:
        c.wait()
    copies = [
        send(out.at[y, :, core], out.at[y, :, core], ys, yr, k, d)
        for k, d in enumerate(y_devices)
    ]
    for c in copies:
        c.wait()
    last = send(out.at[:, :, core], out.at[:, :, core], cs, cr, 0, mate)
    last.wait()


def gather(tile):
    dma = pltpu.SemaphoreType.DMA
    return pl.pallas_call(
        gather_kernel,
        out_shape=jax.ShapeDtypeStruct((NY, NZ, 2, HALF, BLK), bf16),
        in_specs=[VMEM],
        out_specs=VMEM,
        scratch_shapes=[dma((7,)), dma((7,)), dma((3,)), dma((3,)), dma((1,)), dma((1,)), dma((1,))],
        compiler_params=params(0),
    )(tile)


def tgt_exchange(l_ref, got, sends, recvs):
    me = lax.axis_index("tgt")
    devices = [{"tgt": lax.rem(me + k, NX)} for k in range(1, NX)]
    greet(devices)
    copies = [send(l_ref, got.at[me], sends, recvs, k, d) for k, d in enumerate(devices)]
    got[me] = l_ref[...]
    for c in copies:
        c.wait()


def tgt1_kernel(l_ref, a_ref, got, sends, recvs):
    tgt_exchange(l_ref, got, sends, recvs)
    parts = [got[k] for k in range(NX)]
    top = functools.reduce(jnp.maximum, parts)
    s = sum(jnp.exp2((v - top) * C2) for v in parts)
    a_ref[...] = -(top + jnp.log2(s) * (1.0 / C2)) - LOG_NS


def tgt2_kernel(l_ref, old, a_ref, got, sends, recvs):
    tgt_exchange(l_ref, got, sends, recvs)
    s = (got[0] + got[1]) + (got[2] + got[3])
    a_ref[...] = old[...] - jnp.log2(s * NS) * (1.0 / C2)


def tgt_call(kernel, collective_id, *args):
    dma = pltpu.SemaphoreType.DMA
    return pl.pallas_call(
        kernel,
        out_shape=duals(),
        in_specs=[VMEM] * len(args),
        out_specs=VMEM,
        scratch_shapes=[pltpu.VMEM((NX, NBLK, BLK), f32), dma((3,)), dma((3,))],
        compiler_params=params(collective_id),
    )(*args)


def src_reduce(l_ref, combine, order, r1, rows, r2, s1, q1, s2, q2, more):
    y, z, core = place()
    m = y * 2 + core

    def side(k):
        other = lax.rem(m + k, 8)
        return other, at(other // 2, z, lax.rem(other, 2))

    def up(k):
        other = lax.rem(z + k, NZ)
        return other, at(y, other, core)

    sides, ups = [side(k) for k in range(1, 8)], [up(k) for k in range(1, 8)]
    for k in range(8):
        order[k] = l_ref[pl.ds((k // 2) * 2 * NZ + k % 2, NZ, stride=2), :]
    greet([d for _, d in sides + ups])
    copies = [send(order.at[o], r1.at[m], s1, q1, k, d) for k, (o, d) in enumerate(sides)]
    r1[m] = order[m]
    for c in copies:
        c.wait()
    first = combine([r1[k] for k in range(8)])
    for k in range(8):
        rows[k] = jnp.broadcast_to(first[k : k + 1], (8, BLK))
    copies = [send(rows.at[o], r2.at[z], s2, q2, k, d) for k, (o, d) in enumerate(ups)]
    r2[z] = rows[z]
    for c in copies:
        c.wait()
    return combine([r2[k] for k in range(8)]), m, z, sides, ups


def lse(parts):
    top = functools.reduce(jnp.maximum, parts)
    s = sum(jnp.exp2((v - top) * C2) for v in parts)
    return top + jnp.log2(s) * (1.0 / C2)


def src1_kernel(l_ref, b_ref, own_ref, order, r1, rows, r2, r3, tile, r4, s1, q1, s2, q2, s3, q3, s4, q4):
    total, m, z, sides, ups = src_reduce(l_ref, lse, order, r1, rows, r2, s1, q1, s2, q2, None)
    own_ref[...] = -total - LOG_NT
    copies = [send(own_ref, r3.at[z], s3, q3, k, d) for k, (_, d) in enumerate(ups)]
    r3[z] = own_ref[...]
    for c in copies:
        c.wait()
    tile[...] = jnp.concatenate([r3[k][0:1] for k in range(8)], axis=0)
    copies = [send(tile, r4.at[m], s4, q4, k, d) for k, (_, d) in enumerate(sides)]
    r4[m] = tile[...]
    for c in copies:
        c.wait()
    for k in range(8):
        b_ref[pl.ds((k // 2) * 2 * NZ + k % 2, NZ, stride=2), :] = r4[k]


def src2_kernel(l_ref, old, yt_ref, g_ref, order, r1, rows, r2, s1, q1, s2, q2):
    total = src_reduce(l_ref, sum, order, r1, rows, r2, s1, q1, s2, q2, None)[0]
    y = yt_ref[...].astype(f32)
    sq = jnp.sum(y * y, axis=0, keepdims=True)
    b = old[...] - jnp.log2(total * NT) * (1.0 / C2)
    g_ref[...] = b * (1.0 / 32) + sq * (1.0 / 64)


def src_scratch(phases):
    block = pltpu.VMEM((8, 8, BLK), f32)
    kinds = [block] * 4
    if phases == 4:
        kinds += [block, pltpu.VMEM((8, BLK), f32), block]
    return kinds + [pltpu.SemaphoreType.DMA((7,))] * (2 * phases)


def local(source_features, target_features, block_targets):
    xt = source_features.T
    yt_own = target_features[0].T
    bt = block_targets.reshape(-1)
    y_tile = target_features[0].reshape(2, HALF, DIM).transpose(1, 0, 2).reshape(HALF, BLK)
    xfold = source_features.reshape(NBLK, 2, HALF, DIM).transpose(0, 2, 1, 3).reshape(NBLK, HALF, BLK)
    yfold = gather(y_tile).reshape(NBLK, HALF, BLK)
    yt = yfold.reshape(NBLK, HALF, 2, DIM).transpose(0, 3, 2, 1).reshape(NBLK, DIM, BLK)

    row_lse, lists = pl.pallas_call(
        row1_kernel,
        out_shape=(duals(), jax.ShapeDtypeStruct((NBLK * STRIDE + 128,), jnp.int32)),
        in_specs=[SMEM, VMEM, VMEM],
        out_specs=(VMEM, SMEM),
        scratch_shapes=work_scratch(True, False),
        compiler_params=params(),
    )(bt, yfold, xt)
    a = tgt_call(tgt1_kernel, 1, row_lse)
    col_lse = pl.pallas_call(
        col1_kernel,
        out_shape=duals(),
        in_specs=[SMEM, VMEM, VMEM, VMEM],
        out_specs=VMEM,
        scratch_shapes=work_scratch(True, False),
        compiler_params=params(),
    )(lists, a, xfold, yt)
    b, own = pl.pallas_call(
        src1_kernel,
        out_shape=(duals(), duals(8)),
        in_specs=[VMEM],
        out_specs=(VMEM, VMEM),
        scratch_shapes=src_scratch(4),
        compiler_params=params(2),
    )(col_lse)
    row_sum = pl.pallas_call(
        row2_kernel,
        out_shape=duals(),
        in_specs=[SMEM, VMEM, VMEM, VMEM, VMEM],
        out_specs=VMEM,
        scratch_shapes=work_scratch(False, True),
        compiler_params=params(),
    )(bt, a, b, yfold, xt)
    a = tgt_call(tgt2_kernel, 3, row_sum, a)
    col_sum, f = pl.pallas_call(
        col2_kernel,
        out_shape=(duals(), duals()),
        in_specs=[SMEM, VMEM, VMEM, VMEM, VMEM, VMEM],
        out_specs=(VMEM, VMEM),
        scratch_shapes=work_scratch(False, True),
        compiler_params=params(),
    )(lists, a, b, xfold, yt, xt)
    g = pl.pallas_call(
        src2_kernel,
        out_shape=duals(8),
        in_specs=[VMEM, VMEM, VMEM],
        out_specs=VMEM,
        scratch_shapes=src_scratch(2),
        compiler_params=params(4),
    )(col_sum, own, yt_own)
    return f.reshape(-1), g[0:1]


def solution(mesh):
    in_specs = (P("src", None), P("tgt", "src", None), P("src", "tgt", None))
    out_specs = (P("src"), P("tgt", "src"))
    return jax.shard_map(local, mesh=mesh, in_specs=in_specs, out_specs=out_specs, check_vma=False)
```

time: 1050 us -> 154 us (0.15)
  waiting for transfers between devices: 385 us -> 0 us
  local copies, waits for them, and re-layouts: 254 us -> 32.3 us
  other arithmetic: 194 us -> 0 us
  matrix products: 140 us -> 0 us
  Pallas kernels: 0 us -> 121 us
  blocking collectives: 47.7 us -> 0 us
  between operations: 14 us -> 0.76 us
    all_gather x5 -> x0, waiting for transfers between devices: 383 us -> none  [the longest x4 309 us: joined(): everything = jax.tree.map(lambda part: lax.all_gather(part, axis), array)]
    reduce_sum x96 -> x0, other arithmetic: 175 us -> none  [the longest x32 87.8 us: tile_costs(): target_sq = jnp.sum(target_f * target_f, axis=-1)]
    dot_general x32 -> x0, matrix products: 140 us -> none  [tile_costs(): jnp.einsum('gid,gkjd->gkij', source_tile, target_tiles, preferred_element...]
    dynamic_slice x126 -> x0, local copies, waits for them, and re-layouts: 136 us -> none  [turn(): return combine(so_far, jax.tree.map(lambda part: part[k], everything))]
    pallas_call x0 -> x9, Pallas kernels: none -> 121 us  [the longest x1 24.7 us: local(): pl.pallas_call(src1_kernel, out_shape=(duals(), duals(8)), in_specs=[VMEM...]
    gather x50 -> x0, local copies, waits for them, and re-layouts: 81.6 us -> none  [the longest x16 34.7 us: row_one_group(): costs = tile_costs(source_tile, target_tiles[index_tile])]
    pmax x2 -> x0, blocking collectives: 26.1 us -> none  [local(): row_peak = lax.pmax(as_sent(row_peaks), 'tgt').astype(row_peaks.dtype)]
    psum x2 -> x0, blocking collectives: 21.6 us -> none  [local(): lax.psum((row_totals * jnp.exp(row_peaks - row_peak)).astype(jnp.bfloat16...]
  transfers between devices with their start and end apart: 5 -> 0, of which waited for: 5 -> 0; matrix products, arithmetic and copies ran while one was open for 1% -> 0% of each run, Pallas kernels for 0% -> 0%
where the time goes in v1:
time: 154 us
  Pallas kernels  121 us (79%)
  local copies, waits for them, and re-layouts  32.3 us (21%)
    pallas_call x1, Pallas kernels, local(): pl.pallas_call(src1_kernel, out_shape=(duals(), duals(8)), in_specs=[VMEM...  24.7 us
    pallas_call x1, Pallas kernels, gather(): pl.pallas_call(gather_kernel, out_shape=jax.ShapeDtypeStruct((NY, NZ, 2,...  23.5 us
    reshape x3, local copies, waits for them, and re-layouts, local(): source_features.reshape(NBLK, 2, HALF, DIM).transpose(0, 2, 1, 3)  16.2 us
    pallas_call x1, Pallas kernels, local(): pl.pallas_call(row1_kernel, out_shape=(duals(), jax.ShapeDtypeStruct((NBL...  15.6 us
    pallas_call x1, Pallas kernels, local(): pl.pallas_call(col2_kernel, out_shape=(duals(), duals()), in_specs=[SMEM,...  13 us
    pallas_call x1, Pallas kernels, local(): pl.pallas_call(col1_kernel, out_shape=duals(), in_specs=[SMEM, VMEM, VMEM...  11.9 us
    pallas_call x1, Pallas kernels, local(): pl.pallas_call(src2_kernel, out_shape=duals(8), in_specs=[VMEM, VMEM, VME...  11.5 us
    pallas_call x2, Pallas kernels, tgt_call(): pl.pallas_call(kernel, out_shape=duals(), in_specs=[VMEM] * len(args), ou...  11 us

profile of v1, /device:TPU:1, one launch (start us, length us, event | category | flops | bytes accessed | tf_op | source)
XLA Modules:
  0.0 153.8 jit_solution(1385017728309100766)
XLA Ops:
  0.6 0.8 copy.8
  1.4 0.1 reshape.25.bt
  1.5 0.8 reshape_squeeze.3
  2.3 0.1 copy.9
  2.4 0.1 reshape.26.y_ref
  2.5 23.5 %shard_map.50 = bf16[4,8,2,64,128]{4,3,2,1,0:T(8,128)(2,1)S(1)} custom-call(bf16[64,128]{1,0:T(8,128)(2,1)S(1)} %reshape.26.y_ref), custom_call_target="tpu_custom_call" | custom-call | tf_op jit(solution)/shard_map/pallas_call | solution.py:373
  26.1 1.2 copy-done
  27.3 15.6 %shard_map.51 = (f32[64,128]{1,0:T(8,128)S(1)}, s32[4480]{0:T(1024)S(1)}) custom-call(s32[512]{0:T(512)S(1)} %reshape.25.bt, bf16[64,64,128]{2,1,0:T(8,128)(2,1)S(1)} %bitcast.20, bf16[64,8192]{1,0:T(8,128)(2,1)S(1)} %bitcast.17), custom_call_target="tpu_custom_call" | custom-call | tf_op jit(solution)/shard_map/pallas_call | solution.py:496
  42.9 5.4 %shard_map.52.a.old = f32[64,128]{1,0:T(8,128)S(1)} custom-call(f32[64,128]{1,0:T(8,128)S(1)} %get-tuple-element.9.l_ref), custom_call_target="tpu_custom_call" | custom-call | tf_op jit(solution)/shard_map/pallas_call | solution.py:409
  48.3 0.9 reshape_reshape.3
  49.2 6.4 %copy.11 = bf16[64,64,2,64]{1,2,3,0:T(2,128)(2,1)} copy(bf16[64,64,2,64]{3,2,1,0:T(2,128)(2,1)S(1)} %reshape_reshape.3) | data formatting | bytes 2097152 | tf_op jit(solution)/shard_map/reshape;reshape | solution.py:494
  55.6 4.0 %reshape.30.yt = bf16[64,64,128]{2,1,0:T(8,128)(2,1)S(1)} reshape(bf16[64,64,2,64]{3,2,1,0:T(2,128)(2,1)} %bitcast.23) | data formatting | bytes 2097152 | tf_op jit(solution)/shard_map/reshape | solution.py:494
  59.6 3.3 %reshape.28 = bf16[64,2,64,64]{2,1,0,3:T(2,128)(2,1)} reshape(bf16[8192,64]{0,1:T(8,128)(2,1)S(1)} %copy-done.1) | data formatting | bytes 2097152 | tf_op jit(solution)/shard_map/reshape | solution.py:492
  62.9 8.1 %copy.10 = bf16[64,2,64,64]{3,1,2,0:T(2,128)(2,1)} copy(bf16[64,2,64,64]{2,1,0,3:T(2,128)(2,1)} %reshape.28) | data formatting | bytes 2097152 | tf_op jit(solution)/shard_map/reshape | solution.py:492
  71.0 4.7 %reshape.29.xfold = bf16[64,64,128]{2,1,0:T(8,128)(2,1)} reshape(bf16[64,64,2,64]{3,2,1,0:T(2,128)(2,1)} %bitcast.24) | data formatting | bytes 2097152 | tf_op jit(solution)/shard_map/reshape | solution.py:492
  75.8 1.2 copy-done.2
  77.0 11.9 %shard_map.53.l_ref = f32[64,128]{1,0:T(8,128)S(1)} custom-call(s32[4480]{0:T(1024)S(1)} %get-tuple-element.8.lists, f32[64,128]{1,0:T(8,128)S(1)} %shard_map.52.a.old, bf16[64,64,128]{2,1,0:T(8,128)(2,1)S(1)} %copy-done.2, bf16[64,64,128]{2,1,0:T(8,128)(2,1)S(1)} %reshape.30.yt), custom_call_target="tpu_custom_call" | custom-call | tf_op jit(solution)/shard_map/pallas_call | solution.py:505
  88.8 24.7 %shard_map.54 = (f32[64,128]{1,0:T(8,128)S(1)}, f32[8,128]{1,0:T(8,128)S(1)}) custom-call(f32[64,128]{1,0:T(8,128)S(1)} %shard_map.53.l_ref), custom_call_target="tpu_custom_call" | custom-call | tf_op jit(solution)/shard_map/pallas_call | solution.py:513
  113.5 9.6 %shard_map.55.l_ref = f32[64,128]{1,0:T(8,128)S(1)} custom-call(s32[512]{0:T(512)S(1)} %reshape.25.bt, f32[64,128]{1,0:T(8,128)S(1)} %shard_map.52.a.old, f32[64,128]{1,0:T(8,128)S(1)} %get-tuple-element.10.b, bf16[64,64,128]{2,1,0:T(8,128)(2,1)S(1)} %bitcast.21, bf16[64,8192]{1,0:T(8,128)(2,1)S(1)} %bitcast.18), custom_call_target="tpu_custom_call" | custom-call | tf_op jit(solution)/shard_map/pallas_call | solution.py:521
  123.1 0.0 copy-start.4
  123.1 5.6 %shard_map.56.a = f32[64,128]{1,0:T(8,128)S(1)} custom-call(f32[64,128]{1,0:T(8,128)S(1)} %shard_map.55.l_ref, f32[64,128]{1,0:T(8,128)S(1)} %shard_map.52.a.old), custom_call_target="tpu_custom_call" | custom-call | tf_op jit(solution)/shard_map/pallas_call | solution.py:409
  128.8 13.0 %shard_map.57 = (f32[64,128]{1,0:T(8,128)S(1)}, f32[64,128]{1,0:T(8,128)}) custom-call(s32[4480]{0:T(1024)S(1)} %get-tuple-element.8.lists, f32[64,128]{1,0:T(8,128)S(1)} %shard_map.56.a, f32[64,128]{1,0:T(8,128)S(1)} %get-tuple-element.10.b, bf16[64,64,128]{2,1,0:T(8,128)(2,1)S(1)} %copy-done.3, bf16[64,64,128]{2,1,0:T(8,128)(2,1)S(1)} %reshape.30.yt, ...), custom_call_target="tpu_custom_call" | custom-call | tf_op jit(solution)/shard_map/pallas_call | solution.py:530
  141.8 11.5 %shard_map.58 = f32[8,128]{1,0:T(8,128)S(1)} custom-call(f32[64,128]{1,0:T(8,128)S(1)} %get-tuple-element.12.l_ref, f32[8,128]{1,0:T(8,128)S(1)} %get-tuple-element.13.old, bf16[64,128]{1,0:T(8,128)(2,1)S(1)} %bitcast.22), custom_call_target="tpu_custom_call" | custom-call | tf_op jit(solution)/shard_map/pallas_call | solution.py:538
  153.3 0.5 slice.3
  (7 shorter events, 0.0 us)
Async XLA Ops:
  26.0 1.2 copy-start
  55.6 4.0 %copy-start.1 = (bf16[8192,64]{0,1:T(8,128)(2,1)S(1)}, bf16[8192,64]{0,1:T(8,128)(2,1)}, u32[]{:S(2)}) copy-start(bf16[8192,64]{0,1:T(8,128)(2,1)} %param.3) | copy-start | bytes 3145732
  75.7 1.2 copy-start.2
  77.0 51.8 %copy-start.3 = (bf16[64,64,128]{2,1,0:T(8,128)(2,1)S(1)}, bf16[64,64,128]{2,1,0:T(8,128)(2,1)}, u32[]{:S(2)}) copy-start(bf16[64,64,128]{2,1,0:T(8,128)(2,1)} %reshape.29.xfold) | copy-start | bytes 3145732
  123.1 18.7 %copy-start.4 = (bf16[1,128,64]{1,2,0:T(8,128)(2,1)S(1)}, bf16[1,128,64]{1,2,0:T(8,128)(2,1)}, u32[]{:S(2)}) copy-start(bf16[1,128,64]{1,2,0:T(8,128)(2,1)} %param.4) | copy-start | bytes 49156

commit v2 on v0

v2 whole, which is shorter than its diff:
```python
import functools
import math

import jax
import jax.numpy as jnp
from jax import lax
from jax.experimental import pallas as pl
from jax.experimental.pallas import tpu as pltpu
from jax.sharding import PartitionSpec as P

BLK = 128
DIM = 64
HALF = BLK // 2
NBLK = 64
SLOTS = 8
CHUNK = 4
STRIDE = NBLK + CHUNK
EPSILON = 0.01
NS = 524288
NT = 32768
NY, NZ, NX = 4, 8, 4
RATE = 2.0 / (DIM * EPSILON)
C2 = RATE / math.log(2.0)
LOG_NS = math.log(NS) / RATE
LOG_NT = math.log(NT) / RATE
LOW = -1.0e30
BODY = 16
MESH = pl.DeviceIdType.MESH
VMEM = pl.BlockSpec(memory_space=pltpu.VMEM)
SMEM = pl.BlockSpec(memory_space=pltpu.SMEM)
f32, bf16 = jnp.float32, jnp.bfloat16


def iota(shape, dim):
    return lax.broadcasted_iota(jnp.int32, shape, dim)


def pieces(v):
    hi = v.astype(bf16).astype(f32)
    rest = v - hi
    mid = rest.astype(bf16).astype(f32)
    return hi, mid, rest - mid


def params(collective_id=None):
    if collective_id is None:
        return pltpu.CompilerParams(vmem_limit_bytes=40 << 20)
    return pltpu.CompilerParams(
        vmem_limit_bytes=40 << 20, collective_id=collective_id, has_side_effects=True
    )


def picker():
    return (iota((HALF, BLK), 1) % HALF == iota((HALF, BLK), 0)).astype(bf16)


def turn_over(pick, rows):
    return lax.dot_general(pick, rows, (((1,), (1,)), ((), ())), preferred_element_type=f32)


def fold(pick, tile):
    low = (iota((DIM, BLK), 1) < HALF).astype(bf16)
    rows = jnp.concatenate([tile * low, tile * (1.0 - low).astype(bf16)], axis=0)
    return turn_over(pick, rows).astype(bf16)


def fold_potential(pot, aug):
    lane = iota((HALF, BLK), 1)
    pick = picker()
    n = iota((8, 16, BLK), 1)
    h = iota((8, 16, BLK), 2) // HALF
    keep = ((n < 6) & (n // 3 == h)) | ((n >= 6) & (n < 9) & (h == 0))
    for g in range(8):
        hi, mid, lo = (v[:, None, :] for v in pieces(pot[8 * g : 8 * g + 8, :]))
        rows = jnp.where(
            n >= 6, 1.0, jnp.where(n % 3 == 0, hi, jnp.where(n % 3 == 1, mid, lo))
        )
        rows = jnp.where(keep, rows, 0.0).reshape(BLK, BLK).astype(bf16)
        turned = turn_over(pick, rows)
        for k in range(8):
            aug[8 * g + k] = jnp.where(lane // 16 == k, turned, 0.0).astype(bf16)
    n = iota((HALF, BLK), 1)
    aug[NBLK] = jnp.where((n == 0) | (n == 3), LOW, 0.0).astype(bf16)


def spread_rows(pot, rows):
    n = iota((8, 16, BLK), 1)
    for g in range(8):
        hi, mid, lo = (v[:, None, :] for v in pieces(pot[8 * g : 8 * g + 8, :]))
        v = jnp.where(n == 6, hi, jnp.where(n == 7, mid, jnp.where(n == 8, lo, 0.0)))
        rows[8 * g : 8 * g + 8] = v.astype(bf16)


def sweep(chunks, slots, lhs, aug, weights, pot_rows, process):
    n16 = iota((16, BLK), 0)
    left = (n16 < 3).astype(bf16)
    right = ((n16 >= 3) & (n16 < 6)).astype(bf16)
    zero = jnp.zeros((DIM, BLK), bf16)

    @pl.loop(0, (chunks[0] + BODY - 1) // BODY)
    def _(turn):
        for k in range(BODY):
            n = BODY * turn + k
            p, base = chunks[1 + 2 * n], chunks[2 + 2 * n]
            safe = jnp.minimum(p, NBLK - 1)
            ids = slots(p, base)
            w = weights(safe)
            l16, r16 = left, right
            if pot_rows is not None:
                extra = pot_rows[safe]
                l16, r16 = left + extra, right + extra
            top = jnp.concatenate([w, zero], axis=1)
            mid = jnp.concatenate([zero, w], axis=1)
            low = jnp.concatenate([l16, r16], axis=1)
            rhs = jnp.concatenate([top, mid] + [low] * 8, axis=0)
            body = jnp.concatenate([lhs[jnp.minimum(q, NBLK - 1)] for q in ids], axis=0)
            tail = jnp.concatenate([aug[q] for q in ids], axis=0)
            both = jnp.concatenate([body, tail], axis=1)
            u = jnp.dot(both, rhs, preferred_element_type=f32)
            process(p, ids, u.reshape(CHUNK * HALF // 8, 8, 2 * BLK))


def max_process(peak, total):
    def process(p, ids, u):
        top = jnp.max(u, axis=0)
        top = jnp.maximum(top[:, :BLK], top[:, BLK:])
        old = peak[p]
        new = jnp.maximum(old, top)
        new2 = jnp.concatenate([new, new], axis=1)
        e = jnp.sum(jnp.exp2((u - new2[None]) * C2), axis=0)
        peak[p] = new
        total[p] = total[p] * jnp.exp2((old - new) * C2) + (e[:, :BLK] + e[:, BLK:])

    return process


def sum_process(total):
    def process(p, ids, u):
        e = jnp.sum(jnp.exp2(u * C2), axis=0)
        total[p] = total[p] + (e[:, :BLK] + e[:, BLK:])

    return process


def init_peaks(peak, total):
    peak[...] = jnp.full(peak.shape, LOW, f32)
    total[...] = jnp.zeros(total.shape, f32)


def finish_peaks(peak, total):
    m = peak[0:NBLK]
    top = jnp.max(m, axis=1)
    s = jnp.sum(total[0:NBLK] * jnp.exp2((m - top[:, None, :]) * C2), axis=1)
    return top + jnp.log2(s) * (1.0 / C2)


def finish_total(total):
    return jnp.sum(total[0:NBLK], axis=1)


def close_chunks(chunks, count):
    chunks[0] = count
    for k in range(BODY):
        chunks[1 + 2 * (count + k)] = NBLK
        chunks[2 + 2 * (count + k)] = 0


def row_chunks(bt, chunks):
    def step(p, n):
        for half in range(2):
            chunks[1 + 2 * (n + half)] = p
            chunks[2 + 2 * (n + half)] = p * SLOTS + half * CHUNK
        return n + 1 + (bt[p * SLOTS + CHUNK] >= 0).astype(jnp.int32)

    close_chunks(chunks, lax.fori_loop(0, NBLK, step, 0))


def row_slots(bt):
    def slots(p, base):
        ids = [bt[base + k] for k in range(CHUNK)]
        return [jnp.where((v >= 0) & (p < NBLK), v, NBLK) for v in ids]

    return slots


def col_chunks(lists, chunks):
    def step(t, n):
        many = (lists[NBLK * STRIDE + t] + CHUNK - 1) // CHUNK

        def put(c):
            chunks[1 + 2 * (n + c)] = t
            chunks[2 + 2 * (n + c)] = t * STRIDE + c * CHUNK

        put(0)
        put(1)

        @pl.when(many > 2)
        def _():
            pl.loop(2, many)(put)

        return n + many

    close_chunks(chunks, lax.fori_loop(0, NBLK, step, 0))


def col_slots(lists):
    def slots(p, base):
        size = jnp.where(p < NBLK, lists[NBLK * STRIDE + p], 0)
        first = base - p * STRIDE
        return [jnp.where(first + k < size, lists[base + k], NBLK) for k in range(CHUNK)]

    return slots


def x_weights(xt):
    return lambda p: xt[:, pl.ds(pl.multiple_of(p * BLK, BLK), BLK)]


def row1_kernel(bt, b, yfold, xt, peak, total, lists, chunks, cchunks, aug):
    fold_potential(b, aug)
    init_peaks(peak, total)
    for t in range(NBLK + 1):
        lists[NBLK * STRIDE + t] = 0
    row_chunks(bt, chunks)
    work = max_process(peak, total)

    def process(p, ids, u):
        for v in ids:
            real = v < NBLK
            have = jnp.where(real, lists[NBLK * STRIDE + v], 0)
            lists[jnp.where(real, v * STRIDE + have, NBLK * STRIDE + NBLK + 1)] = p
            lists[NBLK * STRIDE + v] = have + 1
        work(p, ids, u)

    sweep(chunks, row_slots(bt), yfold, aug, x_weights(xt), None, process)
    lists[NBLK * STRIDE + NBLK] = 0
    col_chunks(lists, cchunks)


def col1_kernel(lists, chunks, a, xfold, yt, peak, total, aug):
    fold_potential(a, aug)
    init_peaks(peak, total)
    sweep(chunks, col_slots(lists), xfold, aug, lambda t: yt[t], None, max_process(peak, total))


def row2_kernel(bt, chunks, a, b, yfold, xt, total, aug, rows):
    fold_potential(b, aug)
    spread_rows(a, rows)
    total[...] = jnp.zeros(total.shape, f32)
    sweep(chunks, row_slots(bt), yfold, aug, x_weights(xt), rows, sum_process(total))


def col2_kernel(lists, chunks, a, b, xfold, yt, xsq, total, f_out, aug, rows):
    fold_potential(a, aug)
    spread_rows(b, rows)
    total[...] = jnp.zeros(total.shape, f32)
    f_out[...] = a[...] * (1.0 / 32) + xsq[...] * (1.0 / 64)
    sweep(chunks, col_slots(lists), xfold, aug, lambda t: yt[t], rows, sum_process(total))


AUG = pltpu.VMEM((NBLK + 1, HALF, BLK), bf16)
ROWS = pltpu.VMEM((NBLK, 16, BLK), bf16)
ACC = jax.ShapeDtypeStruct((NBLK + 1, 8, BLK), f32)
LISTS = jax.ShapeDtypeStruct((NBLK * STRIDE + 128,), jnp.int32)
CHUNKS = jax.ShapeDtypeStruct((512,), jnp.int32)


def work_call(kernel, ins, outs, out_specs, scratch, *args):
    return pl.pallas_call(
        kernel,
        out_shape=outs,
        in_specs=ins,
        out_specs=out_specs,
        scratch_shapes=scratch,
        compiler_params=params(),
    )(*args)


def duals(n=NBLK):
    return jax.ShapeDtypeStruct((n, BLK), f32)


def place():
    i = lax.axis_index("src")
    core, z, y = lax.rem(i, 2), lax.rem(i // 2, NZ), i // (2 * NZ)
    return y, z, core


def at(y, z, core):
    return {"src": (y * NZ + z) * 2 + core}


def hail(devices):
    barrier = pltpu.get_barrier_semaphore()
    for d in devices:
        pl.semaphore_signal(barrier, inc=1, device_id=d, device_id_type=MESH)


def meet(devices):
    pl.semaphore_wait(pltpu.get_barrier_semaphore(), len(devices))


def send(src, dst, sends, recvs, k, device):
    copy = pltpu.make_async_remote_copy(
        src_ref=src, dst_ref=dst, send_sem=sends.at[k], recv_sem=recvs.at[k],
        device_id=device, device_id_type=MESH,
    )
    copy.start()
    return copy


def slot_of(dz):
    return 2 * dz - 1 if 0 < dz <= 4 else 2 * (NZ - dz) if dz else 0


GROUPS = ((0, 1), (1, 2), (3, 2), (5, 3))


def gather_kernel(own, xt, yt, yfold, b0, xfold, xsq, held, zs, zr, ys, yr, cs, cr):
    y, z, core = place()
    pick = picker()
    z_devices = {k: at(y, lax.rem(z + k, NZ), core) for k in range(1, NZ)}
    y_devices = {k: at(lax.rem(y + k, NY), z, core) for k in range(1, NY)}
    mate = at(y, z, 1 - core)
    everyone = list(z_devices.values()) + list(y_devices.values()) + [mate]
    hail(everyone)
    held[0, 0, 0] = own[...]
    meet(everyone)

    z_copies = {}
    for k in (4, 3, 5, 2, 6, 1, 7):
        z_copies[k] = send(own, held.at[0, 0, slot_of(NZ - k)], zs, zr, k - 1, z_devices[k])
    y_copies = {}

    def on_y(g):
        first, size = GROUPS[g]
        for k in (2, 1, 3):
            part = held.at[0, 0, pl.ds(first, size)]
            dst = held.at[0, NY - k, pl.ds(first, size)]
            y_copies[k, g] = send(part, dst, ys, yr, 4 * (k - 1) + g, y_devices[k])

    c_copies = []

    def on_mate(dy, first, size):
        part = held.at[0, dy, pl.ds(first, size)]
        dst = held.at[1, dy, pl.ds(first, size)]
        c_copies.append(send(part, dst, cs, cr, len(c_copies), mate))

    def fold_x(first, count):
        @pl.loop(first, first + count, step=4)
        def _(p):
            for i in range(4):
                tile = xt[:, pl.ds(pl.multiple_of((p + i) * BLK, BLK), BLK)]
                xfold[p + i] = fold(pick, tile)
                wide = tile.astype(f32)
                xsq[pl.ds(p + i, 1), :] = jnp.sum(wide * wide, axis=0, keepdims=True)

    def take(side, dy, first, count):
        @pl.loop(first, first + count)
        def _(s):
            back = lax.rem(s, 2)
            dz = back * ((s + 1) // 2) + (1 - back) * (NZ - s // 2)
            who = core if side == 0 else 1 - core
            t = (lax.rem(y + dy, NY) * NZ + lax.rem(z + dz, NZ)) * 2 + who
            tile = held[side, dy, s]
            yt[t] = tile
            yfold[t] = fold(pick, tile)
            wide = tile.astype(f32)
            b0[pl.ds(t, 1), :] = -0.5 * jnp.sum(wide * wide, axis=0, keepdims=True)

    on_y(0)
    fold_x(0, 32)
    for g, ks in ((1, (1, 7)), (2, (2, 6)), (3, (3, 5, 4))):
        for k in ks:
            z_copies[k].wait_recv()
        on_y(g)
        if g < 3:
            fold_x(16 + 16 * g, 16)
    on_mate(0, 0, NZ)
    take(0, 0, 0, NZ)
    for k in (1, 3, 2):
        for g in range(3):
            y_copies[k, g].wait_recv()
        on_mate(NY - k, 0, 5)
        take(0, NY - k, 0, 5)
    for k in (1, 3, 2):
        y_copies[k, 3].wait_recv()
        on_mate(NY - k, 5, 3)
        take(0, NY - k, 5, 3)
    c_copies[0].wait_recv()
    take(1, 0, 0, NZ)
    for i, k in enumerate((1, 3, 2)):
        c_copies[1 + i].wait_recv()
        take(1, NY - k, 0, 5)
    for i, k in enumerate((1, 3, 2)):
        c_copies[4 + i].wait_recv()
        take(1, NY - k, 5, 3)
    for c in list(z_copies.values()) + list(y_copies.values()) + c_copies:
        c.wait_send()


def gather(own, xt):
    dma = pltpu.SemaphoreType.DMA
    blocks = jax.ShapeDtypeStruct((NBLK, DIM, BLK), bf16)
    return pl.pallas_call(
        gather_kernel,
        out_shape=(blocks, blocks, duals(), blocks, duals()),
        in_specs=[VMEM] * 2,
        out_specs=(VMEM,) * 5,
        scratch_shapes=[pltpu.VMEM((2, NY, NZ, DIM, BLK), bf16)]
        + [dma((7,)), dma((7,)), dma((12,)), dma((12,)), dma((7,)), dma((7,))],
        compiler_params=params(0),
    )(own, xt)


def tgt_exchange(finish, mine, got, sends, recvs):
    me = lax.axis_index("tgt")
    devices = [{"tgt": lax.rem(me + k, NX)} for k in (2, 1, 3)]
    hail(devices)
    mine[...] = finish()
    meet(devices)
    copies = [send(mine, got.at[me], sends, recvs, k, d) for k, d in enumerate(devices)]
    got[me] = mine[...]
    for c in copies:
        c.wait()


def tgt1_kernel(peak, total, a_ref, mine, got, sends, recvs):
    tgt_exchange(lambda: finish_peaks(peak, total), mine, got, sends, recvs)
    a_ref[...] = -lse([got[k] for k in range(NX)]) - LOG_NS


def tgt2_kernel(total, old, a_ref, mine, got, sends, recvs):
    tgt_exchange(lambda: finish_total(total), mine, got, sends, recvs)
    s = (got[0] + got[1]) + (got[2] + got[3])
    a_ref[...] = old[...] - jnp.log2(s * NS) * (1.0 / C2)


def tgt_call(kernel, collective_id, *args):
    dma = pltpu.SemaphoreType.DMA
    mine = pltpu.VMEM((NBLK, BLK), f32)
    return pl.pallas_call(
        kernel,
        out_shape=duals(),
        in_specs=[VMEM] * len(args),
        out_specs=VMEM,
        scratch_shapes=[mine, pltpu.VMEM((NX, NBLK, BLK), f32), dma((3,)), dma((3,))],
        compiler_params=params(collective_id),
    )(*args)


def lse(parts):
    top = functools.reduce(jnp.maximum, parts)
    s = sum(jnp.exp2((v - top) * C2) for v in parts)
    return top + jnp.log2(s) * (1.0 / C2)


def mates():
    y, z, core = place()
    m = y * 2 + core

    def side(k):
        other = lax.rem(m + k, 8)
        return other, at(other // 2, z, lax.rem(other, 2))

    def up(k):
        other = lax.rem(z + k, NZ)
        return other, at(y, other, core)

    return m, z, [side(k) for k in range(1, 8)], [up(k) for k in (4, 3, 5, 2, 6, 1, 7)]


def rows_of(k):
    return pl.ds((k // 2) * 2 * NZ + k % 2, NZ, stride=2)


def scatter_sides(finish, combine, m, sides, ups, mine, order, r1, sends, recvs):
    devices = [d for _, d in ups + sides]
    hail(devices)
    mine[...] = finish()
    for k in range(8):
        order[k] = mine[rows_of(k), :]
    meet(devices)
    copies = [send(order.at[o], r1.at[m], sends, recvs, k, d) for k, (o, d) in enumerate(sides)]
    r1[m] = order[m]
    for c in copies:
        c.wait()
    return combine([r1[k] for k in range(8)])


def src1_kernel(peak, total, b_ref, own_ref, mine, order, r1, tile, r2, done, r4, s1, q1, s2, q2, s3, q3):
    m, z, sides, ups = mates()
    tile[...] = scatter_sides(
        lambda: finish_peaks(peak, total), lse, m, sides, ups, mine, order, r1, s1, q1
    )
    copies = [send(tile, r2.at[z], s2, q2, k, d) for k, (_, d) in enumerate(ups)]
    r2[z] = tile[...]
    for c in copies:
        c.wait()
    done[...] = -lse([r2[k] for k in range(8)]) - LOG_NT
    copies = [send(done, r4.at[m], s3, q3, k, d) for k, (_, d) in enumerate(sides)]
    r4[m] = done[...]
    own_ref[...] = jnp.broadcast_to(done[pl.ds(z, 1), :], (8, BLK))
    for c in copies:
        c.wait()
    for k in range(8):
        b_ref[rows_of(k), :] = r4[k]


def src2_kernel(total, old, yt_ref, g_ref, mine, order, r1, rows, r2, s1, q1, s2, q2):
    m, z, sides, ups = mates()
    first = scatter_sides(
        lambda: finish_total(total), sum, m, sides, ups, mine, order, r1, s1, q1
    )
    for k in range(8):
        rows[k] = jnp.broadcast_to(first[k : k + 1], (8, BLK))
    copies = [send(rows.at[o], r2.at[z], s2, q2, k, d) for k, (o, d) in enumerate(ups)]
    r2[z] = rows[z]
    y = yt_ref[...].astype(f32)
    sq = jnp.sum(y * y, axis=0, keepdims=True)
    for c in copies:
        c.wait()
    s = sum([r2[k] for k in range(8)])
    b = old[...] - jnp.log2(s * NT) * (1.0 / C2)
    g_ref[...] = b * (1.0 / 32) + sq * (1.0 / 64)


def src_call(kernel, collective_id, outs, scratch, phases, *args):
    mine = pltpu.VMEM((NBLK, BLK), f32)
    return pl.pallas_call(
        kernel,
        out_shape=outs,
        in_specs=[VMEM] * len(args),
        out_specs=jax.tree.map(lambda _: VMEM, outs),
        scratch_shapes=[mine] + scratch + [pltpu.SemaphoreType.DMA((7,))] * (2 * phases),
        compiler_params=params(collective_id),
    )(*args)


def local(source_features, target_features, block_targets):
    xt = source_features.T
    own_yt = target_features[0].T
    bt = block_targets.reshape(-1)
    block, tile = pltpu.VMEM((8, 8, BLK), f32), pltpu.VMEM((8, BLK), f32)

    yt, yfold, b0, xfold, xsq = gather(own_yt, xt)
    peak, total, lists, chunks, cchunks = work_call(
        row1_kernel, [SMEM, VMEM, VMEM, VMEM], (ACC, ACC, LISTS, CHUNKS, CHUNKS),
        (VMEM, VMEM, SMEM, SMEM, SMEM), [AUG], bt, b0, yfold, xt,
    )
    a = tgt_call(tgt1_kernel, 1, peak, total)
    peak, total = work_call(
        col1_kernel, [SMEM, SMEM, VMEM, VMEM, VMEM], (ACC, ACC), (VMEM, VMEM), [AUG],
        lists, cchunks, a, xfold, yt,
    )
    b, own = src_call(
        src1_kernel, 2, (duals(), duals(8)), [block, block, tile, block, tile, block], 3,
        peak, total,
    )
    total = work_call(
        row2_kernel, [SMEM, SMEM, VMEM, VMEM, VMEM, VMEM], ACC, VMEM, [AUG, ROWS],
        bt, chunks, a, b, yfold, xt,
    )
    a = tgt_call(tgt2_kernel, 3, total, a)
    total, f = work_call(
        col2_kernel, [SMEM, SMEM] + [VMEM] * 5, (ACC, duals()), (VMEM, VMEM), [AUG, ROWS],
        lists, cchunks, a, b, xfold, yt, xsq,
    )
    g = src_call(src2_kernel, 4, duals(8), [block] * 4, 2, total, own, own_yt)
    return f.reshape(-1), g[0:1]


def solution(mesh):
    in_specs = (P("src", None), P("tgt", "src", None), P("src", "tgt", None))
    out_specs = (P("src"), P("tgt", "src"))
    return jax.shard_map(local, mesh=mesh, in_specs=in_specs, out_specs=out_specs, check_vma=False)
```

time: 1050 us -> 107 us (0.10)
  waiting for transfers between devices: 385 us -> 0 us
  local copies, waits for them, and re-layouts: 254 us -> 3.23 us
  other arithmetic: 194 us -> 0 us
  matrix products: 140 us -> 0 us
  Pallas kernels: 0 us -> 103 us
  blocking collectives: 47.7 us -> 0 us
  between operations: 14 us -> 0.7 us
    all_gather x5 -> x0, waiting for transfers between devices: 383 us -> none  [the longest x4 309 us: joined(): everything = jax.tree.map(lambda part: lax.all_gather(part, axis), array)]
    reduce_sum x96 -> x0, other arithmetic: 175 us -> none  [the longest x32 87.8 us: tile_costs(): target_sq = jnp.sum(target_f * target_f, axis=-1)]
    dot_general x32 -> x0, matrix products: 140 us -> none  [tile_costs(): jnp.einsum('gid,gkjd->gkij', source_tile, target_tiles, preferred_element...]
    dynamic_slice x126 -> x0, local copies, waits for them, and re-layouts: 136 us -> none  [turn(): return combine(so_far, jax.tree.map(lambda part: part[k], everything))]
    pallas_call x0 -> x9, Pallas kernels: none -> 103 us  [the longest x4 33 us: work_call(): pl.pallas_call(kernel, out_shape=outs, in_specs=ins, out_specs=out_specs,...]
    gather x50 -> x0, local copies, waits for them, and re-layouts: 81.6 us -> none  [the longest x16 34.7 us: row_one_group(): costs = tile_costs(source_tile, target_tiles[index_tile])]
    pmax x2 -> x0, blocking collectives: 26.1 us -> none  [local(): row_peak = lax.pmax(as_sent(row_peaks), 'tgt').astype(row_peaks.dtype)]
    psum x2 -> x0, blocking collectives: 21.6 us -> none  [local(): lax.psum((row_totals * jnp.exp(row_peaks - row_peak)).astype(jnp.bfloat16...]
  transfers between devices with their start and end apart: 5 -> 0, of which waited for: 5 -> 0; matrix products, arithmetic and copies ran while one was open for 1% -> 0% of each run, Pallas kernels for 0% -> 0%
where the time goes in v2:
time: 107 us
  Pallas kernels  103 us (96%)
  local copies, waits for them, and re-layouts  3.23 us (3%)
    pallas_call x4, Pallas kernels, work_call(): pl.pallas_call(kernel, out_shape=outs, in_specs=ins, out_specs=out_specs,...  33 us
    pallas_call x2, Pallas kernels, src_call(): pl.pallas_call(kernel, out_shape=outs, in_specs=[VMEM] * len(args), out_s...  30.7 us
    pallas_call x1, Pallas kernels, gather(): pl.pallas_call(gather_kernel, out_shape=(blocks, blocks, duals(), blocks,...  25.7 us
    pallas_call x2, Pallas kernels, tgt_call(): pl.pallas_call(kernel, out_shape=duals(), in_specs=[VMEM] * len(args), ou...  13.7 us
    unnamed x7, local copies, waits for them, and re-layouts  2.63 us

profile of v2, /device:TPU:1, one launch (start us, length us, event | category | flops | bytes accessed | tf_op | source)
XLA Modules:
  0.0 107.0 jit_solution(1545526993544082056)
XLA Ops:
  0.6 0.8 copy.5
  1.4 0.0 copy-start.2
  1.4 0.1 reshape.10.bt
  1.5 0.6 copy-done.2
  2.1 0.0 copy-start
  2.1 1.2 %copy-done = bf16[8192,64]{0,1:T(8,128)(2,1)S(1)} copy-done((bf16[8192,64]{0,1:T(8,128)(2,1)S(1)}, bf16[8192,64]{0,1:T(8,128)(2,1)}, u32[]{:S(2)}) %copy-start) | copy-done | bytes 1048600
  3.3 0.0 copy-start.1
  3.3 25.7 %shard_map.50 = (bf16[64,64,128]{2,1,0:T(8,128)(2,1)S(1)}, bf16[64,64,128]{2,1,0:T(8,128)(2,1)S(1)}, f32[64,128]{1,0:T(8,128)S(1)}, bf16[64,64,128]{2,1,0:T(8,128)(2,1)S(1)}, f32[64,128]{1,0:T(8,128)S(1)}) custom-call(bf16[64,128]{1,0:T(8,128)(2,1)S(1)} %bitcast.10, bf16[64,8192]{1,0:T(8,128)(2,1)S(1)} %bitcast.7), custom_call_target="tpu_custom_call" | custom-call | tf_op jit(solution)/shard_map/pallas_call | solution.py:405
  29.0 0.0 copy-done.1
  29.1 12.0 %shard_map.51 = (f32[65,8,128]{2,1,0:T(8,128)S(1)}, f32[65,8,128]{2,1,0:T(8,128)S(1)}, s32[4480]{0:T(1024)S(1)}, s32[512]{0:T(512)S(1)}, s32[512]{0:T(512)S(1)}) custom-call(s32[512]{0:T(512)S(1)} %reshape.10.bt, f32[64,128]{1,0:T(8,128)S(1)} %get-tuple-element.18.b, bf16[64,64,128]{2,1,0:T(8,128)(2,1)S(1)} %get-tuple-element.19.yfold, ...), custom_call_target="tpu_custom_call" | custom-call | tf_op jit(solution)/shard_map/pallas_call | solution.py:269
  41.1 6.5 %shard_map.52.a.old = f32[64,128]{1,0:T(8,128)S(1)} custom-call(f32[65,8,128]{2,1,0:T(8,128)S(1)} %get-tuple-element.23.peak, f32[65,8,128]{2,1,0:T(8,128)S(1)} %get-tuple-element.24.total), custom_call_target="tpu_custom_call" | custom-call | tf_op jit(solution)/shard_map/pallas_call | solution.py:442
  47.6 9.2 %shard_map.53 = (f32[65,8,128]{2,1,0:T(8,128)S(1)}, f32[65,8,128]{2,1,0:T(8,128)S(1)}) custom-call(s32[4480]{0:T(1024)S(1)} %get-tuple-element.20.lists, s32[512]{0:T(512)S(1)} %get-tuple-element.21.chunks, f32[64,128]{1,0:T(8,128)S(1)} %shard_map.52.a.old, bf16[64,64,128]{2,1,0:T(8,128)(2,1)S(1)} %get-tuple-element.25.xfold, ...), custom_call_target="tpu_custom_call" | custom-call | tf_op jit(solution)/shard_map/pallas_call | solution.py:269
  56.8 19.4 %shard_map.54 = (f32[64,128]{1,0:T(8,128)S(1)}, f32[8,128]{1,0:T(8,128)S(1)}) custom-call(f32[65,8,128]{2,1,0:T(8,128)S(1)} %get-tuple-element.27.peak, f32[65,8,128]{2,1,0:T(8,128)S(1)} %get-tuple-element.28.total), custom_call_target="tpu_custom_call" | custom-call | tf_op jit(solution)/shard_map/pallas_call | solution.py:530
  76.2 5.5 %shard_map.55.total = f32[65,8,128]{2,1,0:T(8,128)S(1)} custom-call(s32[512]{0:T(512)S(1)} %reshape.10.bt, s32[512]{0:T(512)S(1)} %get-tuple-element.22.chunks, f32[64,128]{1,0:T(8,128)S(1)} %shard_map.52.a.old, f32[64,128]{1,0:T(8,128)S(1)} %get-tuple-element.29.b, bf16[64,64,128]{2,1,0:T(8,128)(2,1)S(1)} %get-tuple-element.19.yfold, ...), custom_call_target="tpu_custom_call" | custom-call | tf_op jit(solution)/shard_map/pallas_call | solution.py:269
  81.7 7.2 %shard_map.56.a = f32[64,128]{1,0:T(8,128)S(1)} custom-call(f32[65,8,128]{2,1,0:T(8,128)S(1)} %shard_map.55.total, f32[64,128]{1,0:T(8,128)S(1)} %shard_map.52.a.old), custom_call_target="tpu_custom_call" | custom-call | tf_op jit(solution)/shard_map/pallas_call | solution.py:442
  88.9 6.3 %shard_map.57 = (f32[65,8,128]{2,1,0:T(8,128)S(1)}, f32[64,128]{1,0:T(8,128)}) custom-call(s32[4480]{0:T(1024)S(1)} %get-tuple-element.20.lists, s32[512]{0:T(512)S(1)} %get-tuple-element.21.chunks, f32[64,128]{1,0:T(8,128)S(1)} %shard_map.56.a, f32[64,128]{1,0:T(8,128)S(1)} %get-tuple-element.29.b, bf16[64,64,128]{2,1,0:T(8,128)(2,1)S(1)} %get-tuple-element.25.xfold, ...), custom_call_target="tpu_custom_call" | custom-call | tf_op jit(solution)/shard_map/pallas_call | solution.py:269
  95.2 11.3 %shard_map.58 = f32[8,128]{1,0:T(8,128)S(1)} custom-call(f32[65,8,128]{2,1,0:T(8,128)S(1)} %get-tuple-element.32.total, f32[8,128]{1,0:T(8,128)S(1)} %get-tuple-element.33.old, bf16[64,128]{1,0:T(8,128)(2,1)S(1)} %bitcast.11), custom_call_target="tpu_custom_call" | custom-call | tf_op jit(solution)/shard_map/pallas_call | solution.py:530
  106.5 0.5 slice.3
Async XLA Ops:
  1.4 0.7 copy-start.2
  2.1 1.2 %copy-start = (bf16[8192,64]{0,1:T(8,128)(2,1)S(1)}, bf16[8192,64]{0,1:T(8,128)(2,1)}, u32[]{:S(2)}) copy-start(bf16[8192,64]{0,1:T(8,128)(2,1)} %param.3) | copy-start | bytes 3145732
  3.3 25.7 %copy-start.1 = (bf16[8192,64]{0,1:T(8,128)(2,1)S(1)}, bf16[8192,64]{0,1:T(8,128)(2,1)}, u32[]{:S(2)}) copy-start(bf16[8192,64]{0,1:T(8,128)(2,1)} %param.3) | copy-start | bytes 3145732

commit v3 on v2

v3 whole, which is shorter than its diff:
```python
import functools
import math

import jax
import jax.numpy as jnp
from jax import lax
from jax.experimental import pallas as pl
from jax.experimental.pallas import tpu as pltpu
from jax.sharding import PartitionSpec as P

BLK = 128
DIM = 64
HALF = BLK // 2
NBLK = 64
SLOTS = 8
CHUNK = 2
LANES = 384
EPSILON = 0.01
NS = 524288
NT = 32768
NY, NZ, NX = 4, 8, 4
RATE = 2.0 / (DIM * EPSILON)
C2 = RATE / math.log(2.0)
LOG_NS = math.log(NS) / RATE
LOG_NT = math.log(NT) / RATE
LOW = -1.0e30
BODY = 48
MESH = pl.DeviceIdType.MESH
VMEM = pl.BlockSpec(memory_space=pltpu.VMEM)
SMEM = pl.BlockSpec(memory_space=pltpu.SMEM)
f32, bf16 = jnp.float32, jnp.bfloat16


def iota(shape, dim):
    return lax.broadcasted_iota(jnp.int32, shape, dim)


def pieces(v):
    hi = v.astype(bf16).astype(f32)
    rest = v - hi
    mid = rest.astype(bf16).astype(f32)
    return hi, mid, rest - mid


def params(collective_id=None):
    if collective_id is None:
        return pltpu.CompilerParams(vmem_limit_bytes=40 << 20)
    return pltpu.CompilerParams(
        vmem_limit_bytes=40 << 20, collective_id=collective_id, has_side_effects=True
    )


def picker():
    return (iota((HALF, BLK), 1) % HALF == iota((HALF, BLK), 0)).astype(bf16)


def turn_over(pick, rows):
    return lax.dot_general(pick, rows, (((1,), (1,)), ((), ())), preferred_element_type=f32)


def fold(pick, tile):
    low = (iota((DIM, BLK), 1) < HALF).astype(bf16)
    rows = jnp.concatenate([tile * low, tile * (1.0 - low).astype(bf16)], axis=0)
    return turn_over(pick, rows).astype(bf16)


def fold_potential(pot, aug):
    lane = iota((HALF, BLK), 1)
    pick = picker()
    n = iota((8, 16, BLK), 1)
    h = iota((8, 16, BLK), 2) // HALF
    keep = ((n < 6) & (n // 3 == h)) | ((n >= 6) & (n < 9) & (h == 0))
    for g in range(8):
        hi, mid, lo = (v[:, None, :] for v in pieces(pot[8 * g : 8 * g + 8, :]))
        rows = jnp.where(
            n >= 6, 1.0, jnp.where(n % 3 == 0, hi, jnp.where(n % 3 == 1, mid, lo))
        )
        rows = jnp.where(keep, rows, 0.0).reshape(BLK, BLK).astype(bf16)
        turned = turn_over(pick, rows)
        for k in range(8):
            aug[8 * g + k] = jnp.where(lane // 16 == k, turned, 0.0).astype(bf16)
    n = iota((HALF, BLK), 1)
    aug[NBLK] = jnp.where((n == 0) | (n == 3), LOW, 0.0).astype(bf16)


def spread_rows(pot, rows):
    n = iota((8, 16, BLK), 1)
    for g in range(8):
        hi, mid, lo = (v[:, None, :] for v in pieces(pot[8 * g : 8 * g + 8, :]))
        v = jnp.where(n == 6, hi, jnp.where(n == 7, mid, jnp.where(n == 8, lo, 0.0)))
        rows[8 * g : 8 * g + 8] = v.astype(bf16)


def chunk_table(member):
    dot = functools.partial(jnp.dot, preferred_element_type=f32)
    m = member.astype(bf16)
    up = (iota((NBLK, NBLK), 0) < iota((NBLK, NBLK), 1)).astype(bf16)
    upto = (iota((NBLK, NBLK), 0) >= iota((NBLK, NBLK), 1)).astype(bf16)
    eye = (iota((NBLK, NBLK), 0) == iota((NBLK, NBLK), 1)).astype(bf16)
    place_of = (member * (dot(m, up) + 1.0)).astype(bf16)
    turned = turn_over(eye, place_of).astype(bf16)
    size = dot(m, jnp.ones((NBLK, LANES), bf16))
    many = jnp.floor((size + (CHUNK - 1.0)) * (1.0 / CHUNK))
    end = dot(upto, many.astype(bf16))
    row = iota((NBLK, LANES), 0).astype(f32)
    n = iota((NBLK, LANES), 1).astype(f32)
    before = (end <= n).astype(f32)
    p = jnp.sum(before, axis=0, keepdims=True)
    first = CHUNK * (n[:1] - jnp.sum(before * many, axis=0, keepdims=True))
    mine = dot(turned, (row == p).astype(bf16))
    rows = [
        NBLK + jnp.sum((row - NBLK) * (mine == first + (k + 1.0)).astype(f32), axis=0, keepdims=True)
        for k in range(CHUNK)
    ]
    rows += [p, end[NBLK - 1 :]] + [jnp.zeros((1, LANES), f32)] * (6 - CHUNK)
    return jnp.concatenate(rows, axis=0).astype(jnp.int32)


def sweep(table, lhs, aug, weights, pot_rows, process):
    n16 = iota((16, BLK), 0)
    left = (n16 < 3).astype(bf16)
    right = ((n16 >= 3) & (n16 < 6)).astype(bf16)
    zero = jnp.zeros((DIM, BLK), bf16)

    @pl.loop(0, (table[3, 0] + BODY - 1) // BODY)
    def _(turn):
        for k in range(BODY):
            n = BODY * turn + k
            p = table[2, n]
            safe = jnp.minimum(p, NBLK - 1)
            ids = [table[i, n] for i in range(CHUNK)]
            w = weights(safe)
            l16, r16 = left, right
            if pot_rows is not None:
                extra = pot_rows[safe]
                l16, r16 = left + extra, right + extra
            top = jnp.concatenate([w, zero], axis=1)
            mid = jnp.concatenate([zero, w], axis=1)
            low = jnp.concatenate([l16, r16], axis=1)
            rhs = jnp.concatenate([top, mid] + [low] * 8, axis=0)
            body = jnp.concatenate([lhs[jnp.minimum(q, NBLK - 1)] for q in ids], axis=0)
            tail = jnp.concatenate([aug[q] for q in ids], axis=0)
            both = jnp.concatenate([body, tail], axis=1)
            process(p, jnp.dot(both, rhs, preferred_element_type=f32))


def max_process(peak, total):
    def process(p, v):
        old, sums = peak[p], total[p]
        for k in range(CHUNK):
            u = v[k * HALF : (k + 1) * HALF].reshape(HALF // 8, 8, 2 * BLK)
            top = jnp.max(u, axis=0)
            new = jnp.maximum(old, jnp.maximum(top[:, :BLK], top[:, BLK:]))
            new2 = jnp.concatenate([new, new], axis=1)
            e = jnp.sum(jnp.exp2((u - new2[None]) * C2), axis=0)
            sums = sums * jnp.exp2((old - new) * C2) + (e[:, :BLK] + e[:, BLK:])
            old = new
        peak[p] = old
        total[p] = sums

    return process


def sum_process(total):
    def process(p, v):
        u = v.reshape(CHUNK * HALF // 8, 8, 2 * BLK)
        e = jnp.sum(jnp.exp2(u * C2), axis=0)
        total[p] = total[p] + (e[:, :BLK] + e[:, BLK:])

    return process


def init_peaks(peak, total):
    peak[...] = jnp.full(peak.shape, LOW, f32)
    total[...] = jnp.zeros(total.shape, f32)


def finish_peaks(peak, total):
    m = peak[0:NBLK]
    top = jnp.max(m, axis=1)
    s = jnp.sum(total[0:NBLK] * jnp.exp2((m - top[:, None, :]) * C2), axis=1)
    return top + jnp.log2(s) * (1.0 / C2)


def finish_total(total):
    return jnp.sum(total[0:NBLK], axis=1)


def x_weights(xt):
    return lambda p: xt[:, pl.ds(pl.multiple_of(p * BLK, BLK), BLK)]


def row1_kernel(table, b, yfold, xt, peak, total, aug):
    fold_potential(b, aug)
    init_peaks(peak, total)
    sweep(table, yfold, aug, x_weights(xt), None, max_process(peak, total))


def col1_kernel(table, a, xfold, yt, peak, total, aug):
    fold_potential(a, aug)
    init_peaks(peak, total)
    sweep(table, xfold, aug, lambda t: yt[t], None, max_process(peak, total))


def row2_kernel(table, rows, b, yfold, xt, total, aug):
    fold_potential(b, aug)
    total[...] = jnp.zeros(total.shape, f32)
    sweep(table, yfold, aug, x_weights(xt), rows, sum_process(total))


def col2_kernel(table, rows, a, xfold, yt, xsq, total, f_out, aug):
    fold_potential(a, aug)
    total[...] = jnp.zeros(total.shape, f32)
    f_out[...] = a[...] * (1.0 / 32) + xsq[...] * (1.0 / 64)
    sweep(table, xfold, aug, lambda t: yt[t], rows, sum_process(total))


AUG = pltpu.VMEM((NBLK + 1, HALF, BLK), bf16)
ROWS = jax.ShapeDtypeStruct((NBLK, 16, BLK), bf16)
ACC = jax.ShapeDtypeStruct((NBLK + 1, 8, BLK), f32)
TABLE = jax.ShapeDtypeStruct((8, LANES), jnp.int32)


def work_call(kernel, outs, *args):
    return pl.pallas_call(
        kernel,
        out_shape=outs,
        in_specs=[SMEM] + [VMEM] * (len(args) - 1),
        out_specs=jax.tree.map(lambda _: VMEM, outs),
        scratch_shapes=[AUG],
        compiler_params=params(),
    )(*args)


def duals(n=NBLK):
    return jax.ShapeDtypeStruct((n, BLK), f32)


def place():
    i = lax.axis_index("src")
    core, z, y = lax.rem(i, 2), lax.rem(i // 2, NZ), i // (2 * NZ)
    return y, z, core


def at(y, z, core):
    return {"src": (y * NZ + z) * 2 + core}


def hail(devices):
    barrier = pltpu.get_barrier_semaphore()
    for d in devices:
        pl.semaphore_signal(barrier, inc=1, device_id=d, device_id_type=MESH)


def meet(devices):
    pl.semaphore_wait(pltpu.get_barrier_semaphore(), len(devices))


def send(src, dst, sends, recvs, k, device):
    copy = pltpu.make_async_remote_copy(
        src_ref=src, dst_ref=dst, send_sem=sends.at[k], recv_sem=recvs.at[k],
        device_id=device, device_id_type=MESH,
    )
    copy.start()
    return copy


def slot_of(dz):
    return 2 * dz - 1 if 0 < dz <= 4 else 2 * (NZ - dz) if dz else 0


GROUPS = ((0, 1), (1, 2), (3, 2), (5, 3))


def gather_kernel(own, bt, yt, yfold, b0, row_table, col_table, held, zs, zr, ys, yr, cs, cr):
    y, z, core = place()
    pick = picker()
    z_devices = {k: at(y, lax.rem(z + k, NZ), core) for k in (4, 3, 5, 2, 6, 1, 7)}
    y_devices = {k: at(lax.rem(y + k, NY), z, core) for k in (2, 1, 3)}
    mate = at(y, z, 1 - core)
    everyone = list(z_devices.values()) + list(y_devices.values()) + [mate]
    hail(everyone)
    held[0, 0, 0] = own[...]
    meet(everyone)

    z_copies = {}
    for k, d in z_devices.items():
        z_copies[k] = send(own, held.at[0, 0, slot_of(NZ - k)], zs, zr, k - 1, d)
    y_copies = {}

    def on_y(g):
        first, size = GROUPS[g]
        for k, d in y_devices.items():
            part = held.at[0, 0, pl.ds(first, size)]
            dst = held.at[0, NY - k, pl.ds(first, size)]
            y_copies[k, g] = send(part, dst, ys, yr, 4 * (k - 1) + g, d)

    c_copies = []

    def on_mate(dy, dys, first, size):
        part = held.at[0, pl.ds(dy, dys), pl.ds(first, size)]
        dst = held.at[1, pl.ds(dy, dys), pl.ds(first, size)]
        c_copies.append(send(part, dst, cs, cr, len(c_copies), mate))

    def take(side, dy, s):
        back = lax.rem(s, 2)
        dz = back * ((s + 1) // 2) + (1 - back) * (NZ - s // 2)
        who = core if side == 0 else 1 - core
        t = (lax.rem(y + dy, NY) * NZ + lax.rem(z + dz, NZ)) * 2 + who
        tile = held[side, dy, s]
        yt[t] = tile
        yfold[t] = fold(pick, tile)
        wide = tile.astype(f32)
        b0[pl.ds(t, 1), :] = -0.5 * jnp.sum(wide * wide, axis=0, keepdims=True)

    def take_column(side):
        @pl.loop(0, NZ, step=4)
        def _(s):
            for i in range(4):
                take(side, 0, s + i)

    def take_group(side, g):
        @pl.loop(GROUPS[g][0], GROUPS[g][0] + GROUPS[g][1])
        def _(s):
            for dy in range(1, NY):
                take(side, dy, s)

    on_y(0)
    t = iota((NBLK, NBLK), 0)
    member = sum((bt[k : k + 1, :] == t).astype(f32) for k in range(SLOTS))
    col_table[...] = chunk_table(member)
    eye = (iota((NBLK, NBLK), 1) == t).astype(bf16)
    row_table[...] = chunk_table(turn_over(eye, member.astype(bf16)))
    for g, ks in ((1, (1, 7)), (2, (2, 6)), (3, (3, 5, 4))):
        for k in ks:
            z_copies[k].wait_recv()
        on_y(g)
    on_mate(0, 1, 0, NZ)
    for g in range(4):
        for k in (1, 3, 2):
            y_copies[k, g].wait_recv()
        on_mate(1, NY - 1, *GROUPS[g])
        if g == 0:
            take_column(0)
        take_group(0, g)
    c_copies[0].wait_recv()
    take_column(1)
    for g in range(4):
        c_copies[1 + g].wait_recv()
        take_group(1, g)
    for c in list(z_copies.values()) + list(y_copies.values()) + c_copies:
        c.wait_send()


def gather(own, bt):
    dma = pltpu.SemaphoreType.DMA
    blocks = jax.ShapeDtypeStruct((NBLK, DIM, BLK), bf16)
    return pl.pallas_call(
        gather_kernel,
        out_shape=(blocks, blocks, duals(), TABLE, TABLE),
        in_specs=[VMEM] * 2,
        out_specs=(VMEM,) * 5,
        scratch_shapes=[pltpu.VMEM((2, NY, NZ, DIM, BLK), bf16)]
        + [dma((7,)), dma((7,)), dma((12,)), dma((12,)), dma((5,)), dma((5,))],
        compiler_params=params(0),
    )(own, bt)


def tgt_exchange(finish, meanwhile, mine, got, sends, recvs):
    me = lax.axis_index("tgt")
    devices = [{"tgt": lax.rem(me + k, NX)} for k in (2, 1, 3)]
    hail(devices)
    mine[...] = finish()
    meet(devices)
    copies = [send(mine, got.at[me], sends, recvs, k, d) for k, d in enumerate(devices)]
    got[me] = mine[...]
    meanwhile()
    for c in copies:
        c.wait()


def tgt1_kernel(peak, total, xt, a_ref, xfold, xsq, mine, got, sends, recvs):
    pick = picker()

    def fold_x():
        @pl.loop(0, NBLK, step=8)
        def _(p):
            for i in range(8):
                tile = xt[:, pl.ds(pl.multiple_of((p + i) * BLK, BLK), BLK)]
                xfold[p + i] = fold(pick, tile)
                wide = tile.astype(f32)
                xsq[pl.ds(p + i, 1), :] = jnp.sum(wide * wide, axis=0, keepdims=True)

    tgt_exchange(lambda: finish_peaks(peak, total), fold_x, mine, got, sends, recvs)
    a_ref[...] = -lse([got[k] for k in range(NX)]) - LOG_NS


def tgt2_kernel(total, old, b_ref, a_ref, rows, mine, got, sends, recvs):
    tgt_exchange(
        lambda: finish_total(total), lambda: spread_rows(b_ref, rows), mine, got, sends, recvs
    )
    s = (got[0] + got[1]) + (got[2] + got[3])
    a_ref[...] = old[...] - jnp.log2(s * NS) * (1.0 / C2)


def tgt_call(kernel, collective_id, outs, *args):
    dma = pltpu.SemaphoreType.DMA
    mine = pltpu.VMEM((NBLK, BLK), f32)
    return pl.pallas_call(
        kernel,
        out_shape=outs,
        in_specs=[VMEM] * len(args),
        out_specs=jax.tree.map(lambda _: VMEM, outs),
        scratch_shapes=[mine, pltpu.VMEM((NX, NBLK, BLK), f32), dma((3,)), dma((3,))],
        compiler_params=params(collective_id),
    )(*args)


def lse(parts):
    top = functools.reduce(jnp.maximum, parts)
    s = sum(jnp.exp2((v - top) * C2) for v in parts)
    return top + jnp.log2(s) * (1.0 / C2)


def mates():
    y, z, core = place()
    m = y * 2 + core

    def side(k):
        other = lax.rem(m + k, 8)
        return other, at(other // 2, z, lax.rem(other, 2))

    def up(k):
        other = lax.rem(z + k, NZ)
        return other, at(y, other, core)

    return m, z, [side(k) for k in range(1, 8)], [up(k) for k in (4, 3, 5, 2, 6, 1, 7)]


def rows_of(k):
    return pl.ds((k // 2) * 2 * NZ + k % 2, NZ, stride=2)


def scatter_sides(finish, combine, m, sides, ups, mine, order, r1, sends, recvs):
    devices = [d for _, d in ups + sides]
    hail(devices)
    mine[...] = finish()
    for k in range(8):
        order[k] = mine[rows_of(k), :]
    meet(devices)
    copies = [send(order.at[o], r1.at[m], sends, recvs, k, d) for k, (o, d) in enumerate(sides)]
    r1[m] = order[m]
    for c in copies:
        c.wait()
    return combine([r1[k] for k in range(8)])


def src1_kernel(peak, total, a_ref, b_ref, own_ref, spread, mine, order, r1, tile, r2, done, r4, s1, q1, s2, q2, s3, q3):
    m, z, sides, ups = mates()
    tile[...] = scatter_sides(
        lambda: finish_peaks(peak, total), lse, m, sides, ups, mine, order, r1, s1, q1
    )
    copies = [send(tile, r2.at[z], s2, q2, k, d) for k, (_, d) in enumerate(ups)]
    r2[z] = tile[...]
    spread_rows(a_ref, spread)
    for c in copies:
        c.wait()
    done[...] = -lse([r2[k] for k in range(8)]) - LOG_NT
    copies = [send(done, r4.at[m], s3, q3, k, d) for k, (_, d) in enumerate(sides)]
    r4[m] = done[...]
    own_ref[...] = jnp.broadcast_to(done[pl.ds(z, 1), :], (8, BLK))
    for c in copies:
        c.wait()
    for k in range(8):
        b_ref[rows_of(k), :] = r4[k]


def src2_kernel(total, old, yt_ref, g_ref, mine, order, r1, rows, r2, s1, q1, s2, q2):
    m, z, sides, ups = mates()
    first = scatter_sides(
        lambda: finish_total(total), sum, m, sides, ups, mine, order, r1, s1, q1
    )
    for k in range(8):
        rows[k] = jnp.broadcast_to(first[k : k + 1], (8, BLK))
    copies = [send(rows.at[o], r2.at[z], s2, q2, k, d) for k, (o, d) in enumerate(ups)]
    r2[z] = rows[z]
    y = yt_ref[...].astype(f32)
    sq = jnp.sum(y * y, axis=0, keepdims=True)
    for c in copies:
        c.wait()
    s = sum([r2[k] for k in range(8)])
    b = old[...] - jnp.log2(s * NT) * (1.0 / C2)
    g_ref[...] = b * (1.0 / 32) + sq * (1.0 / 64)


def src_call(kernel, collective_id, outs, scratch, phases, *args):
    mine = pltpu.VMEM((NBLK, BLK), f32)
    return pl.pallas_call(
        kernel,
        out_shape=outs,
        in_specs=[VMEM] * len(args),
        out_specs=jax.tree.map(lambda _: VMEM, outs),
        scratch_shapes=[mine] + scratch + [pltpu.SemaphoreType.DMA((7,))] * (2 * phases),
        compiler_params=params(collective_id),
    )(*args)


def local(source_features, target_features, block_targets):
    own_yt = target_features[0].T
    block, tile = pltpu.VMEM((8, 8, BLK), f32), pltpu.VMEM((8, BLK), f32)

    xt = source_features.T
    blocks = jax.ShapeDtypeStruct((NBLK, DIM, BLK), bf16)
    yt, yfold, b0, row_table, col_table = gather(own_yt, block_targets[:, 0, :].T)
    peak, total = work_call(row1_kernel, (ACC, ACC), row_table, b0, yfold, xt)
    a, xfold, xsq = tgt_call(tgt1_kernel, 1, (duals(), blocks, duals()), peak, total, xt)
    peak, total = work_call(col1_kernel, (ACC, ACC), col_table, a, xfold, yt)
    b, own, rows = src_call(
        src1_kernel, 2, (duals(), duals(8), ROWS), [block, block, tile, block, tile, block], 3,
        peak, total, a,
    )
    total = work_call(row2_kernel, ACC, row_table, rows, b, yfold, xt)
    a, rows = tgt_call(tgt2_kernel, 3, (duals(), ROWS), total, a, b)
    total, f = work_call(col2_kernel, (ACC, duals()), col_table, rows, a, xfold, yt, xsq)
    g = src_call(src2_kernel, 4, duals(8), [block] * 4, 2, total, own, own_yt)
    return f.reshape(-1), g[0:1]


def solution(mesh):
    in_specs = (P("src", None), P("tgt", "src", None), P("src", "tgt", None))
    out_specs = (P("src"), P("tgt", "src"))
    return jax.shard_map(local, mesh=mesh, in_specs=in_specs, out_specs=out_specs, check_vma=False)
```

time: 107 us -> 92 us (0.86)
  Pallas kernels: 103 us -> 87.9 us
    pallas_call x7, Pallas kernels: 72.4 us -> 58.8 us  [the longest x4 26.4 us: work_call(): pl.pallas_call(kernel, out_shape=outs, in_specs=[SMEM] + [VMEM] * (len(ar...]
    pallas_call x2, Pallas kernels: 30.7 us -> 29.2 us  [src_call(): pl.pallas_call(kernel, out_shape=outs, in_specs=[VMEM] * len(args), out_s...]
    unnamed x7 -> x10, local copies, waits for them, and re-layouts: 2.63 us -> 2.63 us
where the time goes in v3:
time: 92 us; the launch traced here: 91.8 us
  Pallas kernels  87.9 us (96%)
  local copies, waits for them, and re-layouts  3.14 us (3%)
    pallas_call x2, Pallas kernels, src_call(): pl.pallas_call(kernel, out_shape=outs, in_specs=[VMEM] * len(args), out_s...  29.2 us
    pallas_call x4, Pallas kernels, work_call(): pl.pallas_call(kernel, out_shape=outs, in_specs=[SMEM] + [VMEM] * (len(ar...  26.4 us
    pallas_call x1, Pallas kernels, gather(): pl.pallas_call(gather_kernel, out_shape=(blocks, blocks, duals(), TABLE,...  22.2 us
    pallas_call x2, Pallas kernels, tgt_call(): pl.pallas_call(kernel, out_shape=outs, in_specs=[VMEM] * len(args), out_s...  10.2 us
    unnamed x10, local copies, waits for them, and re-layouts  2.63 us

profile of v3, /device:TPU:1, one launch (start us, length us, event | category | flops | bytes accessed | tf_op | source)
XLA Modules:
  0.0 91.8 jit_solution(4684654311477137574)
XLA Ops:
  0.6 0.0 copy-start.4
  0.6 0.7 copy-done.4
  1.3 0.0 copy-start.2
  1.3 0.7 copy-done.2
  2.0 22.2 %shard_map.50 = (bf16[64,64,128]{2,1,0:T(8,128)(2,1)S(1)}, bf16[64,64,128]{2,1,0:T(8,128)(2,1)S(1)}, f32[64,128]{1,0:T(8,128)S(1)}, s32[8,384]{1,0:T(8,128)S(1)}, s32[8,384]{1,0:T(8,128)S(1)}) custom-call(bf16[64,128]{1,0:T(8,128)(2,1)S(1)} %bitcast.11, s32[8,64]{1,0:T(8,128)S(1)} %bitcast.13), custom_call_target="tpu_custom_call" | custom-call | tf_op jit(solution)/shard_map/pallas_call | solution.py:358
  24.2 0.0 copy-start
  24.3 1.2 %copy-done = bf16[8192,64]{0,1:T(8,128)(2,1)S(1)} copy-done((bf16[8192,64]{0,1:T(8,128)(2,1)S(1)}, bf16[8192,64]{0,1:T(8,128)(2,1)}, u32[]{:S(2)}) %copy-start) | copy-done | bytes 1048600
  25.5 0.0 copy-start.1
  25.5 7.6 %shard_map.51 = (f32[65,8,128]{2,1,0:T(8,128)S(1)}, f32[65,8,128]{2,1,0:T(8,128)S(1)}) custom-call(s32[8,384]{1,0:T(8,128)S(1)} %get-tuple-element.22.table, f32[64,128]{1,0:T(8,128)S(1)} %get-tuple-element.23.b, bf16[64,64,128]{2,1,0:T(8,128)(2,1)S(1)} %get-tuple-element.24.yfold, bf16[64,8192]{1,0:T(8,128)(2,1)S(1)} %bitcast.8), custom_call_target="tpu_custom_call" | custom-call | tf_op jit(solution)/shard_map/pallas_call | solution.py:225
  33.1 0.0 copy-done.1
  33.1 5.3 %shard_map.52 = (f32[64,128]{1,0:T(8,128)S(1)}, bf16[64,64,128]{2,1,0:T(8,128)(2,1)S(1)}, f32[64,128]{1,0:T(8,128)S(1)}) custom-call(f32[65,8,128]{2,1,0:T(8,128)S(1)} %get-tuple-element.25.peak, f32[65,8,128]{2,1,0:T(8,128)S(1)} %get-tuple-element.26.total, bf16[64,8192]{1,0:T(8,128)(2,1)S(1)} %bitcast.9), custom_call_target="tpu_custom_call" | custom-call | tf_op jit(solution)/shard_map/pallas_call | solution.py:409
  38.5 7.4 %shard_map.53 = (f32[65,8,128]{2,1,0:T(8,128)S(1)}, f32[65,8,128]{2,1,0:T(8,128)S(1)}) custom-call(s32[8,384]{1,0:T(8,128)S(1)} %get-tuple-element.21.table, f32[64,128]{1,0:T(8,128)S(1)} %get-tuple-element.27.a.a_ref.old, bf16[64,64,128]{2,1,0:T(8,128)(2,1)S(1)} %get-tuple-element.28.xfold, bf16[64,64,128]{2,1,0:T(8,128)(2,1)S(1)} %get-tuple-element.29.yt), custom_call_target="tpu_custom_call" | custom-call | tf_op jit(solution)/shard_map/pallas_call | solution.py:225
  45.9 17.8 %shard_map.54 = (f32[64,128]{1,0:T(8,128)S(1)}, f32[8,128]{1,0:T(8,128)S(1)}, bf16[64,16,128]{2,1,0:T(8,128)(2,1)S(1)}) custom-call(f32[65,8,128]{2,1,0:T(8,128)S(1)} %get-tuple-element.30.peak, f32[65,8,128]{2,1,0:T(8,128)S(1)} %get-tuple-element.31.total, f32[64,128]{1,0:T(8,128)S(1)} %get-tuple-element.27.a.a_ref.old), custom_call_target="tpu_custom_call" | custom-call | tf_op jit(solution)/shard_map/pallas_call | solution.py:498
  63.7 5.4 %shard_map.55.total = f32[65,8,128]{2,1,0:T(8,128)S(1)} custom-call(s32[8,384]{1,0:T(8,128)S(1)} %get-tuple-element.22.table, bf16[64,16,128]{2,1,0:T(8,128)(2,1)S(1)} %get-tuple-element.32.rows, f32[64,128]{1,0:T(8,128)S(1)} %get-tuple-element.33.b.b_ref, bf16[64,64,128]{2,1,0:T(8,128)(2,1)S(1)} %get-tuple-element.24.yfold, bf16[64,8192]{1,0:T(8,128)(2,1)S(1)} %bitcast.10), custom_call_target="tpu_custom_call" | custom-call | tf_op jit(solution)/shard_map/pallas_call | solution.py:225
  69.1 4.9 %shard_map.56 = (f32[64,128]{1,0:T(8,128)S(1)}, bf16[64,16,128]{2,1,0:T(8,128)(2,1)S(1)}) custom-call(f32[65,8,128]{2,1,0:T(8,128)S(1)} %shard_map.55.total, f32[64,128]{1,0:T(8,128)S(1)} %get-tuple-element.27.a.a_ref.old, f32[64,128]{1,0:T(8,128)S(1)} %get-tuple-element.33.b.b_ref), custom_call_target="tpu_custom_call" | custom-call | tf_op jit(solution)/shard_map/pallas_call | solution.py:409
  73.9 0.0 copy-start.3
  73.9 5.9 %shard_map.57 = (f32[65,8,128]{2,1,0:T(8,128)S(1)}, f32[64,128]{1,0:T(8,128)}) custom-call(s32[8,384]{1,0:T(8,128)S(1)} %get-tuple-element.21.table, bf16[64,16,128]{2,1,0:T(8,128)(2,1)S(1)} %get-tuple-element.34.rows, f32[64,128]{1,0:T(8,128)S(1)} %get-tuple-element.35.a, bf16[64,64,128]{2,1,0:T(8,128)(2,1)S(1)} %get-tuple-element.28.xfold, ...), custom_call_target="tpu_custom_call" | custom-call | tf_op jit(solution)/shard_map/pallas_call | solution.py:225
  79.9 0.0 copy-done.3
  79.9 11.4 %shard_map.58 = f32[8,128]{1,0:T(8,128)S(1)} custom-call(f32[65,8,128]{2,1,0:T(8,128)S(1)} %get-tuple-element.38.total, f32[8,128]{1,0:T(8,128)S(1)} %get-tuple-element.39.old, bf16[64,128]{1,0:T(8,128)(2,1)S(1)} %bitcast.12), custom_call_target="tpu_custom_call" | custom-call | tf_op jit(solution)/shard_map/pallas_call | solution.py:498
  91.3 0.5 slice.3
Async XLA Ops:
  0.6 0.7 copy-start.4
  1.3 0.7 copy-start.2
  24.2 1.2 %copy-start = (bf16[8192,64]{0,1:T(8,128)(2,1)S(1)}, bf16[8192,64]{0,1:T(8,128)(2,1)}, u32[]{:S(2)}) copy-start(bf16[8192,64]{0,1:T(8,128)(2,1)} %param.3) | copy-start | bytes 3145732
  25.5 7.6 %copy-start.1 = (bf16[8192,64]{0,1:T(8,128)(2,1)S(1)}, bf16[8192,64]{0,1:T(8,128)(2,1)}, u32[]{:S(2)}) copy-start(bf16[8192,64]{0,1:T(8,128)(2,1)} %param.3) | copy-start | bytes 3145732
  73.9 6.0 %copy-start.3 = (bf16[1,128,64]{1,2,0:T(8,128)(2,1)S(1)}, bf16[1,128,64]{1,2,0:T(8,128)(2,1)}, u32[]{:S(2)}) copy-start(bf16[1,128,64]{1,2,0:T(8,128)(2,1)} %param.4) | copy-start | bytes 49156

commit v4 on v3

--- a/solution.py
+++ b/solution.py
@@ -24,7 +24,7 @@
 LOG_NS = math.log(NS) / RATE
 LOG_NT = math.log(NT) / RATE
 LOW = -1.0e30
-BODY = 48
+BODY = 96
 MESH = pl.DeviceIdType.MESH
 VMEM = pl.BlockSpec(memory_space=pltpu.VMEM)
 SMEM = pl.BlockSpec(memory_space=pltpu.SMEM)
@@ -42,11 +42,11 @@
     return hi, mid, rest - mid
 
 
-def params(collective_id=None):
+def params(collective_id=None, limit=40):
     if collective_id is None:
-        return pltpu.CompilerParams(vmem_limit_bytes=40 << 20)
+        return pltpu.CompilerParams(vmem_limit_bytes=limit << 20)
     return pltpu.CompilerParams(
-        vmem_limit_bytes=40 << 20, collective_id=collective_id, has_side_effects=True
+        vmem_limit_bytes=limit << 20, collective_id=collective_id, has_side_effects=True
     )
 
 
@@ -208,11 +208,14 @@
     sweep(table, yfold, aug, x_weights(xt), rows, sum_process(total))
 
 
-def col2_kernel(table, rows, a, xfold, yt, xsq, total, f_out, aug):
+def col2_kernel(table, rows, a, xfold, yt, xsq, total, f_out, aug, f, sem):
+    f[...] = a[...] * (1.0 / 32) + xsq[...] * (1.0 / 64)
+    leave = pltpu.make_async_copy(f, f_out, sem.at[0])
+    leave.start()
     fold_potential(a, aug)
     total[...] = jnp.zeros(total.shape, f32)
-    f_out[...] = a[...] * (1.0 / 32) + xsq[...] * (1.0 / 64)
     sweep(table, xfold, aug, lambda t: yt[t], rows, sum_process(total))
+    leave.wait()
 
 
 AUG = pltpu.VMEM((NBLK + 1, HALF, BLK), bf16)
@@ -221,13 +224,13 @@
 TABLE = jax.ShapeDtypeStruct((8, LANES), jnp.int32)
 
 
-def work_call(kernel, outs, *args):
+def work_call(kernel, outs, *args, out_specs=None, scratch=()):
     return pl.pallas_call(
         kernel,
         out_shape=outs,
         in_specs=[SMEM] + [VMEM] * (len(args) - 1),
-        out_specs=jax.tree.map(lambda _: VMEM, outs),
-        scratch_shapes=[AUG],
+        out_specs=out_specs or jax.tree.map(lambda _: VMEM, outs),
+        scratch_shapes=[AUG, *scratch],
         compiler_params=params(),
     )(*args)
 
@@ -272,20 +275,29 @@
 GROUPS = ((0, 1), (1, 2), (3, 2), (5, 3))
 
 
-def gather_kernel(own, bt, yt, yfold, b0, row_table, col_table, held, zs, zr, ys, yr, cs, cr):
+def gather_kernel(
+    own, bt_far, xt_far, yt, yfold, b0, row_table, col_table, xt, held, bt, ls, zs, zr, ys, yr, cs, cr
+):
     y, z, core = place()
     pick = picker()
     z_devices = {k: at(y, lax.rem(z + k, NZ), core) for k in (4, 3, 5, 2, 6, 1, 7)}
     y_devices = {k: at(lax.rem(y + k, NY), z, core) for k in (2, 1, 3)}
     mate = at(y, z, 1 - core)
     everyone = list(z_devices.values()) + list(y_devices.values()) + [mate]
+    mine = held.at[0, 0, 0]
     hail(everyone)
-    held[0, 0, 0] = own[...]
+    here = [
+        pltpu.make_async_copy(src, dst, ls.at[k])
+        for k, (src, dst) in enumerate(((own, mine), (bt_far, bt), (xt_far, xt)))
+    ]
+    for c in here:
+        c.start()
+    here[0].wait()
     meet(everyone)
 
     z_copies = {}
     for k, d in z_devices.items():
-        z_copies[k] = send(own, held.at[0, 0, slot_of(NZ - k)], zs, zr, k - 1, d)
+        z_copies[k] = send(mine, held.at[0, 0, slot_of(NZ - k)], zs, zr, k - 1, d)
     y_copies = {}
 
     def on_y(g):
@@ -326,6 +338,8 @@
                 take(side, dy, s)
 
     on_y(0)
+    here[1].wait()
+    here[2].wait()
     t = iota((NBLK, NBLK), 0)
     member = sum((bt[k : k + 1, :] == t).astype(f32) for k in range(SLOTS))
     col_table[...] = chunk_table(member)
@@ -343,27 +357,46 @@
         if g == 0:
             take_column(0)
         take_group(0, g)
-    c_copies[0].wait_recv()
-    take_column(1)
-    for g in range(4):
+        if g == 1:
+            c_copies[0].wait_recv()
+            take_column(1)
+        if g == 2:
+            c_copies[1].wait_recv()
+            take_group(1, 0)
+    for g in range(1, 4):
         c_copies[1 + g].wait_recv()
         take_group(1, g)
     for c in list(z_copies.values()) + list(y_copies.values()) + c_copies:
         c.wait_send()
 
 
-def gather(own, bt):
+def gather(own, bt, xt):
     dma = pltpu.SemaphoreType.DMA
     blocks = jax.ShapeDtypeStruct((NBLK, DIM, BLK), bf16)
     return pl.pallas_call(
         gather_kernel,
-        out_shape=(blocks, blocks, duals(), TABLE, TABLE),
-        in_specs=[VMEM] * 2,
-        out_specs=(VMEM,) * 5,
-        scratch_shapes=[pltpu.VMEM((2, NY, NZ, DIM, BLK), bf16)]
-        + [dma((7,)), dma((7,)), dma((12,)), dma((12,)), dma((5,)), dma((5,))],
-        compiler_params=params(0),
-    )(own, bt)
+        out_shape=(blocks, blocks, duals(), TABLE, TABLE, jax.ShapeDtypeStruct(xt.shape, bf16)),
+        in_specs=[pl.BlockSpec(memory_space=pl.ANY)] * 3,
+        out_specs=(VMEM,) * 6,
+        scratch_shapes=[pltpu.VMEM((2, NY, NZ, DIM, BLK), bf16), pltpu.VMEM(bt.shape, jnp.int32)]
+        + [dma((3,)), dma((7,)), dma((7,)), dma((12,)), dma((12,)), dma((5,)), dma((5,))],
+        compiler_params=params(0, 50),
+    )(own, bt, xt)
+
+
+def spread(pairs, device_of, sends, recvs):
+    for k, (src, dst) in enumerate(pairs):
+        pltpu.make_async_remote_copy(
+            src_ref=src, dst_ref=dst, send_sem=sends.at[0], recv_sem=recvs.at[0],
+            device_id=device_of[k], device_id_type=MESH,
+        ).start()
+
+
+def collect(many, device, sends, recvs):
+    pltpu.make_async_remote_copy(
+        src_ref=many, dst_ref=many, send_sem=sends.at[0], recv_sem=recvs.at[0],
+        device_id=device, device_id_type=MESH,
+    ).wait()
 
 
 def tgt_exchange(finish, meanwhile, mine, got, sends, recvs):
@@ -372,11 +405,10 @@
     hail(devices)
     mine[...] = finish()
     meet(devices)
-    copies = [send(mine, got.at[me], sends, recvs, k, d) for k, d in enumerate(devices)]
+    spread([(mine, got.at[me])] * 3, devices, sends, recvs)
     got[me] = mine[...]
     meanwhile()
-    for c in copies:
-        c.wait()
+    collect(got.at[pl.ds(0, 3)], devices[0], sends, recvs)
 
 
 def tgt1_kernel(peak, total, xt, a_ref, xfold, xsq, mine, got, sends, recvs):
@@ -411,7 +443,7 @@
         out_shape=outs,
         in_specs=[VMEM] * len(args),
         out_specs=jax.tree.map(lambda _: VMEM, outs),
-        scratch_shapes=[mine, pltpu.VMEM((NX, NBLK, BLK), f32), dma((3,)), dma((3,))],
+        scratch_shapes=[mine, pltpu.VMEM((NX, NBLK, BLK), f32), dma((1,)), dma((1,))],
         compiler_params=params(collective_id),
     )(*args)
 
@@ -448,29 +480,26 @@
     for k in range(8):
         order[k] = mine[rows_of(k), :]
     meet(devices)
-    copies = [send(order.at[o], r1.at[m], sends, recvs, k, d) for k, (o, d) in enumerate(sides)]
+    spread([(order.at[o], r1.at[m]) for o, _ in sides], [d for _, d in sides], sends, recvs)
     r1[m] = order[m]
-    for c in copies:
-        c.wait()
+    collect(r1.at[pl.ds(0, 7)], sides[0][1], sends, recvs)
     return combine([r1[k] for k in range(8)])
 
 
-def src1_kernel(peak, total, a_ref, b_ref, own_ref, spread, mine, order, r1, tile, r2, done, r4, s1, q1, s2, q2, s3, q3):
+def src1_kernel(peak, total, a_ref, b_ref, own_ref, a_rows, mine, order, r1, tile, r2, done, r4, s1, q1, s2, q2, s3, q3):
     m, z, sides, ups = mates()
     tile[...] = scatter_sides(
         lambda: finish_peaks(peak, total), lse, m, sides, ups, mine, order, r1, s1, q1
     )
-    copies = [send(tile, r2.at[z], s2, q2, k, d) for k, (_, d) in enumerate(ups)]
+    spread([(tile, r2.at[z])] * 7, [d for _, d in ups], s2, q2)
     r2[z] = tile[...]
-    spread_rows(a_ref, spread)
-    for c in copies:
-        c.wait()
+    spread_rows(a_ref, a_rows)
+    collect(r2.at[pl.ds(0, 7)], ups[0][1], s2, q2)
     done[...] = -lse([r2[k] for k in range(8)]) - LOG_NT
-    copies = [send(done, r4.at[m], s3, q3, k, d) for k, (_, d) in enumerate(sides)]
+    spread([(done, r4.at[m])] * 7, [d for _, d in sides], s3, q3)
     r4[m] = done[...]
     own_ref[...] = jnp.broadcast_to(done[pl.ds(z, 1), :], (8, BLK))
-    for c in copies:
-        c.wait()
+    collect(r4.at[pl.ds(0, 7)], sides[0][1], s3, q3)
     for k in range(8):
         b_ref[rows_of(k), :] = r4[k]
 
@@ -482,12 +511,11 @@
     )
     for k in range(8):
         rows[k] = jnp.broadcast_to(first[k : k + 1], (8, BLK))
-    copies = [send(rows.at[o], r2.at[z], s2, q2, k, d) for k, (o, d) in enumerate(ups)]
+    spread([(rows.at[o], r2.at[z]) for o, _ in ups], [d for _, d in ups], s2, q2)
     r2[z] = rows[z]
     y = yt_ref[...].astype(f32)
     sq = jnp.sum(y * y, axis=0, keepdims=True)
-    for c in copies:
-        c.wait()
+    collect(r2.at[pl.ds(0, 7)], ups[0][1], s2, q2)
     s = sum([r2[k] for k in range(8)])
     b = old[...] - jnp.log2(s * NT) * (1.0 / C2)
     g_ref[...] = b * (1.0 / 32) + sq * (1.0 / 64)
@@ -500,7 +528,7 @@
         out_shape=outs,
         in_specs=[VMEM] * len(args),
         out_specs=jax.tree.map(lambda _: VMEM, outs),
-        scratch_shapes=[mine] + scratch + [pltpu.SemaphoreType.DMA((7,))] * (2 * phases),
+        scratch_shapes=[mine] + scratch + [pltpu.SemaphoreType.DMA((1,))] * (2 * phases),
         compiler_params=params(collective_id),
     )(*args)
 
@@ -509,9 +537,10 @@
     own_yt = target_features[0].T
     block, tile = pltpu.VMEM((8, 8, BLK), f32), pltpu.VMEM((8, BLK), f32)
 
-    xt = source_features.T
     blocks = jax.ShapeDtypeStruct((NBLK, DIM, BLK), bf16)
-    yt, yfold, b0, row_table, col_table = gather(own_yt, block_targets[:, 0, :].T)
+    yt, yfold, b0, row_table, col_table, xt = gather(
+        own_yt, block_targets[:, 0, :].T, source_features.T
+    )
     peak, total = work_call(row1_kernel, (ACC, ACC), row_table, b0, yfold, xt)
     a, xfold, xsq = tgt_call(tgt1_kernel, 1, (duals(), blocks, duals()), peak, total, xt)
     peak, total = work_call(col1_kernel, (ACC, ACC), col_table, a, xfold, yt)
@@ -521,7 +550,11 @@
     )
     total = work_call(row2_kernel, ACC, row_table, rows, b, yfold, xt)
     a, rows = tgt_call(tgt2_kernel, 3, (duals(), ROWS), total, a, b)
-    total, f = work_call(col2_kernel, (ACC, duals()), col_table, rows, a, xfold, yt, xsq)
+    total, f = work_call(
+        col2_kernel, (ACC, duals()), col_table, rows, a, xfold, yt, xsq,
+        out_specs=(VMEM, pl.BlockSpec(memory_space=pl.ANY)),
+        scratch=(pltpu.VMEM((NBLK, BLK), f32), pltpu.SemaphoreType.DMA((1,))),
+    )
     g = src_call(src2_kernel, 4, duals(8), [block] * 4, 2, total, own, own_yt)
     return f.reshape(-1), g[0:1]
 

time: 92 us -> 88.1 us (0.958)
  Pallas kernels: 87.9 us -> 85.3 us
  local copies, waits for them, and re-layouts: 3.14 us -> 1.91 us
    pallas_call x4, Pallas kernels: 26.4 us -> 24.8 us  [work_call(): pl.pallas_call(kernel, out_shape=outs, in_specs=[SMEM] + [VMEM] * (len(ar...]
    pallas_call x2, Pallas kernels: 29.2 us -> 27.9 us  [src_call(): pl.pallas_call(kernel, out_shape=outs, in_specs=[VMEM] * len(args), out_s...]
    unnamed x10 -> x4, local copies, waits for them, and re-layouts: 2.63 us -> 1.4 us
where the time goes in v4:
time: 88.1 us; the launch traced here: 87.9 us
  Pallas kernels  85.3 us (97%)
  local copies, waits for them, and re-layouts  1.91 us (2%)
    pallas_call x2, Pallas kernels, src_call(): pl.pallas_call(kernel, out_shape=outs, in_specs=[VMEM] * len(args), out_s...  27.9 us
    pallas_call x4, Pallas kernels, work_call(): pl.pallas_call(kernel, out_shape=outs, in_specs=[SMEM] + [VMEM] * (len(ar...  24.8 us
    pallas_call x1, Pallas kernels, gather(): pl.pallas_call(gather_kernel, out_shape=(blocks, blocks, duals(), TABLE,...  22.2 us
    pallas_call x2, Pallas kernels, tgt_call(): pl.pallas_call(kernel, out_shape=outs, in_specs=[VMEM] * len(args), out_s...  10.3 us

profile of v4, /device:TPU:1, one launch (start us, length us, event | category | flops | bytes accessed | tf_op | source)
XLA Modules:
  0.0 87.9 jit_solution(9787605472312819625)
XLA Ops:
  0.6 0.0 copy-start.1
  0.6 0.7 copy-done.1
  1.3 0.0 copy-start
  1.3 0.7 copy-done
  2.0 22.2 %shard_map.50 = (bf16[64,64,128]{2,1,0:T(8,128)(2,1)S(1)}, bf16[64,64,128]{2,1,0:T(8,128)(2,1)S(1)}, f32[64,128]{1,0:T(8,128)S(1)}, s32[8,384]{1,0:T(8,128)S(1)}...) custom-call(bf16[64,128]{1,0:T(8,128)(2,1)S(1)} %bitcast.8, s32[8,64]{1,0:T(8,128)S(1)} %bitcast.10, ...), custom_call_target="tpu_custom_call" | custom-call | tf_op jit(solution)/shard_map/pallas_call | solution.py:376
  24.3 7.3 %shard_map.51 = (f32[65,8,128]{2,1,0:T(8,128)S(1)}, f32[65,8,128]{2,1,0:T(8,128)S(1)}) custom-call(s32[8,384]{1,0:T(8,128)S(1)} %get-tuple-element.23.table, f32[64,128]{1,0:T(8,128)S(1)} %get-tuple-element.24.b, bf16[64,64,128]{2,1,0:T(8,128)(2,1)S(1)} %get-tuple-element.25.yfold, bf16[64,8192]{1,0:T(8,128)(2,1)S(1)} %get-tuple-element.26.xt), custom_call_target="tpu_custom_call" | custom-call | tf_op jit(solution)/shard_map/pallas_call | solution.py:228
  31.6 5.5 %shard_map.52 = (f32[64,128]{1,0:T(8,128)S(1)}, bf16[64,64,128]{2,1,0:T(8,128)(2,1)S(1)}, f32[64,128]{1,0:T(8,128)S(1)}) custom-call(f32[65,8,128]{2,1,0:T(8,128)S(1)} %get-tuple-element.27.peak, f32[65,8,128]{2,1,0:T(8,128)S(1)} %get-tuple-element.28.total, bf16[64,8192]{1,0:T(8,128)(2,1)S(1)} %get-tuple-element.26.xt), custom_call_target="tpu_custom_call" | custom-call | tf_op jit(solution)/shard_map/pallas_call | solution.py:441
  37.1 7.2 %shard_map.53 = (f32[65,8,128]{2,1,0:T(8,128)S(1)}, f32[65,8,128]{2,1,0:T(8,128)S(1)}) custom-call(s32[8,384]{1,0:T(8,128)S(1)} %get-tuple-element.22.table, f32[64,128]{1,0:T(8,128)S(1)} %get-tuple-element.29.a.a_ref.old, bf16[64,64,128]{2,1,0:T(8,128)(2,1)S(1)} %get-tuple-element.30.xfold, bf16[64,64,128]{2,1,0:T(8,128)(2,1)S(1)} %get-tuple-element.31.yt), custom_call_target="tpu_custom_call" | custom-call | tf_op jit(solution)/shard_map/pallas_call | solution.py:228
  44.3 16.7 %shard_map.54 = (f32[64,128]{1,0:T(8,128)S(1)}, f32[8,128]{1,0:T(8,128)S(1)}, bf16[64,16,128]{2,1,0:T(8,128)(2,1)S(1)}) custom-call(f32[65,8,128]{2,1,0:T(8,128)S(1)} %get-tuple-element.32.peak, f32[65,8,128]{2,1,0:T(8,128)S(1)} %get-tuple-element.33.total, f32[64,128]{1,0:T(8,128)S(1)} %get-tuple-element.29.a.a_ref.old), custom_call_target="tpu_custom_call" | custom-call | tf_op jit(solution)/shard_map/pallas_call | solution.py:526
  61.0 5.2 %shard_map.55.total = f32[65,8,128]{2,1,0:T(8,128)S(1)} custom-call(s32[8,384]{1,0:T(8,128)S(1)} %get-tuple-element.23.table, bf16[64,16,128]{2,1,0:T(8,128)(2,1)S(1)} %get-tuple-element.34.rows, f32[64,128]{1,0:T(8,128)S(1)} %get-tuple-element.35.b.b_ref, bf16[64,64,128]{2,1,0:T(8,128)(2,1)S(1)} %get-tuple-element.25.yfold, ...), custom_call_target="tpu_custom_call" | custom-call | tf_op jit(solution)/shard_map/pallas_call | solution.py:228
  66.3 4.9 %shard_map.56 = (f32[64,128]{1,0:T(8,128)S(1)}, bf16[64,16,128]{2,1,0:T(8,128)(2,1)S(1)}) custom-call(f32[65,8,128]{2,1,0:T(8,128)S(1)} %shard_map.55.total, f32[64,128]{1,0:T(8,128)S(1)} %get-tuple-element.29.a.a_ref.old, f32[64,128]{1,0:T(8,128)S(1)} %get-tuple-element.35.b.b_ref), custom_call_target="tpu_custom_call" | custom-call | tf_op jit(solution)/shard_map/pallas_call | solution.py:441
  71.1 5.1 %shard_map.57 = (f32[65,8,128]{2,1,0:T(8,128)S(1)}, f32[64,128]{1,0:T(8,128)}) custom-call(s32[8,384]{1,0:T(8,128)S(1)} %get-tuple-element.22.table, bf16[64,16,128]{2,1,0:T(8,128)(2,1)S(1)} %get-tuple-element.36.rows, f32[64,128]{1,0:T(8,128)S(1)} %get-tuple-element.37.a, bf16[64,64,128]{2,1,0:T(8,128)(2,1)S(1)} %get-tuple-element.30.xfold, ...), custom_call_target="tpu_custom_call" | custom-call | tf_op jit(solution)/shard_map/pallas_call | solution.py:228
  76.2 11.2 %shard_map.58 = f32[8,128]{1,0:T(8,128)S(1)} custom-call(f32[65,8,128]{2,1,0:T(8,128)S(1)} %get-tuple-element.40.total, f32[8,128]{1,0:T(8,128)S(1)} %get-tuple-element.41.old, bf16[64,128]{1,0:T(8,128)(2,1)S(1)} %bitcast.9), custom_call_target="tpu_custom_call" | custom-call | tf_op jit(solution)/shard_map/pallas_call | solution.py:526
  87.4 0.5 slice.3
Async XLA Ops:
  0.6 0.7 copy-start.1
  1.3 0.7 copy-start

commit v5 on v4

--- a/solution.py
+++ b/solution.py
@@ -27,7 +27,6 @@
 BODY = 96
 MESH = pl.DeviceIdType.MESH
 VMEM = pl.BlockSpec(memory_space=pltpu.VMEM)
-SMEM = pl.BlockSpec(memory_space=pltpu.SMEM)
 f32, bf16 = jnp.float32, jnp.bfloat16
 
 
@@ -112,8 +111,8 @@
         NBLK + jnp.sum((row - NBLK) * (mine == first + (k + 1.0)).astype(f32), axis=0, keepdims=True)
         for k in range(CHUNK)
     ]
-    rows += [p, end[NBLK - 1 :]] + [jnp.zeros((1, LANES), f32)] * (6 - CHUNK)
-    return jnp.concatenate(rows, axis=0).astype(jnp.int32)
+    word = p + BLK * (rows[0] + BLK * rows[1])
+    return jnp.where(n[:1] == LANES - 1, end[NBLK - 1 :], word).astype(jnp.int32)
 
 
 def sweep(table, lhs, aug, weights, pot_rows, process):
@@ -122,13 +121,13 @@
     right = ((n16 >= 3) & (n16 < 6)).astype(bf16)
     zero = jnp.zeros((DIM, BLK), bf16)
 
-    @pl.loop(0, (table[3, 0] + BODY - 1) // BODY)
+    @pl.loop(0, (table[0, LANES - 1] + BODY - 1) // BODY)
     def _(turn):
         for k in range(BODY):
-            n = BODY * turn + k
-            p = table[2, n]
+            word = table[0, BODY * turn + k]
+            p = word & (BLK - 1)
             safe = jnp.minimum(p, NBLK - 1)
-            ids = [table[i, n] for i in range(CHUNK)]
+            ids = [(word >> 7) & (BLK - 1), word >> 14]
             w = weights(safe)
             l16, r16 = left, right
             if pot_rows is not None:
@@ -190,30 +189,44 @@
     return lambda p: xt[:, pl.ds(pl.multiple_of(p * BLK, BLK), BLK)]
 
 
-def row1_kernel(table, b, yfold, xt, peak, total, aug):
+def fetch(far, table, sem):
+    copy = pltpu.make_async_copy(far, table, sem.at[0])
+    copy.start()
+    return copy
+
+
+def row1_kernel(far, b, yfold, xt, peak, total, aug, table, sem):
+    listed = fetch(far, table, sem)
     fold_potential(b, aug)
     init_peaks(peak, total)
+    listed.wait()
     sweep(table, yfold, aug, x_weights(xt), None, max_process(peak, total))
 
 
-def col1_kernel(table, a, xfold, yt, peak, total, aug):
+def col1_kernel(far, a, xfold, yt, peak, total, aug, table, sem):
+    listed = fetch(far, table, sem)
     fold_potential(a, aug)
     init_peaks(peak, total)
+    listed.wait()
     sweep(table, xfold, aug, lambda t: yt[t], None, max_process(peak, total))
 
 
-def row2_kernel(table, rows, b, yfold, xt, total, aug):
+def row2_kernel(far, rows, b, yfold, xt, total, aug, table, sem):
+    listed = fetch(far, table, sem)
     fold_potential(b, aug)
     total[...] = jnp.zeros(total.shape, f32)
+    listed.wait()
     sweep(table, yfold, aug, x_weights(xt), rows, sum_process(total))
 
 
-def col2_kernel(table, rows, a, xfold, yt, xsq, total, f_out, aug, f, sem):
+def col2_kernel(far, rows, a, xfold, yt, xsq, total, f_out, aug, table, sem, f, f_sem):
+    listed = fetch(far, table, sem)
     f[...] = a[...] * (1.0 / 32) + xsq[...] * (1.0 / 64)
-    leave = pltpu.make_async_copy(f, f_out, sem.at[0])
+    leave = pltpu.make_async_copy(f, f_out, f_sem.at[0])
     leave.start()
     fold_potential(a, aug)
     total[...] = jnp.zeros(total.shape, f32)
+    listed.wait()
     sweep(table, xfold, aug, lambda t: yt[t], rows, sum_process(total))
     leave.wait()
 
@@ -221,16 +234,16 @@
 AUG = pltpu.VMEM((NBLK + 1, HALF, BLK), bf16)
 ROWS = jax.ShapeDtypeStruct((NBLK, 16, BLK), bf16)
 ACC = jax.ShapeDtypeStruct((NBLK + 1, 8, BLK), f32)
-TABLE = jax.ShapeDtypeStruct((8, LANES), jnp.int32)
+TABLE = jax.ShapeDtypeStruct((1, LANES), jnp.int32)
 
 
 def work_call(kernel, outs, *args, out_specs=None, scratch=()):
     return pl.pallas_call(
         kernel,
         out_shape=outs,
-        in_specs=[SMEM] + [VMEM] * (len(args) - 1),
+        in_specs=[VMEM] * len(args),
         out_specs=out_specs or jax.tree.map(lambda _: VMEM, outs),
-        scratch_shapes=[AUG, *scratch],
+        scratch_shapes=[AUG, pltpu.SMEM(TABLE.shape, TABLE.dtype), pltpu.SemaphoreType.DMA((1,)), *scratch],
         compiler_params=params(),
     )(*args)
 
@@ -276,7 +289,7 @@
 
 
 def gather_kernel(
-    own, bt_far, xt_far, yt, yfold, b0, row_table, col_table, xt, held, bt, ls, zs, zr, ys, yr, cs, cr
+    packed, xt_far, yt, yfold, b0, row_table, col_table, xt, held, ls, zs, zr, ys, yr, cs, cr
 ):
     y, z, core = place()
     pick = picker()
@@ -286,13 +299,9 @@
     everyone = list(z_devices.values()) + list(y_devices.values()) + [mate]
     mine = held.at[0, 0, 0]
     hail(everyone)
-    here = [
-        pltpu.make_async_copy(src, dst, ls.at[k])
-        for k, (src, dst) in enumerate(((own, mine), (bt_far, bt), (xt_far, xt)))
-    ]
-    for c in here:
-        c.start()
-    here[0].wait()
+    here = pltpu.make_async_copy(xt_far, xt, ls.at[0])
+    here.start()
+    mine[...] = packed[0:DIM, :]
     meet(everyone)
 
     z_copies = {}
@@ -338,10 +347,9 @@
                 take(side, dy, s)
 
     on_y(0)
-    here[1].wait()
-    here[2].wait()
     t = iota((NBLK, NBLK), 0)
-    member = sum((bt[k : k + 1, :] == t).astype(f32) for k in range(SLOTS))
+    bt = packed[DIM:, 0:NBLK].astype(f32)
+    member = sum((bt[k : k + 1, :] == t.astype(f32)).astype(f32) for k in range(SLOTS))
     col_table[...] = chunk_table(member)
     eye = (iota((NBLK, NBLK), 1) == t).astype(bf16)
     row_table[...] = chunk_table(turn_over(eye, member.astype(bf16)))
@@ -366,22 +374,23 @@
     for g in range(1, 4):
         c_copies[1 + g].wait_recv()
         take_group(1, g)
+    here.wait()
     for c in list(z_copies.values()) + list(y_copies.values()) + c_copies:
         c.wait_send()
 
 
-def gather(own, bt, xt):
+def gather(packed, xt):
     dma = pltpu.SemaphoreType.DMA
     blocks = jax.ShapeDtypeStruct((NBLK, DIM, BLK), bf16)
     return pl.pallas_call(
         gather_kernel,
         out_shape=(blocks, blocks, duals(), TABLE, TABLE, jax.ShapeDtypeStruct(xt.shape, bf16)),
-        in_specs=[pl.BlockSpec(memory_space=pl.ANY)] * 3,
+        in_specs=[VMEM, pl.BlockSpec(memory_space=pl.ANY)],
         out_specs=(VMEM,) * 6,
-        scratch_shapes=[pltpu.VMEM((2, NY, NZ, DIM, BLK), bf16), pltpu.VMEM(bt.shape, jnp.int32)]
-        + [dma((3,)), dma((7,)), dma((7,)), dma((12,)), dma((12,)), dma((5,)), dma((5,))],
+        scratch_shapes=[pltpu.VMEM((2, NY, NZ, DIM, BLK), bf16)]
+        + [dma((1,)), dma((7,)), dma((7,)), dma((12,)), dma((12,)), dma((5,)), dma((5,))],
         compiler_params=params(0, 50),
-    )(own, bt, xt)
+    )(packed, xt)
 
 
 def spread(pairs, device_of, sends, recvs):
@@ -403,7 +412,7 @@
     me = lax.axis_index("tgt")
     devices = [{"tgt": lax.rem(me + k, NX)} for k in (2, 1, 3)]
     hail(devices)
-    mine[...] = finish()
+    mine[...] = finish().astype(mine.dtype)
     meet(devices)
     spread([(mine, got.at[me])] * 3, devices, sends, recvs)
     got[me] = mine[...]
@@ -431,19 +440,20 @@
     tgt_exchange(
         lambda: finish_total(total), lambda: spread_rows(b_ref, rows), mine, got, sends, recvs
     )
-    s = (got[0] + got[1]) + (got[2] + got[3])
+    g0, g1, g2, g3 = (got[k].astype(f32) for k in range(NX))
+    s = (g0 + g1) + (g2 + g3)
     a_ref[...] = old[...] - jnp.log2(s * NS) * (1.0 / C2)
 
 
-def tgt_call(kernel, collective_id, outs, *args):
+def tgt_call(kernel, collective_id, kind, outs, *args):
     dma = pltpu.SemaphoreType.DMA
-    mine = pltpu.VMEM((NBLK, BLK), f32)
+    mine = pltpu.VMEM((NBLK, BLK), kind)
     return pl.pallas_call(
         kernel,
         out_shape=outs,
         in_specs=[VMEM] * len(args),
         out_specs=jax.tree.map(lambda _: VMEM, outs),
-        scratch_shapes=[mine, pltpu.VMEM((NX, NBLK, BLK), f32), dma((1,)), dma((1,))],
+        scratch_shapes=[mine, pltpu.VMEM((NX, NBLK, BLK), kind), dma((1,)), dma((1,))],
         compiler_params=params(collective_id),
     )(*args)
 
@@ -466,7 +476,8 @@
         other = lax.rem(z + k, NZ)
         return other, at(y, other, core)
 
-    return m, z, [side(k) for k in range(1, 8)], [up(k) for k in (4, 3, 5, 2, 6, 1, 7)]
+    far_first = (4, 3, 5, 2, 6, 1, 7)
+    return m, z, [side(k) for k in far_first], [up(k) for k in far_first]
 
 
 def rows_of(k):
@@ -538,18 +549,18 @@
     block, tile = pltpu.VMEM((8, 8, BLK), f32), pltpu.VMEM((8, BLK), f32)
 
     blocks = jax.ShapeDtypeStruct((NBLK, DIM, BLK), bf16)
-    yt, yfold, b0, row_table, col_table, xt = gather(
-        own_yt, block_targets[:, 0, :].T, source_features.T
-    )
+    listed = block_targets[:, 0, :].T.astype(bf16)
+    packed = jnp.concatenate([own_yt, jnp.pad(listed, ((0, 8), (0, BLK - NBLK)))], axis=0)
+    yt, yfold, b0, row_table, col_table, xt = gather(packed, source_features.T)
     peak, total = work_call(row1_kernel, (ACC, ACC), row_table, b0, yfold, xt)
-    a, xfold, xsq = tgt_call(tgt1_kernel, 1, (duals(), blocks, duals()), peak, total, xt)
+    a, xfold, xsq = tgt_call(tgt1_kernel, 1, f32, (duals(), blocks, duals()), peak, total, xt)
     peak, total = work_call(col1_kernel, (ACC, ACC), col_table, a, xfold, yt)
     b, own, rows = src_call(
         src1_kernel, 2, (duals(), duals(8), ROWS), [block, block, tile, block, tile, block], 3,
         peak, total, a,
     )
     total = work_call(row2_kernel, ACC, row_table, rows, b, yfold, xt)
-    a, rows = tgt_call(tgt2_kernel, 3, (duals(), ROWS), total, a, b)
+    a, rows = tgt_call(tgt2_kernel, 3, bf16, (duals(), ROWS), total, a, b)
     total, f = work_call(
         col2_kernel, (ACC, duals()), col_table, rows, a, xfold, yt, xsq,
         out_specs=(VMEM, pl.BlockSpec(memory_space=pl.ANY)),

time: 88.1 us -> 85.6 us (0.972)
  Pallas kernels: 85.3 us -> 82.8 us
  other arithmetic: 0 us -> 1.41 us
  local copies, waits for them, and re-layouts: 1.91 us -> 0.52 us
    pallas_call x4, Pallas kernels: 24.8 us -> 22.9 us  [work_call(): pl.pallas_call(kernel, out_shape=outs, in_specs=[VMEM] * len(args), out_s...]
    unnamed x4 -> x2, local copies, waits for them, and re-layouts: 1.4 us -> 0.01 us
where the time goes in v5:
time: 85.6 us; the launch traced here: 85.4 us
  Pallas kernels  82.8 us (97%)
  other arithmetic  1.41 us (2%)
    pallas_call x2, Pallas kernels, src_call(): pl.pallas_call(kernel, out_shape=outs, in_specs=[VMEM] * len(args), out_s...  27.7 us
    pallas_call x4, Pallas kernels, work_call(): pl.pallas_call(kernel, out_shape=outs, in_specs=[VMEM] * len(args), out_s...  22.9 us
    pallas_call x1, Pallas kernels, gather(): pl.pallas_call(gather_kernel, out_shape=(blocks, blocks, duals(), TABLE,...  22.3 us
    pallas_call x2, Pallas kernels, tgt_call(): pl.pallas_call(kernel, out_shape=outs, in_specs=[VMEM] * len(args), out_s...  9.96 us

profile of v5, /device:TPU:1, one launch (start us, length us, event | category | flops | bytes accessed | tf_op | source)
XLA Modules:
  0.0 85.4 jit_solution(15855085067458486219)
XLA Ops:
  0.6 0.7 convert_bitcast_fusion
  1.3 0.7 fusion.1.packed
  2.0 22.3 %shard_map.50 = (bf16[64,64,128]{2,1,0:T(8,128)(2,1)S(1)}, bf16[64,64,128]{2,1,0:T(8,128)(2,1)S(1)}, f32[64,128]{1,0:T(8,128)S(1)}, s32[1,384]{1,0:T(1,128)S(1)}...) custom-call(bf16[80,128]{1,0:T(8,128)(2,1)S(1)} %fusion.1.packed, bf16[64,8192]{1,0:T(8,128)(2,1)} %bitcast.11), custom_call_target="tpu_custom_call" | custom-call | tf_op jit(solution)/shard_map/pallas_call | solution.py:385
  24.3 6.8 %shard_map.51 = (f32[65,8,128]{2,1,0:T(8,128)S(1)}, f32[65,8,128]{2,1,0:T(8,128)S(1)}) custom-call(s32[1,384]{1,0:T(1,128)S(1)} %get-tuple-element.23.far, f32[64,128]{1,0:T(8,128)S(1)} %get-tuple-element.24.b, bf16[64,64,128]{2,1,0:T(8,128)(2,1)S(1)} %get-tuple-element.25.yfold, bf16[64,8192]{1,0:T(8,128)(2,1)S(1)} %get-tuple-element.26.xt), custom_call_target="tpu_custom_call" | custom-call | tf_op jit(solution)/shard_map/pallas_call | solution.py:241
  31.2 5.5 %shard_map.52 = (f32[64,128]{1,0:T(8,128)S(1)}, bf16[64,64,128]{2,1,0:T(8,128)(2,1)S(1)}, f32[64,128]{1,0:T(8,128)S(1)}) custom-call(f32[65,8,128]{2,1,0:T(8,128)S(1)} %get-tuple-element.27.peak, f32[65,8,128]{2,1,0:T(8,128)S(1)} %get-tuple-element.28.total, bf16[64,8192]{1,0:T(8,128)(2,1)S(1)} %get-tuple-element.26.xt), custom_call_target="tpu_custom_call" | custom-call | tf_op jit(solution)/shard_map/pallas_call | solution.py:451
  36.7 6.7 %shard_map.53 = (f32[65,8,128]{2,1,0:T(8,128)S(1)}, f32[65,8,128]{2,1,0:T(8,128)S(1)}) custom-call(s32[1,384]{1,0:T(1,128)S(1)} %get-tuple-element.22.far, f32[64,128]{1,0:T(8,128)S(1)} %get-tuple-element.29.a.a_ref.old, bf16[64,64,128]{2,1,0:T(8,128)(2,1)S(1)} %get-tuple-element.30.xfold, bf16[64,64,128]{2,1,0:T(8,128)(2,1)S(1)} %get-tuple-element.31.yt), custom_call_target="tpu_custom_call" | custom-call | tf_op jit(solution)/shard_map/pallas_call | solution.py:241
  43.4 16.6 %shard_map.54 = (f32[64,128]{1,0:T(8,128)S(1)}, f32[8,128]{1,0:T(8,128)S(1)}, bf16[64,16,128]{2,1,0:T(8,128)(2,1)S(1)}) custom-call(f32[65,8,128]{2,1,0:T(8,128)S(1)} %get-tuple-element.32.peak, f32[65,8,128]{2,1,0:T(8,128)S(1)} %get-tuple-element.33.total, f32[64,128]{1,0:T(8,128)S(1)} %get-tuple-element.29.a.a_ref.old), custom_call_target="tpu_custom_call" | custom-call | tf_op jit(solution)/shard_map/pallas_call | solution.py:537
  60.0 4.7 %shard_map.55.total = f32[65,8,128]{2,1,0:T(8,128)S(1)} custom-call(s32[1,384]{1,0:T(1,128)S(1)} %get-tuple-element.23.far, bf16[64,16,128]{2,1,0:T(8,128)(2,1)S(1)} %get-tuple-element.34.rows, f32[64,128]{1,0:T(8,128)S(1)} %get-tuple-element.35.b.b_ref, bf16[64,64,128]{2,1,0:T(8,128)(2,1)S(1)} %get-tuple-element.25.yfold, ...), custom_call_target="tpu_custom_call" | custom-call | tf_op jit(solution)/shard_map/pallas_call | solution.py:241
  64.7 4.5 %shard_map.56 = (f32[64,128]{1,0:T(8,128)S(1)}, bf16[64,16,128]{2,1,0:T(8,128)(2,1)S(1)}) custom-call(f32[65,8,128]{2,1,0:T(8,128)S(1)} %shard_map.55.total, f32[64,128]{1,0:T(8,128)S(1)} %get-tuple-element.29.a.a_ref.old, f32[64,128]{1,0:T(8,128)S(1)} %get-tuple-element.35.b.b_ref), custom_call_target="tpu_custom_call" | custom-call | tf_op jit(solution)/shard_map/pallas_call | solution.py:451
  69.2 0.0 copy-start
  69.2 4.6 %shard_map.57 = (f32[65,8,128]{2,1,0:T(8,128)S(1)}, f32[64,128]{1,0:T(8,128)}) custom-call(s32[1,384]{1,0:T(1,128)S(1)} %get-tuple-element.22.far, bf16[64,16,128]{2,1,0:T(8,128)(2,1)S(1)} %get-tuple-element.36.rows, f32[64,128]{1,0:T(8,128)S(1)} %get-tuple-element.37.a, bf16[64,64,128]{2,1,0:T(8,128)(2,1)S(1)} %get-tuple-element.30.xfold, ...), custom_call_target="tpu_custom_call" | custom-call | tf_op jit(solution)/shard_map/pallas_call | solution.py:241
  73.8 0.0 copy-done
  73.8 11.1 %shard_map.58 = f32[8,128]{1,0:T(8,128)S(1)} custom-call(f32[65,8,128]{2,1,0:T(8,128)S(1)} %get-tuple-element.40.total, f32[8,128]{1,0:T(8,128)S(1)} %get-tuple-element.41.old, bf16[64,128]{1,0:T(8,128)(2,1)S(1)} %bitcast.10), custom_call_target="tpu_custom_call" | custom-call | tf_op jit(solution)/shard_map/pallas_call | solution.py:537
  84.9 0.5 slice.3
Async XLA Ops:
  69.2 4.6 %copy-start = (bf16[1,128,64]{1,2,0:T(8,128)(2,1)S(1)}, bf16[1,128,64]{1,2,0:T(8,128)(2,1)}, u32[]{:S(2)}) copy-start(bf16[1,128,64]{1,2,0:T(8,128)(2,1)} %param.4) | copy-start | bytes 49156

commit v6 on v5

--- a/solution.py
+++ b/solution.py
@@ -143,11 +143,11 @@
             process(p, jnp.dot(both, rhs, preferred_element_type=f32))
 
 
-def max_process(peak, total):
+def max_process(peak, total, piece):
     def process(p, v):
         old, sums = peak[p], total[p]
-        for k in range(CHUNK):
-            u = v[k * HALF : (k + 1) * HALF].reshape(HALF // 8, 8, 2 * BLK)
+        for k in range(0, CHUNK * HALF, piece):
+            u = v[k : k + piece].reshape(piece // 8, 8, 2 * BLK)
             top = jnp.max(u, axis=0)
             new = jnp.maximum(old, jnp.maximum(top[:, :BLK], top[:, BLK:]))
             new2 = jnp.concatenate([new, new], axis=1)
@@ -200,7 +200,7 @@
     fold_potential(b, aug)
     init_peaks(peak, total)
     listed.wait()
-    sweep(table, yfold, aug, x_weights(xt), None, max_process(peak, total))
+    sweep(table, yfold, aug, x_weights(xt), None, max_process(peak, total, 64))
 
 
 def col1_kernel(far, a, xfold, yt, peak, total, aug, table, sem):
@@ -208,7 +208,7 @@
     fold_potential(a, aug)
     init_peaks(peak, total)
     listed.wait()
-    sweep(table, xfold, aug, lambda t: yt[t], None, max_process(peak, total))
+    sweep(table, xfold, aug, lambda t: yt[t], None, max_process(peak, total, 32))
 
 
 def row2_kernel(far, rows, b, yfold, xt, total, aug, table, sem):
@@ -285,11 +285,12 @@
     return 2 * dz - 1 if 0 < dz <= 4 else 2 * (NZ - dz) if dz else 0
 
 
-GROUPS = ((0, 1), (1, 2), (3, 2), (5, 3))
+GROUPS = ((0, 1), (1, 2), (3, 2), (5, 2), (7, 1))
 
 
 def gather_kernel(
-    packed, xt_far, yt, yfold, b0, row_table, col_table, xt, held, ls, zs, zr, ys, yr, cs, cr
+    own, bt_far, xt_far, yt, yfold, b0, row_table, member_ref, xt,
+    held, bt_ref, ls, zs, zr, ys, yr, cs, cr,
 ):
     y, z, core = place()
     pick = picker()
@@ -299,9 +300,13 @@
     everyone = list(z_devices.values()) + list(y_devices.values()) + [mate]
     mine = held.at[0, 0, 0]
     hail(everyone)
-    here = pltpu.make_async_copy(xt_far, xt, ls.at[0])
-    here.start()
-    mine[...] = packed[0:DIM, :]
+    here = [
+        pltpu.make_async_copy(src, dst, ls.at[k])
+        for k, (src, dst) in enumerate(((own, mine), (bt_far, bt_ref), (xt_far, xt)))
+    ]
+    for c in here:
+        c.start()
+    here[0].wait()
     meet(everyone)
 
     z_copies = {}
@@ -314,7 +319,7 @@
         for k, d in y_devices.items():
             part = held.at[0, 0, pl.ds(first, size)]
             dst = held.at[0, NY - k, pl.ds(first, size)]
-            y_copies[k, g] = send(part, dst, ys, yr, 4 * (k - 1) + g, d)
+            y_copies[k, g] = send(part, dst, ys, yr, len(GROUPS) * (k - 1) + g, d)
 
     c_copies = []
 
@@ -324,8 +329,7 @@
         c_copies.append(send(part, dst, cs, cr, len(c_copies), mate))
 
     def take(side, dy, s):
-        back = lax.rem(s, 2)
-        dz = back * ((s + 1) // 2) + (1 - back) * (NZ - s // 2)
+        dz = (s + 1) // 2 if s % 2 else NZ - s // 2
         who = core if side == 0 else 1 - core
         t = (lax.rem(y + dy, NY) * NZ + lax.rem(z + dz, NZ)) * 2 + who
         tile = held[side, dy, s]
@@ -335,62 +339,70 @@
         b0[pl.ds(t, 1), :] = -0.5 * jnp.sum(wide * wide, axis=0, keepdims=True)
 
     def take_column(side):
-        @pl.loop(0, NZ, step=4)
-        def _(s):
-            for i in range(4):
-                take(side, 0, s + i)
+        for s in range(NZ):
+            take(side, 0, s)
 
     def take_group(side, g):
-        @pl.loop(GROUPS[g][0], GROUPS[g][0] + GROUPS[g][1])
-        def _(s):
+        for s in range(GROUPS[g][0], GROUPS[g][0] + GROUPS[g][1]):
             for dy in range(1, NY):
                 take(side, dy, s)
 
     on_y(0)
-    t = iota((NBLK, NBLK), 0)
-    bt = packed[DIM:, 0:NBLK].astype(f32)
-    member = sum((bt[k : k + 1, :] == t.astype(f32)).astype(f32) for k in range(SLOTS))
-    col_table[...] = chunk_table(member)
-    eye = (iota((NBLK, NBLK), 1) == t).astype(bf16)
-    row_table[...] = chunk_table(turn_over(eye, member.astype(bf16)))
-    for g, ks in ((1, (1, 7)), (2, (2, 6)), (3, (3, 5, 4))):
+    def pass_on(g):
+        for k in (1, 3, 2):
+            y_copies[k, g].wait_recv()
+        on_mate(1, NY - 1, *GROUPS[g])
+
+    for g, ks in ((1, (1, 7)), (2, (2, 6)), (3, (3, 5)), (4, (4,))):
         for k in ks:
             z_copies[k].wait_recv()
         on_y(g)
+        if g == 2:
+            pass_on(0)
     on_mate(0, 1, 0, NZ)
-    for g in range(4):
-        for k in (1, 3, 2):
-            y_copies[k, g].wait_recv()
-        on_mate(1, NY - 1, *GROUPS[g])
-        if g == 0:
-            take_column(0)
-        take_group(0, g)
-        if g == 1:
-            c_copies[0].wait_recv()
-            take_column(1)
-        if g == 2:
-            c_copies[1].wait_recv()
-            take_group(1, 0)
-    for g in range(1, 4):
+    here[1].wait()
+    t = iota((NBLK, NBLK), 0)
+    bt = bt_ref[...]
+    member = sum((bt[k : k + 1, :] == t).astype(f32) for k in range(SLOTS))
+    eye = (iota((NBLK, NBLK), 1) == t).astype(bf16)
+    member_ref[...] = member
+    row_table[...] = chunk_table(turn_over(eye, member.astype(bf16)))
+    take_column(0)
+    take_group(0, 0)
+    pass_on(1)
+    take_group(0, 1)
+    c_copies[0].wait_recv()
+    take_group(1, 0)
+    pass_on(2)
+    take_group(0, 2)
+    c_copies[1].wait_recv()
+    take_column(1)
+    pass_on(3)
+    take_group(0, 3)
+    c_copies[2].wait_recv()
+    take_group(1, 1)
+    pass_on(4)
+    take_group(0, 4)
+    for g in range(2, 5):
         c_copies[1 + g].wait_recv()
         take_group(1, g)
-    here.wait()
+    here[2].wait()
     for c in list(z_copies.values()) + list(y_copies.values()) + c_copies:
         c.wait_send()
 
 
-def gather(packed, xt):
+def gather(own, bt, xt):
     dma = pltpu.SemaphoreType.DMA
     blocks = jax.ShapeDtypeStruct((NBLK, DIM, BLK), bf16)
     return pl.pallas_call(
         gather_kernel,
-        out_shape=(blocks, blocks, duals(), TABLE, TABLE, jax.ShapeDtypeStruct(xt.shape, bf16)),
-        in_specs=[VMEM, pl.BlockSpec(memory_space=pl.ANY)],
+        out_shape=(blocks, blocks, duals(), TABLE, jax.ShapeDtypeStruct((NBLK, NBLK), f32), jax.ShapeDtypeStruct(xt.shape, bf16)),
+        in_specs=[pl.BlockSpec(memory_space=pl.ANY)] * 3,
         out_specs=(VMEM,) * 6,
-        scratch_shapes=[pltpu.VMEM((2, NY, NZ, DIM, BLK), bf16)]
-        + [dma((1,)), dma((7,)), dma((7,)), dma((12,)), dma((12,)), dma((5,)), dma((5,))],
+        scratch_shapes=[pltpu.VMEM((2, NY, NZ, DIM, BLK), bf16), pltpu.VMEM(bt.shape, jnp.int32)]
+        + [dma((3,)), dma((7,)), dma((7,)), dma((15,)), dma((15,)), dma((6,)), dma((6,))],
         compiler_params=params(0, 50),
-    )(packed, xt)
+    )(own, bt, xt)
 
 
 def spread(pairs, device_of, sends, recvs):
@@ -420,10 +432,12 @@
     collect(got.at[pl.ds(0, 3)], devices[0], sends, recvs)
 
 
-def tgt1_kernel(peak, total, xt, a_ref, xfold, xsq, mine, got, sends, recvs):
+def tgt1_kernel(peak, total, xt, member, a_ref, xfold, xsq, col_table, mine, got, sends, recvs):
     pick = picker()
 
-    def fold_x():
+    def meanwhile():
+        col_table[...] = chunk_table(member[...])
+
         @pl.loop(0, NBLK, step=8)
         def _(p):
             for i in range(8):
@@ -432,7 +446,7 @@
                 wide = tile.astype(f32)
                 xsq[pl.ds(p + i, 1), :] = jnp.sum(wide * wide, axis=0, keepdims=True)
 
-    tgt_exchange(lambda: finish_peaks(peak, total), fold_x, mine, got, sends, recvs)
+    tgt_exchange(lambda: finish_peaks(peak, total), meanwhile, mine, got, sends, recvs)
     a_ref[...] = -lse([got[k] for k in range(NX)]) - LOG_NS
 
 
@@ -549,11 +563,13 @@
     block, tile = pltpu.VMEM((8, 8, BLK), f32), pltpu.VMEM((8, BLK), f32)
 
     blocks = jax.ShapeDtypeStruct((NBLK, DIM, BLK), bf16)
-    listed = block_targets[:, 0, :].T.astype(bf16)
-    packed = jnp.concatenate([own_yt, jnp.pad(listed, ((0, 8), (0, BLK - NBLK)))], axis=0)
-    yt, yfold, b0, row_table, col_table, xt = gather(packed, source_features.T)
+    yt, yfold, b0, row_table, member, xt = gather(
+        own_yt, block_targets[:, 0, :].T, source_features.T
+    )
     peak, total = work_call(row1_kernel, (ACC, ACC), row_table, b0, yfold, xt)
-    a, xfold, xsq = tgt_call(tgt1_kernel, 1, f32, (duals(), blocks, duals()), peak, total, xt)
+    a, xfold, xsq, col_table = tgt_call(
+        tgt1_kernel, 1, f32, (duals(), blocks, duals(), TABLE), peak, total, xt, member
+    )
     peak, total = work_call(col1_kernel, (ACC, ACC), col_table, a, xfold, yt)
     b, own, rows = src_call(
         src1_kernel, 2, (duals(), duals(8), ROWS), [block, block, tile, block, tile, block], 3,

time: 85.6 us -> 84.8 us (level)
  other arithmetic: 1.41 us -> 0 us
  local copies, waits for them, and re-layouts: 0.52 us -> 1.91 us
    unnamed x2 -> x4, local copies, waits for them, and re-layouts: 0.01 us -> 1.4 us
    pallas_call x2, Pallas kernels: 27.7 us -> 26.6 us  [src_call(): pl.pallas_call(kernel, out_shape=outs, in_specs=[VMEM] * len(args), out_s...]
where the time goes in v6:
time: 84.8 us; the launch traced here: 84.6 us
  Pallas kernels  82 us (97%)
  local copies, waits for them, and re-layouts  1.91 us (2%)
    pallas_call x2, Pallas kernels, src_call(): pl.pallas_call(kernel, out_shape=outs, in_specs=[VMEM] * len(args), out_s...  26.6 us
    pallas_call x4, Pallas kernels, work_call(): pl.pallas_call(kernel, out_shape=outs, in_specs=[VMEM] * len(args), out_s...  22.7 us
    pallas_call x1, Pallas kernels, gather(): pl.pallas_call(gather_kernel, out_shape=(blocks, blocks, duals(), TABLE,...  21.9 us
    pallas_call x2, Pallas kernels, tgt_call(): pl.pallas_call(kernel, out_shape=outs, in_specs=[VMEM] * len(args), out_s...  10.8 us

profile of v6, /device:TPU:1, one launch (start us, length us, event | category | flops | bytes accessed | tf_op | source)
XLA Modules:
  0.0 84.6 jit_solution(9576120409136404775)
XLA Ops:
  0.6 0.0 copy-start.1
  0.6 0.7 copy-done.1
  1.3 0.0 copy-start
  1.3 0.7 copy-done
  2.0 21.9 %shard_map.50 = (bf16[64,64,128]{2,1,0:T(8,128)(2,1)S(1)}, bf16[64,64,128]{2,1,0:T(8,128)(2,1)S(1)}, f32[64,128]{1,0:T(8,128)S(1)}, s32[1,384]{1,0:T(1,128)S(1)}...) custom-call(bf16[64,128]{1,0:T(8,128)(2,1)S(1)} %bitcast.8, s32[8,64]{1,0:T(8,128)S(1)} %bitcast.10, ...), custom_call_target="tpu_custom_call" | custom-call | tf_op jit(solution)/shard_map/pallas_call | solution.py:397
  24.0 6.8 %shard_map.51 = (f32[65,8,128]{2,1,0:T(8,128)S(1)}, f32[65,8,128]{2,1,0:T(8,128)S(1)}) custom-call(s32[1,384]{1,0:T(1,128)S(1)} %get-tuple-element.23.far, f32[64,128]{1,0:T(8,128)S(1)} %get-tuple-element.24.b, bf16[64,64,128]{2,1,0:T(8,128)(2,1)S(1)} %get-tuple-element.25.yfold, bf16[64,8192]{1,0:T(8,128)(2,1)S(1)} %get-tuple-element.26.xt), custom_call_target="tpu_custom_call" | custom-call | tf_op jit(solution)/shard_map/pallas_call | solution.py:241
  30.8 6.3 %shard_map.52 = (f32[64,128]{1,0:T(8,128)S(1)}, bf16[64,64,128]{2,1,0:T(8,128)(2,1)S(1)}, f32[64,128]{1,0:T(8,128)S(1)}, s32[1,384]{1,0:T(1,128)S(1)}) custom-call(f32[65,8,128]{2,1,0:T(8,128)S(1)} %get-tuple-element.27.peak, f32[65,8,128]{2,1,0:T(8,128)S(1)} %get-tuple-element.28.total, bf16[64,8192]{1,0:T(8,128)(2,1)S(1)} %get-tuple-element.26.xt, ...), custom_call_target="tpu_custom_call" | custom-call | tf_op jit(solution)/shard_map/pallas_call | solution.py:465
  37.1 6.5 %shard_map.53 = (f32[65,8,128]{2,1,0:T(8,128)S(1)}, f32[65,8,128]{2,1,0:T(8,128)S(1)}) custom-call(s32[1,384]{1,0:T(1,128)S(1)} %get-tuple-element.30.far, f32[64,128]{1,0:T(8,128)S(1)} %get-tuple-element.31.a.a_ref.old, bf16[64,64,128]{2,1,0:T(8,128)(2,1)S(1)} %get-tuple-element.32.xfold, bf16[64,64,128]{2,1,0:T(8,128)(2,1)S(1)} %get-tuple-element.33.yt), custom_call_target="tpu_custom_call" | custom-call | tf_op jit(solution)/shard_map/pallas_call | solution.py:241
  43.6 15.5 %shard_map.54 = (f32[64,128]{1,0:T(8,128)S(1)}, f32[8,128]{1,0:T(8,128)S(1)}, bf16[64,16,128]{2,1,0:T(8,128)(2,1)S(1)}) custom-call(f32[65,8,128]{2,1,0:T(8,128)S(1)} %get-tuple-element.34.peak, f32[65,8,128]{2,1,0:T(8,128)S(1)} %get-tuple-element.35.total, f32[64,128]{1,0:T(8,128)S(1)} %get-tuple-element.31.a.a_ref.old), custom_call_target="tpu_custom_call" | custom-call | tf_op jit(solution)/shard_map/pallas_call | solution.py:551
  59.1 4.8 %shard_map.55.total = f32[65,8,128]{2,1,0:T(8,128)S(1)} custom-call(s32[1,384]{1,0:T(1,128)S(1)} %get-tuple-element.23.far, bf16[64,16,128]{2,1,0:T(8,128)(2,1)S(1)} %get-tuple-element.36.rows, f32[64,128]{1,0:T(8,128)S(1)} %get-tuple-element.37.b.b_ref, bf16[64,64,128]{2,1,0:T(8,128)(2,1)S(1)} %get-tuple-element.25.yfold, ...), custom_call_target="tpu_custom_call" | custom-call | tf_op jit(solution)/shard_map/pallas_call | solution.py:241
  63.9 4.5 %shard_map.56 = (f32[64,128]{1,0:T(8,128)S(1)}, bf16[64,16,128]{2,1,0:T(8,128)(2,1)S(1)}) custom-call(f32[65,8,128]{2,1,0:T(8,128)S(1)} %shard_map.55.total, f32[64,128]{1,0:T(8,128)S(1)} %get-tuple-element.31.a.a_ref.old, f32[64,128]{1,0:T(8,128)S(1)} %get-tuple-element.37.b.b_ref), custom_call_target="tpu_custom_call" | custom-call | tf_op jit(solution)/shard_map/pallas_call | solution.py:465
  68.4 4.6 %shard_map.57 = (f32[65,8,128]{2,1,0:T(8,128)S(1)}, f32[64,128]{1,0:T(8,128)}) custom-call(s32[1,384]{1,0:T(1,128)S(1)} %get-tuple-element.30.far, bf16[64,16,128]{2,1,0:T(8,128)(2,1)S(1)} %get-tuple-element.38.rows, f32[64,128]{1,0:T(8,128)S(1)} %get-tuple-element.39.a, bf16[64,64,128]{2,1,0:T(8,128)(2,1)S(1)} %get-tuple-element.32.xfold, ...), custom_call_target="tpu_custom_call" | custom-call | tf_op jit(solution)/shard_map/pallas_call | solution.py:241
  72.9 11.1 %shard_map.58 = f32[8,128]{1,0:T(8,128)S(1)} custom-call(f32[65,8,128]{2,1,0:T(8,128)S(1)} %get-tuple-element.42.total, f32[8,128]{1,0:T(8,128)S(1)} %get-tuple-element.43.old, bf16[64,128]{1,0:T(8,128)(2,1)S(1)} %bitcast.9), custom_call_target="tpu_custom_call" | custom-call | tf_op jit(solution)/shard_map/pallas_call | solution.py:551
  84.1 0.5 slice.3
Async XLA Ops:
  0.6 0.7 copy-start.1
  1.3 0.7 copy-start

commit v7 on v6

--- a/solution.py
+++ b/solution.py
@@ -25,6 +25,7 @@
 LOG_NT = math.log(NT) / RATE
 LOW = -1.0e30
 BODY = 96
+REST = 16
 MESH = pl.DeviceIdType.MESH
 VMEM = pl.BlockSpec(memory_space=pltpu.VMEM)
 f32, bf16 = jnp.float32, jnp.bfloat16
@@ -121,26 +122,38 @@
     right = ((n16 >= 3) & (n16 < 6)).astype(bf16)
     zero = jnp.zeros((DIM, BLK), bf16)
 
-    @pl.loop(0, (table[0, LANES - 1] + BODY - 1) // BODY)
+    def work(n):
+        word = table[0, n]
+        p = word & (BLK - 1)
+        safe = jnp.minimum(p, NBLK - 1)
+        ids = [(word >> 7) & (BLK - 1), word >> 14]
+        w = weights(safe)
+        l16, r16 = left, right
+        if pot_rows is not None:
+            extra = pot_rows[safe]
+            l16, r16 = left + extra, right + extra
+        top = jnp.concatenate([w, zero], axis=1)
+        mid = jnp.concatenate([zero, w], axis=1)
+        low = jnp.concatenate([l16, r16], axis=1)
+        rhs = jnp.concatenate([top, mid] + [low] * 8, axis=0)
+        body = jnp.concatenate([lhs[jnp.minimum(q, NBLK - 1)] for q in ids], axis=0)
+        tail = jnp.concatenate([aug[q] for q in ids], axis=0)
+        both = jnp.concatenate([body, tail], axis=1)
+        process(p, jnp.dot(both, rhs, preferred_element_type=f32))
+
+    count = table[0, LANES - 1]
+    full = (count + BODY - 1 - 2 * REST) // BODY
+    done = BODY * full
+
+    @pl.loop(0, full)
     def _(turn):
         for k in range(BODY):
-            word = table[0, BODY * turn + k]
-            p = word & (BLK - 1)
-            safe = jnp.minimum(p, NBLK - 1)
-            ids = [(word >> 7) & (BLK - 1), word >> 14]
-            w = weights(safe)
-            l16, r16 = left, right
-            if pot_rows is not None:
-                extra = pot_rows[safe]
-                l16, r16 = left + extra, right + extra
-            top = jnp.concatenate([w, zero], axis=1)
-            mid = jnp.concatenate([zero, w], axis=1)
-            low = jnp.concatenate([l16, r16], axis=1)
-            rhs = jnp.concatenate([top, mid] + [low] * 8, axis=0)
-            body = jnp.concatenate([lhs[jnp.minimum(q, NBLK - 1)] for q in ids], axis=0)
-            tail = jnp.concatenate([aug[q] for q in ids], axis=0)
-            both = jnp.concatenate([body, tail], axis=1)
-            process(p, jnp.dot(both, rhs, preferred_element_type=f32))
+            work(BODY * turn + k)
+
+    @pl.loop(0, jnp.maximum(count - done + REST - 1, 0) // REST)
+    def _(turn):
+        for k in range(REST):
+            work(done + REST * turn + k)
 
 
 def max_process(peak, total, piece):

time: 84.8 us -> 84.8 us (level)
  no operation moved by 1% of the time
where the time goes in v7:
time: 84.8 us; the launch traced here: 84.6 us
  Pallas kernels  82 us (97%)
  local copies, waits for them, and re-layouts  1.91 us (2%)
    pallas_call x2, Pallas kernels, src_call(): pl.pallas_call(kernel, out_shape=outs, in_specs=[VMEM] * len(args), out_s...  26.6 us
    pallas_call x4, Pallas kernels, work_call(): pl.pallas_call(kernel, out_shape=outs, in_specs=[VMEM] * len(args), out_s...  22.6 us
    pallas_call x1, Pallas kernels, gather(): pl.pallas_call(gather_kernel, out_shape=(blocks, blocks, duals(), TABLE,...  21.9 us
    pallas_call x2, Pallas kernels, tgt_call(): pl.pallas_call(kernel, out_shape=outs, in_specs=[VMEM] * len(args), out_s...  10.8 us

profile of v7, /device:TPU:1, one launch (start us, length us, event | category | flops | bytes accessed | tf_op | source)
XLA Modules:
  0.0 84.6 jit_solution(17478721830844461084)
XLA Ops:
  0.6 0.0 copy-start.1
  0.6 0.7 copy-done.1
  1.3 0.0 copy-start
  1.3 0.7 copy-done
  2.0 21.9 %shard_map.50 = (bf16[64,64,128]{2,1,0:T(8,128)(2,1)S(1)}, bf16[64,64,128]{2,1,0:T(8,128)(2,1)S(1)}, f32[64,128]{1,0:T(8,128)S(1)}, s32[1,384]{1,0:T(1,128)S(1)}...) custom-call(bf16[64,128]{1,0:T(8,128)(2,1)S(1)} %bitcast.8, s32[8,64]{1,0:T(8,128)S(1)} %bitcast.10, ...), custom_call_target="tpu_custom_call" | custom-call | tf_op jit(solution)/shard_map/pallas_call | solution.py:410
  24.0 6.8 %shard_map.51 = (f32[65,8,128]{2,1,0:T(8,128)S(1)}, f32[65,8,128]{2,1,0:T(8,128)S(1)}) custom-call(s32[1,384]{1,0:T(1,128)S(1)} %get-tuple-element.23.far, f32[64,128]{1,0:T(8,128)S(1)} %get-tuple-element.24.b, bf16[64,64,128]{2,1,0:T(8,128)(2,1)S(1)} %get-tuple-element.25.yfold, bf16[64,8192]{1,0:T(8,128)(2,1)S(1)} %get-tuple-element.26.xt), custom_call_target="tpu_custom_call" | custom-call | tf_op jit(solution)/shard_map/pallas_call | solution.py:254
  30.8 6.3 %shard_map.52 = (f32[64,128]{1,0:T(8,128)S(1)}, bf16[64,64,128]{2,1,0:T(8,128)(2,1)S(1)}, f32[64,128]{1,0:T(8,128)S(1)}, s32[1,384]{1,0:T(1,128)S(1)}) custom-call(f32[65,8,128]{2,1,0:T(8,128)S(1)} %get-tuple-element.27.peak, f32[65,8,128]{2,1,0:T(8,128)S(1)} %get-tuple-element.28.total, bf16[64,8192]{1,0:T(8,128)(2,1)S(1)} %get-tuple-element.26.xt, ...), custom_call_target="tpu_custom_call" | custom-call | tf_op jit(solution)/shard_map/pallas_call | solution.py:478
  37.1 6.5 %shard_map.53 = (f32[65,8,128]{2,1,0:T(8,128)S(1)}, f32[65,8,128]{2,1,0:T(8,128)S(1)}) custom-call(s32[1,384]{1,0:T(1,128)S(1)} %get-tuple-element.30.far, f32[64,128]{1,0:T(8,128)S(1)} %get-tuple-element.31.a.a_ref.old, bf16[64,64,128]{2,1,0:T(8,128)(2,1)S(1)} %get-tuple-element.32.xfold, bf16[64,64,128]{2,1,0:T(8,128)(2,1)S(1)} %get-tuple-element.33.yt), custom_call_target="tpu_custom_call" | custom-call | tf_op jit(solution)/shard_map/pallas_call | solution.py:254
  43.6 15.5 %shard_map.54 = (f32[64,128]{1,0:T(8,128)S(1)}, f32[8,128]{1,0:T(8,128)S(1)}, bf16[64,16,128]{2,1,0:T(8,128)(2,1)S(1)}) custom-call(f32[65,8,128]{2,1,0:T(8,128)S(1)} %get-tuple-element.34.peak, f32[65,8,128]{2,1,0:T(8,128)S(1)} %get-tuple-element.35.total, f32[64,128]{1,0:T(8,128)S(1)} %get-tuple-element.31.a.a_ref.old), custom_call_target="tpu_custom_call" | custom-call | tf_op jit(solution)/shard_map/pallas_call | solution.py:564
  59.1 4.8 %shard_map.55.total = f32[65,8,128]{2,1,0:T(8,128)S(1)} custom-call(s32[1,384]{1,0:T(1,128)S(1)} %get-tuple-element.23.far, bf16[64,16,128]{2,1,0:T(8,128)(2,1)S(1)} %get-tuple-element.36.rows, f32[64,128]{1,0:T(8,128)S(1)} %get-tuple-element.37.b.b_ref, bf16[64,64,128]{2,1,0:T(8,128)(2,1)S(1)} %get-tuple-element.25.yfold, ...), custom_call_target="tpu_custom_call" | custom-call | tf_op jit(solution)/shard_map/pallas_call | solution.py:254
  63.9 4.5 %shard_map.56 = (f32[64,128]{1,0:T(8,128)S(1)}, bf16[64,16,128]{2,1,0:T(8,128)(2,1)S(1)}) custom-call(f32[65,8,128]{2,1,0:T(8,128)S(1)} %shard_map.55.total, f32[64,128]{1,0:T(8,128)S(1)} %get-tuple-element.31.a.a_ref.old, f32[64,128]{1,0:T(8,128)S(1)} %get-tuple-element.37.b.b_ref), custom_call_target="tpu_custom_call" | custom-call | tf_op jit(solution)/shard_map/pallas_call | solution.py:478
  68.4 4.6 %shard_map.57 = (f32[65,8,128]{2,1,0:T(8,128)S(1)}, f32[64,128]{1,0:T(8,128)}) custom-call(s32[1,384]{1,0:T(1,128)S(1)} %get-tuple-element.30.far, bf16[64,16,128]{2,1,0:T(8,128)(2,1)S(1)} %get-tuple-element.38.rows, f32[64,128]{1,0:T(8,128)S(1)} %get-tuple-element.39.a, bf16[64,64,128]{2,1,0:T(8,128)(2,1)S(1)} %get-tuple-element.32.xfold, ...), custom_call_target="tpu_custom_call" | custom-call | tf_op jit(solution)/shard_map/pallas_call | solution.py:254
  73.0 11.1 %shard_map.58 = f32[8,128]{1,0:T(8,128)S(1)} custom-call(f32[65,8,128]{2,1,0:T(8,128)S(1)} %get-tuple-element.42.total, f32[8,128]{1,0:T(8,128)S(1)} %get-tuple-element.43.old, bf16[64,128]{1,0:T(8,128)(2,1)S(1)} %bitcast.9), custom_call_target="tpu_custom_call" | custom-call | tf_op jit(solution)/shard_map/pallas_call | solution.py:564
  84.1 0.5 slice.3
Async XLA Ops:
  0.6 0.7 copy-start.1
  1.3 0.7 copy-start

commit v8 on v7

--- a/solution.py
+++ b/solution.py
@@ -122,7 +122,7 @@
     right = ((n16 >= 3) & (n16 < 6)).astype(bf16)
     zero = jnp.zeros((DIM, BLK), bf16)
 
-    def work(n):
+    def work(n, bank):
         word = table[0, n]
         p = word & (BLK - 1)
         safe = jnp.minimum(p, NBLK - 1)
@@ -139,7 +139,7 @@
         body = jnp.concatenate([lhs[jnp.minimum(q, NBLK - 1)] for q in ids], axis=0)
         tail = jnp.concatenate([aug[q] for q in ids], axis=0)
         both = jnp.concatenate([body, tail], axis=1)
-        process(p, jnp.dot(both, rhs, preferred_element_type=f32))
+        process[bank](p, jnp.dot(both, rhs, preferred_element_type=f32))
 
     count = table[0, LANES - 1]
     full = (count + BODY - 1 - 2 * REST) // BODY
@@ -148,12 +148,12 @@
     @pl.loop(0, full)
     def _(turn):
         for k in range(BODY):
-            work(BODY * turn + k)
+            work(BODY * turn + k, k % len(process))
 
     @pl.loop(0, jnp.maximum(count - done + REST - 1, 0) // REST)
     def _(turn):
         for k in range(REST):
-            work(done + REST * turn + k)
+            work(done + REST * turn + k, k % len(process))
 
 
 def max_process(peak, total, piece):
@@ -187,10 +187,14 @@
     total[...] = jnp.zeros(total.shape, f32)
 
 
-def finish_peaks(peak, total):
-    m = peak[0:NBLK]
+def finish_peaks(peak, total, *more):
+    m, sums = peak[0:NBLK], total[0:NBLK]
+    if more:
+        old, other = m, more[0][0:NBLK]
+        m = jnp.maximum(old, other)
+        sums = sums * jnp.exp2((old - m) * C2) + more[1][0:NBLK] * jnp.exp2((other - m) * C2)
     top = jnp.max(m, axis=1)
-    s = jnp.sum(total[0:NBLK] * jnp.exp2((m - top[:, None, :]) * C2), axis=1)
+    s = jnp.sum(sums * jnp.exp2((m - top[:, None, :]) * C2), axis=1)
     return top + jnp.log2(s) * (1.0 / C2)
 
 
@@ -208,12 +212,13 @@
     return copy
 
 
-def row1_kernel(far, b, yfold, xt, peak, total, aug, table, sem):
+def row1_kernel(far, b, yfold, xt, peak, total, peak2, total2, aug, table, sem):
     listed = fetch(far, table, sem)
     fold_potential(b, aug)
     init_peaks(peak, total)
+    init_peaks(peak2, total2)
     listed.wait()
-    sweep(table, yfold, aug, x_weights(xt), None, max_process(peak, total, 64))
+    sweep(table, yfold, aug, x_weights(xt), None, [max_process(peak, total, 64), max_process(peak2, total2, 64)])
 
 
 def col1_kernel(far, a, xfold, yt, peak, total, aug, table, sem):
@@ -221,7 +226,7 @@
     fold_potential(a, aug)
     init_peaks(peak, total)
     listed.wait()
-    sweep(table, xfold, aug, lambda t: yt[t], None, max_process(peak, total, 32))
+    sweep(table, xfold, aug, lambda t: yt[t], None, [max_process(peak, total, 32)])
 
 
 def row2_kernel(far, rows, b, yfold, xt, total, aug, table, sem):
@@ -229,7 +234,7 @@
     fold_potential(b, aug)
     total[...] = jnp.zeros(total.shape, f32)
     listed.wait()
-    sweep(table, yfold, aug, x_weights(xt), rows, sum_process(total))
+    sweep(table, yfold, aug, x_weights(xt), rows, [sum_process(total)])
 
 
 def col2_kernel(far, rows, a, xfold, yt, xsq, total, f_out, aug, table, sem, f, f_sem):
@@ -240,7 +245,7 @@
     fold_potential(a, aug)
     total[...] = jnp.zeros(total.shape, f32)
     listed.wait()
-    sweep(table, xfold, aug, lambda t: yt[t], rows, sum_process(total))
+    sweep(table, xfold, aug, lambda t: yt[t], rows, [sum_process(total)])
     leave.wait()
 
 
@@ -445,7 +450,7 @@
     collect(got.at[pl.ds(0, 3)], devices[0], sends, recvs)
 
 
-def tgt1_kernel(peak, total, xt, member, a_ref, xfold, xsq, col_table, mine, got, sends, recvs):
+def tgt1_kernel(peak, total, peak2, total2, xt, member, a_ref, xfold, xsq, col_table, mine, got, sends, recvs):
     pick = picker()
 
     def meanwhile():
@@ -459,7 +464,7 @@
                 wide = tile.astype(f32)
                 xsq[pl.ds(p + i, 1), :] = jnp.sum(wide * wide, axis=0, keepdims=True)
 
-    tgt_exchange(lambda: finish_peaks(peak, total), meanwhile, mine, got, sends, recvs)
+    tgt_exchange(lambda: finish_peaks(peak, total, peak2, total2), meanwhile, mine, got, sends, recvs)
     a_ref[...] = -lse([got[k] for k in range(NX)]) - LOG_NS
 
 
@@ -579,9 +584,9 @@
     yt, yfold, b0, row_table, member, xt = gather(
         own_yt, block_targets[:, 0, :].T, source_features.T
     )
-    peak, total = work_call(row1_kernel, (ACC, ACC), row_table, b0, yfold, xt)
+    sums = work_call(row1_kernel, (ACC,) * 4, row_table, b0, yfold, xt)
     a, xfold, xsq, col_table = tgt_call(
-        tgt1_kernel, 1, f32, (duals(), blocks, duals(), TABLE), peak, total, xt, member
+        tgt1_kernel, 1, f32, (duals(), blocks, duals(), TABLE), *sums, xt, member
     )
     peak, total = work_call(col1_kernel, (ACC, ACC), col_table, a, xfold, yt)
     b, own, rows = src_call(

time: 84.8 us -> 84.6 us (level)
  no operation moved by 1% of the time
where the time goes in v8:
time: 84.6 us; the launch traced here: 84.5 us
  Pallas kernels  81.8 us (97%)
  local copies, waits for them, and re-layouts  1.91 us (2%)
    pallas_call x2, Pallas kernels, src_call(): pl.pallas_call(kernel, out_shape=outs, in_specs=[VMEM] * len(args), out_s...  26.5 us
    pallas_call x4, Pallas kernels, work_call(): pl.pallas_call(kernel, out_shape=outs, in_specs=[VMEM] * len(args), out_s...  22.6 us
    pallas_call x1, Pallas kernels, gather(): pl.pallas_call(gather_kernel, out_shape=(blocks, blocks, duals(), TABLE,...  21.9 us
    pallas_call x2, Pallas kernels, tgt_call(): pl.pallas_call(kernel, out_shape=outs, in_specs=[VMEM] * len(args), out_s...  10.8 us

profile of v8, /device:TPU:1, one launch (start us, length us, event | category | flops | bytes accessed | tf_op | source)
XLA Modules:
  0.0 84.5 jit_solution(7854307222223107683)
XLA Ops:
  0.6 0.0 copy-start.1
  0.6 0.7 copy-done.1
  1.3 0.0 copy-start
  1.3 0.7 copy-done
  2.0 21.9 %shard_map.50 = (bf16[64,64,128]{2,1,0:T(8,128)(2,1)S(1)}, bf16[64,64,128]{2,1,0:T(8,128)(2,1)S(1)}, f32[64,128]{1,0:T(8,128)S(1)}, s32[1,384]{1,0:T(1,128)S(1)}...) custom-call(bf16[64,128]{1,0:T(8,128)(2,1)S(1)} %bitcast.8, s32[8,64]{1,0:T(8,128)S(1)} %bitcast.10, ...), custom_call_target="tpu_custom_call" | custom-call | tf_op jit(solution)/shard_map/pallas_call | solution.py:415
  24.0 6.7 %shard_map.51 = (f32[65,8,128]{2,1,0:T(8,128)S(1)}, f32[65,8,128]{2,1,0:T(8,128)S(1)}, f32[65,8,128]{2,1,0:T(8,128)S(1)}, f32[65,8,128]{2,1,0:T(8,128)S(1)}) custom-call(s32[1,384]{1,0:T(1,128)S(1)} %get-tuple-element.25.far, f32[64,128]{1,0:T(8,128)S(1)} %get-tuple-element.26.b, bf16[64,64,128]{2,1,0:T(8,128)(2,1)S(1)} %get-tuple-element.27.yfold, ...), custom_call_target="tpu_custom_call" | custom-call | tf_op jit(solution)/shard_map/pallas_call | solution.py:259
  30.7 6.4 %shard_map.52 = (f32[64,128]{1,0:T(8,128)S(1)}, bf16[64,64,128]{2,1,0:T(8,128)(2,1)S(1)}, f32[64,128]{1,0:T(8,128)S(1)}, s32[1,384]{1,0:T(1,128)S(1)}) custom-call(f32[65,8,128]{2,1,0:T(8,128)S(1)} %get-tuple-element.29.peak, f32[65,8,128]{2,1,0:T(8,128)S(1)} %get-tuple-element.30.total, f32[65,8,128]{2,1,0:T(8,128)S(1)} %get-tuple-element.31.peak2, ...), custom_call_target="tpu_custom_call" | custom-call | tf_op jit(solution)/shard_map/pallas_call | solution.py:483
  37.1 6.5 %shard_map.53 = (f32[65,8,128]{2,1,0:T(8,128)S(1)}, f32[65,8,128]{2,1,0:T(8,128)S(1)}) custom-call(s32[1,384]{1,0:T(1,128)S(1)} %get-tuple-element.34.far, f32[64,128]{1,0:T(8,128)S(1)} %get-tuple-element.35.a.a_ref.old, bf16[64,64,128]{2,1,0:T(8,128)(2,1)S(1)} %get-tuple-element.36.xfold, bf16[64,64,128]{2,1,0:T(8,128)(2,1)S(1)} %get-tuple-element.37.yt), custom_call_target="tpu_custom_call" | custom-call | tf_op jit(solution)/shard_map/pallas_call | solution.py:259
  43.6 15.4 %shard_map.54 = (f32[64,128]{1,0:T(8,128)S(1)}, f32[8,128]{1,0:T(8,128)S(1)}, bf16[64,16,128]{2,1,0:T(8,128)(2,1)S(1)}) custom-call(f32[65,8,128]{2,1,0:T(8,128)S(1)} %get-tuple-element.38.peak, f32[65,8,128]{2,1,0:T(8,128)S(1)} %get-tuple-element.39.total, f32[64,128]{1,0:T(8,128)S(1)} %get-tuple-element.35.a.a_ref.old), custom_call_target="tpu_custom_call" | custom-call | tf_op jit(solution)/shard_map/pallas_call | solution.py:569
  59.0 4.8 %shard_map.55.total = f32[65,8,128]{2,1,0:T(8,128)S(1)} custom-call(s32[1,384]{1,0:T(1,128)S(1)} %get-tuple-element.25.far, bf16[64,16,128]{2,1,0:T(8,128)(2,1)S(1)} %get-tuple-element.40.rows, f32[64,128]{1,0:T(8,128)S(1)} %get-tuple-element.41.b.b_ref, bf16[64,64,128]{2,1,0:T(8,128)(2,1)S(1)} %get-tuple-element.27.yfold, ...), custom_call_target="tpu_custom_call" | custom-call | tf_op jit(solution)/shard_map/pallas_call | solution.py:259
  63.8 4.5 %shard_map.56 = (f32[64,128]{1,0:T(8,128)S(1)}, bf16[64,16,128]{2,1,0:T(8,128)(2,1)S(1)}) custom-call(f32[65,8,128]{2,1,0:T(8,128)S(1)} %shard_map.55.total, f32[64,128]{1,0:T(8,128)S(1)} %get-tuple-element.35.a.a_ref.old, f32[64,128]{1,0:T(8,128)S(1)} %get-tuple-element.41.b.b_ref), custom_call_target="tpu_custom_call" | custom-call | tf_op jit(solution)/shard_map/pallas_call | solution.py:483
  68.3 4.6 %shard_map.57 = (f32[65,8,128]{2,1,0:T(8,128)S(1)}, f32[64,128]{1,0:T(8,128)}) custom-call(s32[1,384]{1,0:T(1,128)S(1)} %get-tuple-element.34.far, bf16[64,16,128]{2,1,0:T(8,128)(2,1)S(1)} %get-tuple-element.42.rows, f32[64,128]{1,0:T(8,128)S(1)} %get-tuple-element.43.a, bf16[64,64,128]{2,1,0:T(8,128)(2,1)S(1)} %get-tuple-element.36.xfold, ...), custom_call_target="tpu_custom_call" | custom-call | tf_op jit(solution)/shard_map/pallas_call | solution.py:259
  72.9 11.1 %shard_map.58 = f32[8,128]{1,0:T(8,128)S(1)} custom-call(f32[65,8,128]{2,1,0:T(8,128)S(1)} %get-tuple-element.46.total, f32[8,128]{1,0:T(8,128)S(1)} %get-tuple-element.47.old, bf16[64,128]{1,0:T(8,128)(2,1)S(1)} %bitcast.9), custom_call_target="tpu_custom_call" | custom-call | tf_op jit(solution)/shard_map/pallas_call | solution.py:569
  83.9 0.5 slice.3
Async XLA Ops:
  0.6 0.7 copy-start.1
  1.3 0.7 copy-start
